TPU v7x, 32 devices: a whole 2x2x4 slice. The times are simulated.
32 devices in a mesh: dp: 8 (over y, x, core), mp: 4 (over z).
Axes of the slice: x: 2, y: 2, z: 4, core: 2. Of those that a mesh axis runs over, the one named last changes fastest.
Arguments:
- hidden_in: float32 [16384, 768], P(('dp', 'mp')), may hold values from -6 to 6
- out_grad: float32 [16384, 768], P(('dp', 'mp')), may hold values from -6 to 6
- attn_weight: float32 [3, 768, 768], P(None, 'dp', 'mp'), may hold values from -0.109375 to 0.109375
- out_weight: float32 [768, 768], P('mp', 'dp'), may hold values from -2.5 to 2.5
- inner_weight: float32 [768, 3072], P('dp', 'mp'), may hold values from -0.21875 to 0.21875
- outer_weight: float32 [3072, 768], P('mp', 'dp'), may hold values from -0.109375 to 0.109375
- rel_bias: float32 [32, 12], replicated, may hold values from -4 to 4
- gains: float32 [2, 768], replicated, may hold values from 0.4 to 2.9
- lengths: int32 [16], P('dp'), may hold values from 256 to 1024, as said below
- table: int32 [2047], replicated, may hold values from 0 to 31, as said below
- attn_first: float32 [3, 768, 768], P(None, 'dp', 'mp'), may hold values from -0.0009765625 to 0.0009765625
- attn_second: float32 [3, 768, 768], P(None, 'dp', 'mp'), may hold values from 4.2385526e-10 to 1.695421e-09
- out_first: float32 [768, 768], P('mp', 'dp'), may hold values from -3.8146973e-05 to 3.8146973e-05
- out_second: float32 [768, 768], P('mp', 'dp'), may hold values from 5.298191e-13 to 2.1192763e-12
- inner_first: float32 [768, 3072], P('dp', 'mp'), may hold values from -6.1035156e-05 to 6.1035156e-05
- inner_second: float32 [768, 3072], P('dp', 'mp'), may hold values from 1.695421e-12 to 6.781684e-12
- outer_first: float32 [3072, 768], P('mp', 'dp'), may hold values from -9.1552734e-05 to 9.1552734e-05
- outer_second: float32 [3072, 768], P('mp', 'dp'), may hold values from 3.390842e-12 to 1.3563368e-11
- rel_first: float32 [32, 12], replicated, may hold values from -3.8146973e-05 to 3.8146973e-05
- rel_second: float32 [32, 12], replicated, may hold values from 5.298191e-13 to 2.1192763e-12
- gain_first: float32 [2, 768], replicated, may hold values from -0.0007324219 to 0.0007324219
- gain_second: float32 [2, 768], replicated, may hold values from 2.1192763e-10 to 8.477105e-10
Outputs:
- block_out: float32 [16384, 768], P(('dp', 'mp'))
- input_grad: float32 [16384, 768], P(('dp', 'mp'))
- grad_norm: float32 [], replicated
- attn_master: float32 [3, 768, 768], P(None, 'dp', 'mp')
- attn_moment: float32 [3, 768, 768], P(None, 'dp', 'mp')
- attn_square: float32 [3, 768, 768], P(None, 'dp', 'mp')
- out_master: float32 [768, 768], P('mp', 'dp')
- out_moment: float32 [768, 768], P('mp', 'dp')
- out_square: float32 [768, 768], P('mp', 'dp')
- inner_master: float32 [768, 3072], P('dp', 'mp')
- inner_moment: float32 [768, 3072], P('dp', 'mp')
- inner_square: float32 [768, 3072], P('dp', 'mp')
- outer_master: float32 [3072, 768], P('mp', 'dp')
- outer_moment: float32 [3072, 768], P('mp', 'dp')
- outer_square: float32 [3072, 768], P('mp', 'dp')
- rel_master: float32 [32, 12], replicated
- rel_moment: float32 [32, 12], replicated
- rel_square: float32 [32, 12], replicated
- gain_master: float32 [2, 768], replicated
- gain_moment: float32 [2, 768], replicated
- gain_square: float32 [2, 768], replicated
Inputs may be any that keep to these rules, and one draw needn't show every extreme that they name: `lengths`: in each aligned group of 2 sequences at least one has length 1024. `table`: entry r + 1023 depends only on |r| and the sign of r: it is |r| for |r| < 8, does not fall as |r| grows, is 15 for |r| >= 128, and 16 is added where r > 0.
All inputs are finite; a program needn't handle non-finite values.
Results may differ from a plain program's by a relative error of at most 0.022.
The roundings to bfloat16 on the way count: a program that leaves them out, or rounds other values in their place, can miss the bound.
Values may be sent and summed in bfloat16 or wider, within the bound.
A program may use at most 192 MiB of HBM per device.

v0:
```python
import jax
import jax.numpy as jnp
from jax import lax
from jax.sharding import PartitionSpec as P

HDIM = 64
SEQLEN = 1024
STEP = 10


NORM_EPS = 1e-06
CLIP = 1.0
BETA_ONE = 0.9
BETA_TWO = 0.999
ADAM_EPS = 1e-08
DECAY = 0.01
RATE_MATRIX = 0.05
RATE_OUT = 0.6
RATE_SMALL = 1.0


def rms_scaled(value, gain):
    return value * lax.rsqrt(jnp.mean(value * value, axis=-1, keepdims=True) + NORM_EPS) * gain


def rms_back(value, gain, grad):
    factor = lax.rsqrt(jnp.mean(value * value, axis=-1, keepdims=True) + NORM_EPS)
    unit = value * factor
    gain_part = jnp.sum(grad * unit, axis=0)
    scaled = grad * gain
    result = factor * (scaled - unit * jnp.mean(scaled * unit, axis=-1, keepdims=True))
    return (result, gain_part)


def toeplitz(line, offset, block, length):
    heads = line.shape[0]
    segment = lax.dynamic_slice_in_dim(line, offset, length + block - 1, 1)
    spread = jnp.broadcast_to(segment[:, None, :], (heads, block, length + block - 1))
    spread = spread.reshape(heads, block * (length + block - 1))
    spread = jnp.pad(spread, ((0, 0), (0, block))).reshape(heads, block, length + block)
    return spread[:, ::-1, :length]


def diag_sums(matrix):
    heads, block, length = matrix.shape
    flipped = jnp.pad(matrix[:, ::-1, :], ((0, 0), (0, 0), (0, block)))
    flat = flipped.reshape(heads, block * (length + block))[:, : block * (length + block - 1)]
    return jnp.sum(flat.reshape(heads, block, length + block - 1), axis=1)


def adam_step(master, grad, first, second, factor, rate):
    clipped = grad * factor
    first_new = BETA_ONE * first + (1.0 - BETA_ONE) * clipped
    second_new = BETA_TWO * second + (1.0 - BETA_TWO) * clipped * clipped
    first_hat = first_new / (1.0 - BETA_ONE**STEP)
    second_hat = second_new / (1.0 - BETA_TWO**STEP)
    master_new = master - rate * (first_hat / (jnp.sqrt(second_hat) + ADAM_EPS) + DECAY * master)
    return (master_new, first_new, second_new)


def body(
    hidden_in,
    out_grad,
    attn_weight,
    out_weight,
    inner_weight,
    outer_weight,
    rel_bias,
    gains,
    lengths,
    table,
    attn_first,
    attn_second,
    out_first,
    out_second,
    inner_first,
    inner_second,
    outer_first,
    outer_second,
    rel_first,
    rel_second,
    gain_first,
    gain_second,
):
    low_type = jnp.bfloat16
    w_attn, w_out, w_inner, w_outer = (
        lax.all_gather(attn_weight.astype(low_type), "dp", axis=1, tiled=True),
        lax.all_gather(out_weight.astype(low_type), "dp", axis=1, tiled=True),
        lax.all_gather(inner_weight.astype(low_type), "dp", axis=0, tiled=True),
        lax.all_gather(outer_weight.astype(low_type), "dp", axis=1, tiled=True),
    )
    width = w_attn.shape[1]
    local_width = w_attn.shape[2]
    heads_local = local_width // HDIM
    w_joined = jnp.transpose(w_attn, (1, 0, 2)).reshape(width, 3 * local_width)
    seq_count = lengths.shape[0]
    block = min(512, SEQLEN)
    nblocks = SEQLEN // block
    turns = seq_count * nblocks
    total_rows = seq_count * SEQLEN
    normed_one = rms_scaled(hidden_in, gains[0]).astype(low_type)
    rows_one = lax.all_gather(normed_one, "mp", axis=0, tiled=True)
    joined = jnp.dot(rows_one, w_joined, preferred_element_type=jnp.float32).astype(low_type)
    query = joined[:, :local_width]
    keys = joined[:, local_width : 2 * local_width]
    values = joined[:, 2 * local_width :]
    mp_index = lax.axis_index("mp")
    rel_local = lax.dynamic_slice_in_dim(rel_bias, mp_index * heads_local, heads_local, 1)
    one_hot = (table[:, None] == jnp.arange(rel_bias.shape[0], dtype=jnp.int32)[None, :]).astype(
        jnp.float32
    )
    bias_line = jnp.dot(one_hot, rel_local, precision=lax.Precision.HIGHEST).T
    bias_blocks = jnp.stack(
        [
            toeplitz(bias_line, SEQLEN - block - portion * block, block, SEQLEN)
            for portion in range(nblocks)
        ]
    )
    key_index = jnp.arange(SEQLEN)

    def scores_of(turn):
        sequence = turn // nblocks
        portion = turn % nblocks
        q_block = lax.dynamic_slice_in_dim(
            query, sequence * SEQLEN + portion * block, block, 0
        ).reshape(block, heads_local, HDIM)
        k_seq = lax.dynamic_slice_in_dim(keys, sequence * SEQLEN, SEQLEN, 0).reshape(
            SEQLEN, heads_local, HDIM
        )
        v_seq = lax.dynamic_slice_in_dim(values, sequence * SEQLEN, SEQLEN, 0).reshape(
            SEQLEN, heads_local, HDIM
        )
        scores = (
            jnp.einsum("qhd,khd->hqk", q_block, k_seq, preferred_element_type=jnp.float32)
            + bias_blocks[portion]
        )
        scores = jnp.where((key_index < lengths[sequence])[None, None, :], scores, -1e30)
        return (scores, q_block, k_seq, v_seq, sequence, portion)

    def forward_step(carry, turn):
        scores, q_block, k_seq, v_seq, sequence, portion = scores_of(turn)
        peak = jnp.max(scores, axis=-1, keepdims=True)
        expo = jnp.exp(scores - peak)
        summed = jnp.sum(expo, axis=-1, keepdims=True)
        chances = (expo / summed).astype(low_type)
        context = jnp.einsum("hqk,khd->qhd", chances, v_seq, preferred_element_type=jnp.float32)
        return (
            carry,
            (context.astype(low_type).reshape(block, local_width), peak + jnp.log(summed)),
        )

    unused, (context, logsum) = lax.scan(
        forward_step, jnp.zeros((), jnp.float32), jnp.arange(turns)
    )
    context = context.reshape(total_rows, local_width)
    middle = hidden_in + lax.psum_scatter(
        jnp.dot(context, w_out, preferred_element_type=jnp.float32),
        "mp",
        scatter_dimension=0,
        tiled=True,
    )
    normed_two = rms_scaled(middle, gains[1]).astype(low_type)
    rows_two = lax.all_gather(normed_two, "mp", axis=0, tiled=True)
    inner = jnp.dot(rows_two, w_inner, preferred_element_type=jnp.float32)
    active = jax.nn.gelu(inner).astype(low_type)
    block_out = middle + lax.psum_scatter(
        jnp.dot(active, w_outer, preferred_element_type=jnp.float32).astype(jnp.bfloat16),
        "mp",
        scatter_dimension=0,
        tiled=True,
    ).astype(jnp.float32)
    outer_back = lax.all_gather(out_grad.astype(low_type), "mp", axis=0, tiled=True)
    grad_outer = jnp.einsum("tf,td->fd", active, outer_back, preferred_element_type=jnp.float32)
    active_back = jnp.einsum("td,fd->tf", outer_back, w_outer, preferred_element_type=jnp.float32)
    unused_value, gelu_pull = jax.vjp(jax.nn.gelu, inner)
    inner_back = gelu_pull(active_back)[0].astype(low_type)
    grad_inner = jnp.einsum("td,tf->df", rows_two, inner_back, preferred_element_type=jnp.float32)
    two_back = lax.psum_scatter(
        jnp.einsum("tf,df->td", inner_back, w_inner, preferred_element_type=jnp.float32),
        "mp",
        scatter_dimension=0,
        tiled=True,
    )
    middle_back, gain_two_part = rms_back(middle, gains[1], two_back)
    middle_back = middle_back + out_grad
    attn_back = lax.all_gather(middle_back.astype(low_type), "mp", axis=0, tiled=True)
    grad_out = jnp.einsum("tc,td->cd", context, attn_back, preferred_element_type=jnp.float32)
    context_back = jnp.einsum(
        "td,cd->tc", attn_back, w_out, preferred_element_type=jnp.float32
    ).astype(low_type)

    def backward_step(carry, turn):
        key_acc, value_acc, line_acc = carry
        scores, q_block, k_seq, v_seq, sequence, portion = scores_of(turn)
        chances = jnp.exp(scores - logsum[turn])
        chances_low = chances.astype(low_type)
        back_block = lax.dynamic_slice_in_dim(
            context_back, sequence * SEQLEN + portion * block, block, 0
        ).reshape(block, heads_local, HDIM)
        chance_back = jnp.einsum(
            "qhd,khd->hqk", back_block, v_seq, preferred_element_type=jnp.float32
        )
        value_part = jnp.einsum(
            "hqk,qhd->khd", chances_low, back_block, preferred_element_type=jnp.float32
        )
        center = jnp.sum(chances * chance_back, axis=-1, keepdims=True)
        score_back = (chances * (chance_back - center)).astype(low_type)
        query_part = jnp.einsum(
            "hqk,khd->qhd", score_back, k_seq, preferred_element_type=jnp.float32
        )
        key_part = jnp.einsum(
            "hqk,qhd->khd", score_back, q_block, preferred_element_type=jnp.float32
        )
        offset = SEQLEN - block - portion * block
        line_piece = lax.dynamic_slice_in_dim(line_acc, offset, SEQLEN + block - 1, 1) + diag_sums(
            score_back.astype(jnp.float32)
        )
        line_acc = lax.dynamic_update_slice_in_dim(line_acc, line_piece, offset, 1)
        key_piece = lax.dynamic_slice_in_dim(key_acc, sequence * SEQLEN, SEQLEN, 0) + key_part
        key_acc = lax.dynamic_update_slice_in_dim(key_acc, key_piece, sequence * SEQLEN, 0)
        value_piece = lax.dynamic_slice_in_dim(value_acc, sequence * SEQLEN, SEQLEN, 0) + value_part
        value_acc = lax.dynamic_update_slice_in_dim(value_acc, value_piece, sequence * SEQLEN, 0)
        return ((key_acc, value_acc, line_acc), query_part.reshape(block, local_width))

    start_carry = (
        jnp.zeros((total_rows, heads_local, HDIM), jnp.float32),
        jnp.zeros((total_rows, heads_local, HDIM), jnp.float32),
        jnp.zeros(bias_line.shape, jnp.float32),
    )
    (key_acc, value_acc, line_acc), query_back = lax.scan(
        backward_step, start_carry, jnp.arange(turns)
    )
    joined_back = jnp.concatenate(
        [
            query_back.reshape(total_rows, local_width),
            key_acc.reshape(total_rows, local_width),
            value_acc.reshape(total_rows, local_width),
        ],
        axis=1,
    ).astype(low_type)
    grad_joined = jnp.einsum("td,tc->dc", rows_one, joined_back, preferred_element_type=jnp.float32)
    grad_attn = jnp.transpose(grad_joined.reshape(width, 3, local_width), (1, 0, 2))
    one_back = lax.psum_scatter(
        jnp.einsum("tc,dc->td", joined_back, w_joined, preferred_element_type=jnp.float32).astype(
            jnp.bfloat16
        ),
        "mp",
        scatter_dimension=0,
        tiled=True,
    ).astype(jnp.float32)
    input_grad, gain_one_part = rms_back(hidden_in, gains[0], one_back)
    input_grad = input_grad + middle_back
    rel_local_grad = jnp.dot(one_hot.T, line_acc.T, precision=lax.Precision.HIGHEST)
    rel_part = lax.dynamic_update_slice(
        jnp.zeros(rel_bias.shape, jnp.float32), rel_local_grad, (0, mp_index * heads_local)
    )
    partials = (grad_attn, grad_out, grad_inner, grad_outer)
    summed = lax.psum((partials[0], partials[1], partials[2], partials[3]), "dp")
    dp_index = lax.axis_index("dp")
    owned = (
        lax.dynamic_slice_in_dim(
            summed[0], dp_index * attn_weight.shape[1], attn_weight.shape[1], 1
        ),
        lax.dynamic_slice_in_dim(summed[1], dp_index * out_weight.shape[1], out_weight.shape[1], 1),
        lax.dynamic_slice_in_dim(
            summed[2], dp_index * inner_weight.shape[0], inner_weight.shape[0], 0
        ),
        lax.dynamic_slice_in_dim(
            summed[3], dp_index * outer_weight.shape[1], outer_weight.shape[1], 1
        ),
    )
    square_part = (
        jnp.sum(owned[0] * owned[0])
        + jnp.sum(owned[1] * owned[1])
        + jnp.sum(owned[2] * owned[2])
        + jnp.sum(owned[3] * owned[3])
    )
    gain_grad, rel_grad, square_total = lax.psum(
        (jnp.stack([gain_one_part, gain_two_part]), rel_part, square_part), ("dp", "mp")
    )
    grad_norm = jnp.sqrt(
        square_total + jnp.sum(gain_grad * gain_grad) + jnp.sum(rel_grad * rel_grad)
    )
    factor = jnp.minimum(1.0, CLIP / (grad_norm + 1e-06))
    attn_new = adam_step(attn_weight, owned[0], attn_first, attn_second, factor, RATE_MATRIX)
    out_new = adam_step(out_weight, owned[1], out_first, out_second, factor, RATE_OUT)
    inner_new = adam_step(inner_weight, owned[2], inner_first, inner_second, factor, RATE_MATRIX)
    outer_new = adam_step(outer_weight, owned[3], outer_first, outer_second, factor, RATE_MATRIX)
    rel_new = adam_step(rel_bias, rel_grad, rel_first, rel_second, factor, RATE_SMALL)
    gain_new = adam_step(gains, gain_grad, gain_first, gain_second, factor, RATE_SMALL)
    return (
        block_out,
        input_grad,
        grad_norm,
        attn_new[0],
        attn_new[1],
        attn_new[2],
        out_new[0],
        out_new[1],
        out_new[2],
        inner_new[0],
        inner_new[1],
        inner_new[2],
        outer_new[0],
        outer_new[1],
        outer_new[2],
        rel_new[0],
        rel_new[1],
        rel_new[2],
        gain_new[0],
        gain_new[1],
        gain_new[2],
    )


def solution(mesh):
    in_specs = (
        P(("dp", "mp"), None),
        P(("dp", "mp"), None),
        P(None, "dp", "mp"),
        P("mp", "dp"),
        P("dp", "mp"),
        P("mp", "dp"),
        P(),
        P(),
        P("dp"),
        P(),
        P(None, "dp", "mp"),
        P(None, "dp", "mp"),
        P("mp", "dp"),
        P("mp", "dp"),
        P("dp", "mp"),
        P("dp", "mp"),
        P("mp", "dp"),
        P("mp", "dp"),
        P(),
        P(),
        P(),
        P(),
    )
    out_specs = (
        P(("dp", "mp"), None),
        P(("dp", "mp"), None),
        P(),
        P(None, "dp", "mp"),
        P(None, "dp", "mp"),
        P(None, "dp", "mp"),
        P("mp", "dp"),
        P("mp", "dp"),
        P("mp", "dp"),
        P("dp", "mp"),
        P("dp", "mp"),
        P("dp", "mp"),
        P("mp", "dp"),
        P("mp", "dp"),
        P("mp", "dp"),
        P(),
        P(),
        P(),
        P(),
        P(),
        P(),
    )
    return jax.shard_map(body, mesh=mesh, in_specs=in_specs, out_specs=out_specs, check_vma=False)
```

profile of v0, /device:TPU:0, one launch (start us, length us, event | category | flops | bytes accessed | tf_op | source)
XLA Modules:
  0.0 1506.9 jit_solution(15894192351887102508)
XLA Ops:
  14.6 14.6 all_gather.25
  32.8 4.8 broadcast_in_dim.92
  37.5 15.4 %reshape.223 = f32[2357760]{0:T(1024)} reshape(f32[3,512,1535]{2,1,0:T(8,128)} %broadcast_in_dim.92) | data formatting | bytes 18862080
  52.9 13.2 reshape.199
  66.1 7.2 pad.14
  73.3 6.4 copy.68
  79.7 6.6 slice.41
  86.3 48.4 %rev.12 = f32[3,512,1024]{2,1,0:T(8,128)} reverse(f32[3,512,1024]{2,1,0:T(8,128)} %slice.41), dimensions={1} | reverse | bytes 12582912 | tf_op jit(solution)/shard_map/rev | solution.py:41
  134.7 4.7 broadcast_in_dim.93
  139.4 15.5 %reshape.221 = f32[2357760]{0:T(1024)} reshape(f32[3,512,1535]{2,1,0:T(8,128)} %broadcast_in_dim.93) | data formatting | bytes 18862080
  154.9 13.1 reshape.201
  168.0 6.8 pad.15
  174.9 6.4 copy.67
  181.3 6.6 slice.42
  187.9 48.4 %rev.13 = f32[3,512,1024]{2,1,0:T(8,128)} reverse(f32[3,512,1024]{2,1,0:T(8,128)} %slice.42), dimensions={1} | reverse | bytes 12582912 | tf_op jit(solution)/shard_map/rev | solution.py:41
  236.3 8.5 all_gather.26
  244.8 12.0 pad_maximum_fusion
  261.4 52.2 %while.34 = (s32[]{:T(128)}, bf16[4,512,192]{1,2,0:T(8,128)(2,1)}, f32[4,3,512,1]{2,1,3,0:T(4,128)}, s32[4]{0:T(128)S(1)}, bf16[2048,192]{0,1:T(8,128)(2,1)S(1)}...) while((s32[]{:T(128)}, bf16[4,512,192]{1,2,0:T(8,128)(2,1)}, ...), condition=%wide.region_4.5_spmd.clone, body=%wide.region_1.4_spmd.clone.sunk | while | flops 415333920 | bytes 28758580 | solution.py:152
  325.8 139.2 %reduce-scatter.5.cloned.1.call-done = f32[512,768]{1,0:T(8,128)} async-done(((f32[2048,768]{1,0:T(8,128)}), f32[512,768]{1,0:T(8,128)}) %reduce-scatter.5.cloned.1.call-update) | async-done | bytes 1572880 | tf_op jit(solution)/shard_map/reduce_scatter | solution.py:156
  469.0 12.7 all-gather.15.cloned.1.call-done
  481.7 7.4 fusion.66
  489.1 18.4 %all-gather.11.cloned.1.call-done = bf16[768,768]{1,0:T(8,128)(2,1)} async-done(((bf16[96,768]{1,0:T(8,128)(2,1)}), bf16[768,768]{1,0:T(8,128)(2,1)}) %all-gather.11.cloned.1.call-update) | async-done | bytes 1179664 | tf_op jit(solution)/shard_map/all_gather | solution.py:89
  507.5 65.0 %all-gather.9.cloned.1.call-done = bf16[2048,768]{1,0:T(8,128)(2,1)} async-done(((bf16[512,768]{1,0:T(8,128)(2,1)}), bf16[2048,768]{1,0:T(8,128)(2,1)}) %all-gather.9.cloned.1.call-update) | async-done | bytes 3145744 | tf_op jit(solution)/shard_map/all_gather | solution.py:163
  572.4 10.0 fusion.30
  584.1 4.5 fusion.67
  589.8 8.3 convolution_convert_fusion
  598.2 99.8 %reduce-scatter.9.cloned.1.call-done = f32[512,768]{1,0:T(8,128)} async-done(((f32[2048,768]{1,0:T(8,128)}), f32[512,768]{1,0:T(8,128)}) %reduce-scatter.9.cloned.1.call-update) | async-done | bytes 1572880 | tf_op jit(solution)/shard_map/reduce_scatter | solution.py:178
  700.5 60.7 %reduce-scatter.7.cloned.1.call-done = bf16[512,768]{1,0:T(8,128)(2,1)} async-done(((bf16[2048,768]{1,0:T(8,128)(2,1)}), bf16[512,768]{1,0:T(8,128)(2,1)}) %reduce-scatter.7.cloned.1.call-update) | async-done | bytes 786448 | tf_op jit(solution)/shard_map/reduce_scatter | solution.py:166
  761.1 4.5 fusion.59
  765.7 7.1 fusion.69
  772.8 7.9 fusion.52
  780.7 48.5 %all-gather.17.cloned.1.call-done = bf16[2048,768]{1,0:T(8,128)(2,1)} async-done(((bf16[512,768]{1,0:T(8,128)(2,1)}), bf16[2048,768]{1,0:T(8,128)(2,1)}) %all-gather.17.cloned.1.call-update) | async-done | bytes 3145744 | tf_op jit(solution)/shard_map/all_gather | solution.py:186
  835.0 464.5 %while.35 = (s32[]{:T(128)}, f32[2048,3,64]{0,2,1:T(8,128)}, f32[2048,3,64]{0,2,1:T(8,128)}, f32[3,2047]{1,0:T(4,128)S(1)}, bf16[4,512,192]{1,2,0:T(8,128)(2,1)}...) while((s32[]{:T(128)}, f32[2048,3,64]{0,2,1:T(8,128)}, ...), condition=%wide.region_13.14_spmd.clone, body=%wide.region_10.13_spmd.clone.sunk | while | flops 1023539200 | bytes 190614352 | solution.py:230
  843.9 4.4 multiply_reduce_fusion.12
  856.3 31.6 %rev.16 = f32[3,512,1024]{2,1,0:T(8,128)} reverse(bf16[3,512,1024]{2,1,0:T(8,128)(2,1)S(1)} %multiply_convert_fusion.7), dimensions={1} | reverse | bytes 9437184 | tf_op jit(solution)/shard_map/while/body/eval_jaxpr/rev | solution.py:46
  891.9 19.9 %copy.70 = f32[1,3,512,1536]{3,1,2,0:T(4,128)S(1)} copy(f32[1,3,512,1536]{3,2,1,0:T(8,128)S(1)} %pad_bitcast_fusion.2) | data formatting | bytes 18874368 | tf_op jit(solution)/shard_map/while
  911.8 5.9 slice.49
  917.6 13.2 reshape.227
  930.8 15.6 %reshape.228 = f32[3,512,1535]{2,1,0:T(8,128)} reshape(f32[2357760]{0:T(1024)} %reshape.227) | data formatting | bytes 18862080 | tf_op jit(solution)/shard_map/while/body/eval_jaxpr/reshape | solution.py:48
  946.4 4.4 reduce_sum.186
  959.9 4.4 multiply_reduce_fusion.12
  972.3 31.6 %rev.16 = f32[3,512,1024]{2,1,0:T(8,128)} reverse(bf16[3,512,1024]{2,1,0:T(8,128)(2,1)S(1)} %multiply_convert_fusion.7), dimensions={1} | reverse | bytes 9437184 | tf_op jit(solution)/shard_map/while/body/eval_jaxpr/rev | solution.py:46
  1007.9 19.9 %copy.70 = f32[1,3,512,1536]{3,1,2,0:T(4,128)S(1)} copy(f32[1,3,512,1536]{3,2,1,0:T(8,128)S(1)} %pad_bitcast_fusion.2) | data formatting | bytes 18874368 | tf_op jit(solution)/shard_map/while
  1027.8 5.9 slice.49
  1033.7 13.2 reshape.227
  1046.8 15.6 %reshape.228 = f32[3,512,1535]{2,1,0:T(8,128)} reshape(f32[2357760]{0:T(1024)} %reshape.227) | data formatting | bytes 18862080 | tf_op jit(solution)/shard_map/while/body/eval_jaxpr/reshape | solution.py:48
  1062.4 4.4 reduce_sum.186
  1076.0 4.4 multiply_reduce_fusion.12
  1088.3 31.6 %rev.16 = f32[3,512,1024]{2,1,0:T(8,128)} reverse(bf16[3,512,1024]{2,1,0:T(8,128)(2,1)S(1)} %multiply_convert_fusion.7), dimensions={1} | reverse | bytes 9437184 | tf_op jit(solution)/shard_map/while/body/eval_jaxpr/rev | solution.py:46
  1124.0 19.9 %copy.70 = f32[1,3,512,1536]{3,1,2,0:T(4,128)S(1)} copy(f32[1,3,512,1536]{3,2,1,0:T(8,128)S(1)} %pad_bitcast_fusion.2) | data formatting | bytes 18874368 | tf_op jit(solution)/shard_map/while
  1143.8 5.9 slice.49
  1149.7 13.2 reshape.227
  1162.9 15.6 %reshape.228 = f32[3,512,1535]{2,1,0:T(8,128)} reshape(f32[2357760]{0:T(1024)} %reshape.227) | data formatting | bytes 18862080 | tf_op jit(solution)/shard_map/while/body/eval_jaxpr/reshape | solution.py:48
  1178.5 4.4 reduce_sum.186
  1192.0 4.4 multiply_reduce_fusion.12
  1204.4 31.6 %rev.16 = f32[3,512,1024]{2,1,0:T(8,128)} reverse(bf16[3,512,1024]{2,1,0:T(8,128)(2,1)S(1)} %multiply_convert_fusion.7), dimensions={1} | reverse | bytes 9437184 | tf_op jit(solution)/shard_map/while/body/eval_jaxpr/rev | solution.py:46
  1240.0 19.9 %copy.70 = f32[1,3,512,1536]{3,1,2,0:T(4,128)S(1)} copy(f32[1,3,512,1536]{3,2,1,0:T(8,128)S(1)} %pad_bitcast_fusion.2) | data formatting | bytes 18874368 | tf_op jit(solution)/shard_map/while
  1259.9 5.9 slice.49
  1265.7 13.2 reshape.227
  1278.9 15.6 %reshape.228 = f32[3,512,1535]{2,1,0:T(8,128)} reshape(f32[2357760]{0:T(1024)} %reshape.227) | data formatting | bytes 18862080 | tf_op jit(solution)/shard_map/while/body/eval_jaxpr/reshape | solution.py:48
  1294.5 4.4 reduce_sum.186
  1314.1 4.1 convolution_convert_fusion.1
  1319.7 111.0 %all-reduce.7.cloned.1.call-done = (f32[3,768,192]{2,1,0:T(8,128)}, f32[192,768]{1,0:T(8,128)}, f32[768,768]{1,0:T(8,128)}, f32[768,768]{0,1:T(8,128)}) async-done(((f32[3,768,192]{2,1,0:T(8,128)}, f32[192,768]{1,0:T(8,128)}, f32[768,768]{1,0:T(8,128)}, f32[768,768]{0,1:T(8,128)}), (f32[3,768,192]{2,1,0:T(8,128)}, f32[192,768]{1,0:T(8,128)}, f32[768,768]{1,0:T(8,128)}, ...) | async-done | bytes 7077904 | tf_op jit(solution)/shard_map/psum | solution.py:258
  1443.0 39.9 %all-reduce.3 = (f32[]{:T(128)}, f32[2,768]{1,0:T(2,128)}, f32[32,12]{0,1:T(8,128)S(1)}) all-reduce(f32[]{:T(128)S(6)} %add.359, f32[2,768]{1,0:T(2,128)} %pad_maximum_fusion.4, f32[32,12]{0,1:T(8,128)} %copy-done.39), channel_id=1, replica_groups=mesh['dp'=8,'mp'=4] {'dp','mp'}, use_global_device_ids=true, to_apply=%region_24.25 | all-reduce | flops 1921 | bytes 15368 | tf_op jit(solution)/shard_map/psum | solution.py:278
  (337 shorter events, 190.2 us)
Async XLA Ops:
  8.0 6.3 copy-start.28
  8.0 6.4 copy-start.18
  8.0 248.7 %all-gather.7.cloned.1.call-start = ((), (), s32[]{:S(2)}) async-start(), calls=%async_computation.4 | async-start | bytes 3932160 | tf_op jit(solution)/shard_map/all_gather | solution.py:102
  14.2 17.1 %copy-start.55 = (s32[2047]{0:T(1024)S(1)}, s32[2047]{0:T(1024)}, u32[]{:S(2)}) copy-start(s32[2047]{0:T(1024)} %param.35) | copy-start | bytes 24568
  14.2 450.7 %reduce-scatter.5.cloned.1.call-start = ((), (), s32[]{:S(2)}) async-start(), calls=%async_computation.5 | async-start | bytes 7864320 | tf_op jit(solution)/shard_map/reduce_scatter | solution.py:156
  244.8 12.0 copy-start.20
  313.6 6.1 copy-start.11
  319.7 145.2 %copy-start = (f32[512,768]{1,0:T(8,128)S(1)}, f32[512,768]{1,0:T(8,128)}, u32[]{:S(2)}) copy-start(f32[512,768]{1,0:T(8,128)} %param.26) | copy-start | bytes 4718596
  319.7 149.2 %all-gather.13.cloned.1.call-start = ((), (), s32[]{:S(2)}) async-start(), calls=%async_computation.8 | async-start | bytes 1327104 | tf_op jit(solution)/shard_map/all_gather | solution.py:90
  321.6 160.1 %all-gather.15.cloned.1.call-start = ((), (), s32[]{:S(2)}) async-start(), calls=%async_computation.10 | async-start | bytes 3932160 | tf_op jit(solution)/shard_map/all_gather | solution.py:172
  324.0 143.8 %copy-start.36 = (f32[768]{0:T(1024)S(1)}, f32[768]{0:T(1024)}, u32[]{:S(2)}) copy-start(f32[768]{0:T(1024)} %get-tuple-element.389) | copy-start | bytes 9220
  324.0 183.5 %all-gather.11.cloned.1.call-start = ((), (), s32[]{:S(2)}) async-start(), calls=%async_computation.7 | async-start | bytes 1327104 | tf_op jit(solution)/shard_map/all_gather | solution.py:89
  325.7 246.7 %all-gather.9.cloned.1.call-start = ((), (), s32[]{:S(2)}) async-start(), calls=%async_computation.6 | async-start | bytes 3932160 | tf_op jit(solution)/shard_map/all_gather | solution.py:163
  468.9 229.1 %reduce-scatter.9.cloned.1.call-start = ((), (), s32[]{:S(2)}) async-start(), calls=%async_computation.11 | async-start | bytes 7864320 | tf_op jit(solution)/shard_map/reduce_scatter | solution.py:178
  507.5 76.6 %copy-start.54 = (bf16[768,768]{1,0:T(8,128)(2,1)S(1)}, bf16[768,768]{1,0:T(8,128)(2,1)}, u32[]{:S(2)}) copy-start(bf16[768,768]{1,0:T(8,128)(2,1)} %all-gather.11.cloned.1.call-done) | copy-start | bytes 3538948
  588.6 172.6 %reduce-scatter.7.cloned.1.call-start = ((), (), s32[]{:S(2)}) async-start(), calls=%async_computation.9 | async-start | bytes 3932160 | tf_op jit(solution)/shard_map/reduce_scatter | solution.py:166
  598.1 99.9 %copy-start.8 = (f32[512,768]{1,0:T(8,128)S(1)}, f32[512,768]{1,0:T(8,128)}, u32[]{:S(2)}) copy-start(f32[512,768]{1,0:T(8,128)} %copy-done.7) | copy-start | bytes 4718596
  598.1 231.1 %all-gather.17.cloned.1.call-start = ((), (), s32[]{:S(2)}) async-start(), calls=%async_computation.12 | async-start | bytes 3932160 | tf_op jit(solution)/shard_map/all_gather | solution.py:186
  765.6 665.1 %all-reduce.7.cloned.1.call-start = ((), (), s32[]{:S(2)}) async-start(), calls=%async_computation.14 | async-start | bytes 15335424 | tf_op jit(solution)/shard_map/psum | solution.py:258
  765.7 7.1 copy-start.52
  835.2 8.7 copy-start.3
  835.2 8.7 copy-start.5
  835.2 8.7 copy-start.13
  946.4 4.8 copy-start.14
  951.2 8.7 copy-start.3
  951.2 8.7 copy-start.5
  951.2 8.7 copy-start.13
  1062.4 4.9 copy-start.4
  1062.4 4.9 copy-start.6
  1062.4 4.9 copy-start.14
  1067.3 8.7 copy-start.3
  1067.3 8.7 copy-start.5
  1067.3 8.7 copy-start.13
  1183.3 8.7 copy-start.3
  1183.3 8.7 copy-start.5
  1183.3 8.7 copy-start.13
  1294.5 4.9 copy-start.4
  1294.5 4.9 copy-start.6
  1294.5 4.9 copy-start.14
  1301.0 5.5 copy-start.22
  1312.3 127.7 %reduce-scatter.11.cloned.1.call-start = ((), (), s32[]{:S(2)}) async-start(), calls=%async_computation.13 | async-start | bytes 3932160 | tf_op jit(solution)/shard_map/reduce_scatter | solution.py:243
  1318.3 121.7 %copy-start.1 = (f32[512,768]{1,0:T(8,128)S(1)}, f32[512,768]{1,0:T(8,128)}, u32[]{:S(2)}) copy-start(f32[512,768]{1,0:T(8,128)} %param.26) | copy-start | bytes 4718596
  1318.3 121.7 %copy-start.38 = (f32[768]{0:T(1024)S(1)}, f32[768]{0:T(1024)}, u32[]{:S(2)}) copy-start(f32[768]{0:T(1024)} %copy-done.37) | copy-start | bytes 9220
  1318.3 121.7 %copy-start.41 = (f32[512]{0:T(512)S(1)}, f32[512]{0:T(512)}, u32[]{:S(2)}) copy-start(f32[512]{0:T(512)} %copy-done.40) | copy-start | bytes 6148
  1318.3 168.6 %copy-start.16 = (f32[768,96]{0,1:T(8,128)S(1)}, f32[768,96]{0,1:T(8,128)}, u32[]{:S(2)}) copy-start(f32[768,96]{0,1:T(8,128)} %param.31) | copy-start | bytes 884740
  1318.3 168.6 %copy-start.30 = (f32[768,96]{0,1:T(8,128)S(1)}, f32[768,96]{0,1:T(8,128)}, u32[]{:S(2)}) copy-start(f32[768,96]{0,1:T(8,128)} %param.42) | copy-start | bytes 884740
  1318.3 168.6 %copy-start.31 = (f32[768,96]{0,1:T(8,128)S(1)}, f32[768,96]{0,1:T(8,128)}, u32[]{:S(2)}) copy-start(f32[768,96]{0,1:T(8,128)} %param.43) | copy-start | bytes 884740
  1318.4 171.0 %copy-start.17 = (f32[96,768]{1,0:T(8,128)S(1)}, f32[96,768]{1,0:T(8,128)}, u32[]{:S(2)}) copy-start(f32[96,768]{1,0:T(8,128)} %param.30) | copy-start | bytes 884740
  1319.7 119.6 %copy-start.39 = (f32[32,12]{0,1:T(8,128)}, f32[32,12]{0,1:T(8,128)S(1)}, u32[]{:S(2)}) copy-start(f32[32,12]{0,1:T(8,128)S(1)} %dynamic_update_slice.42) | copy-start | bytes 4612
  1439.9 51.6 %copy-start.19 = (f32[3,96,192]{2,1,0:T(8,128)S(1)}, f32[3,96,192]{2,1,0:T(8,128)}, u32[]{:S(2)}) copy-start(f32[3,96,192]{2,1,0:T(8,128)} %param.28) | copy-start | bytes 663556
  1439.9 51.6 %copy-start.32 = (f32[3,96,192]{2,1,0:T(8,128)S(1)}, f32[3,96,192]{2,1,0:T(8,128)}, u32[]{:S(2)}) copy-start(f32[3,96,192]{2,1,0:T(8,128)} %param.36) | copy-start | bytes 663556
  1441.8 51.8 %copy-start.29 = (f32[192,96]{1,0:T(8,128)S(1)}, f32[192,96]{1,0:T(8,128)}, u32[]{:S(2)}) copy-start(f32[192,96]{1,0:T(8,128)} %param.29) | copy-start | bytes 221188
  1441.8 51.8 %copy-start.34 = (f32[192,96]{1,0:T(8,128)S(1)}, f32[192,96]{1,0:T(8,128)}, u32[]{:S(2)}) copy-start(f32[192,96]{1,0:T(8,128)} %param.38) | copy-start | bytes 221188
  1486.9 6.7 copy-start.35
  1486.9 8.5 copy-start.42
  1486.9 8.5 copy-start.43
  1487.0 8.4 copy-start.49
  1487.0 8.4 copy-start.50
  1487.0 9.1 copy-start.46
  1487.0 9.1 copy-start.47
  1487.0 9.0 copy-start.48
  1487.0 9.7 copy-start.12
  1487.0 9.7 copy-start.15
  1487.0 9.6 copy-start.45
  (24 other events, 60.6 us)
Sparse Core Ops, SparseCore 0:
  14.4 66.1 all-gather.6
  319.8 145.0 reduce-scatter.4
  765.8 63.3 all-gather.16
  1318.5 58.8 reduce-scatter.10
Sparse Core Ops, SparseCore 1:
  322.7 24.2 all-gather.12
  348.9 132.7 all-gather.14
  484.0 23.4 all-gather.10
  509.1 63.3 all-gather.8
  588.7 109.3 reduce-scatter.8
  700.3 60.8 reduce-scatter.6
  1312.4 118.3 all-reduce.6
where the time goes:
time: 1530 us; the launch traced here: 1510 us
  local copies, waits for them, and re-layouts  609 us (40%)
  waiting for transfers between devices  555 us (36%)
  matrix products  139 us (9%)
  other arithmetic  90.3 us (6%)
  blocking collectives  63.1 us (4%)
  loops' own time  27.7 us (2%)
  between operations  22.1 us (1%)
    while x60, local copies, waits for them, and re-layouts  148 us
    reduce_scatter x1, waiting for transfers between devices, body(): lax.psum_scatter(jnp.dot(context, w_out, preferred_element_type=jnp.float...  139 us
    rev x4, local copies, waits for them, and re-layouts, diag_sums(): flipped = jnp.pad(matrix[:, ::-1, :], ((0, 0), (0, 0), (0, block)))  126 us
    psum x1, waiting for transfers between devices, body(): lax.psum((partials[0], partials[1], partials[2], partials[3]), 'dp')  111 us
    reduce_scatter x1, waiting for transfers between devices, body(): lax.psum_scatter(jnp.einsum('tf,df->td', inner_back, w_inner, preferred_e...  99.8 us
    rev x2, local copies, waits for them, and re-layouts, toeplitz(): return spread[:, ::-1, :length]  96.8 us
    all_gather x1, waiting for transfers between devices, body(): rows_two = lax.all_gather(normed_two, 'mp', axis=0, tiled=True)  65 us
    reshape x4, local copies, waits for them, and re-layouts, diag_sums(): return jnp.sum(flat.reshape(heads, block, length + block - 1), axis=1)  62.3 us
  transfers between devices with their start and end apart: 11, of which 8 were waited for; matrix products, arithmetic and copies ran while one was open for 18% of the time, Pallas kernels for 0%

commit v1 on v0

v1 whole, which is shorter than its diff:
```python
import functools

import jax
import jax.numpy as jnp
from jax import lax
from jax.experimental import pallas as pl
from jax.experimental.pallas import tpu as pltpu
from jax.sharding import PartitionSpec as P

HDIM = 64
SEQLEN = 1024
STEP = 10
NORM_EPS = 1e-06
CLIP = 1.0
BETA_ONE = 0.9
BETA_TWO = 0.999
ADAM_EPS = 1e-08
DECAY = 0.01
RATE_MATRIX = 0.05
RATE_OUT = 0.6
RATE_SMALL = 1.0

F32 = jnp.float32
BF16 = jnp.bfloat16
LANES = 128
NEG = -1e30

HEAD_AT = ((0, 0, 1, 2, 0), (0, 1, 1, 2, 1), (4, 0, 5, 4, 1))


def mm(a, b):
    return lax.dot_general(a, b, (((1,), (0,)), ((), ())), preferred_element_type=F32)


def mt(a, b):
    return lax.dot_general(a, b, (((1,), (1,)), ((), ())), preferred_element_type=F32)


def rms_scaled(value, gain):
    return value * lax.rsqrt(jnp.mean(value * value, axis=-1, keepdims=True) + NORM_EPS) * gain


def rms_back(value, gain, grad):
    factor = lax.rsqrt(jnp.mean(value * value, axis=-1, keepdims=True) + NORM_EPS)
    unit = value * factor
    gain_part = jnp.sum(grad * unit, axis=0, keepdims=True)
    scaled = grad * gain
    result = factor * (scaled - unit * jnp.mean(scaled * unit, axis=-1, keepdims=True))
    return (result, gain_part)


def adam_step(master, grad, first, second, factor, rate):
    clipped = grad * factor
    first_new = BETA_ONE * first + (1.0 - BETA_ONE) * clipped
    second_new = BETA_TWO * second + (1.0 - BETA_TWO) * clipped * clipped
    first_hat = first_new / (1.0 - BETA_ONE**STEP)
    second_hat = second_new / (1.0 - BETA_TWO**STEP)
    master_new = master - rate * (first_hat / (jnp.sqrt(second_hat) + ADAM_EPS) + DECAY * master)
    return (master_new, first_new, second_new)


def half_rows(half):
    lane = lax.broadcasted_iota(jnp.int32, (1, LANES), 1)
    keep = (lane < HDIM) if half == 0 else (lane >= HDIM)
    return keep.astype(F32).astype(BF16)


def bias_tile(line):
    wide = jnp.broadcast_to(line, (LANES, 4 * LANES))
    return pltpu.roll(wide, 0, 1, stride=1, stride_axis=0)


def near_parts(tile):
    return tile[:, LANES : 2 * LANES], tile[:, :LANES], tile[:, 3 * LANES :]


def corner_parts(tile, line, flags):
    before, same, after = near_parts(tile)
    first = (after - line[:, 3 * LANES : 3 * LANES + 1]) * flags[0]
    last = (before - line[:, LANES : LANES + 1]) * flags[1]
    return first, last


def add_bias(scores, tile, line, flags, nq):
    parts = near_parts(tile)
    corner = corner_parts(tile, line, flags)
    rows = []
    for jb in range(2 * nq):
        row = []
        for ib in range(nq):
            block = scores[jb * LANES : (jb + 1) * LANES, ib * LANES : (ib + 1) * LANES]
            if jb < nq and abs(jb - ib) <= 1:
                block = block + parts[jb - ib + 1]
            elif jb == nq and ib == nq - 1:
                block = block + corner[0]
            elif jb == 2 * nq - 1 and ib == 0:
                block = block + corner[1]
            row.append(block)
        rows.append(jnp.concatenate(row, axis=1))
    return rows


def query_aug(qaug, i, nq):
    rows = qaug.shape[0]
    return jnp.concatenate(
        [jnp.broadcast_to(qaug[i * nq + ib : i * nq + ib + 1, :], (LANES, LANES)) for ib in range(nq)], axis=0
    )


def forward_kernel(
    x_ref, xo_ref, w_ref, line_ref, qaug_ref, kaug_ref, hidden_ref,
    own_ref, oth_ref, ctx_ref, lse_ref, middle_ref,
    acc, s_ref, e_ref,
):
    m = pl.program_id(0)
    tokens = x_ref.shape[0]
    nq = tokens // LANES
    x, xo = x_ref[...], xo_ref[...]
    p_a = mm(x, w_ref[:, : 3 * LANES]).astype(BF16)
    p_b = mm(x, w_ref[:, 4 * LANES :]).astype(BF16)
    o_a = mm(xo, w_ref[:, LANES : 3 * LANES]).astype(BF16)
    o_b = mm(xo, w_ref[:, 4 * LANES :]).astype(BF16)
    own_ref[0, :, : 3 * LANES] = p_a
    own_ref[0, :, 3 * LANES :] = p_b
    oth_ref[0, :, : 2 * LANES] = o_a
    oth_ref[0, :, 2 * LANES :] = o_b
    cols_own = {0: p_a[:, :LANES], 1: p_a[:, LANES : 2 * LANES], 2: p_a[:, 2 * LANES :], 4: p_b[:, :LANES], 5: p_b[:, LANES:]}
    cols_oth = {1: o_a[:, :LANES], 2: o_a[:, LANES:], 4: o_b[:, :LANES], 5: o_b[:, LANES:]}
    both = {c: jnp.concatenate([cols_own[c], cols_oth[c]], axis=0) for c in (1, 2, 4, 5)}
    masks = [half_rows(0), half_rows(1)]
    flags = (line_ref[0, 3:4, :LANES], line_ref[0, 4:5, :LANES])
    v_t = {2: both[2].T, 4: both[4].T}
    count = lax.broadcasted_iota(jnp.int32, (HDIM, 2 * tokens), 0)
    ones = (count == 0).astype(F32).astype(BF16)
    pieces = []
    stats = []
    for i, (qc, qh, kc, vc, vh) in enumerate(HEAD_AT):
        line = line_ref[0, i : i + 1, :]
        tile = bias_tile(line)
        qa = cols_own[qc] * masks[qh] + query_aug(qaug_ref[0], i, nq) * masks[1 - qh]
        ka = both[kc] * masks[qh] + kaug_ref[...] * masks[1 - qh]
        scores = mt(ka, qa)
        peak = None
        for jb, row in enumerate(add_bias(scores, tile, line, flags, nq)):
            s_ref[i, jb * LANES : (jb + 1) * LANES, :] = row
            top = jnp.max(row.reshape(LANES // 8, 8, tokens), axis=0)
            peak = top if peak is None else jnp.maximum(peak, top)
        peak = jnp.max(peak, axis=0, keepdims=True)
        for jb in range(2 * nq):
            rows = slice(jb * LANES, (jb + 1) * LANES)
            e_ref[i, rows, :] = jnp.exp(s_ref[i, rows, :] - peak).astype(BF16)
        if vh == 0:
            va = jnp.concatenate([v_t[vc][:HDIM], ones], axis=0)
        else:
            va = jnp.concatenate([ones, v_t[vc][HDIM:]], axis=0)
        ot = mm(va, e_ref[i])
        at = HDIM if vh == 0 else 0
        total = ot[at : at + 1, :]
        stats.append(peak + jnp.log(total))
        real = ot[:HDIM] if vh == 0 else ot[HDIM:]
        pieces.append(real / total)
    zero = jnp.zeros((HDIM, tokens), F32)
    ctx_a = jnp.concatenate([pieces[0], pieces[1]], axis=0).T.astype(BF16)
    ctx_b = jnp.concatenate([zero, pieces[2]], axis=0).T.astype(BF16)
    ctx_ref[0, :, :LANES] = ctx_a
    ctx_ref[0, :, LANES:] = ctx_b
    for i in range(3):
        lse_ref[0, i : i + 1, :] = stats[i]
    lse_ref[0, 3:8, :] = jnp.zeros((5, tokens), F32)
    part = mt(ctx_a, w_ref[:, 3 * LANES : 4 * LANES]) + mt(ctx_b, w_ref[:, 5 * LANES :])

    @pl.when(m == 0)
    def _():
        acc[...] = hidden_ref[...] + part

    @pl.when(m > 0)
    def _():
        acc[...] += part

    @pl.when(m == pl.num_programs(0) - 1)
    def _():
        middle_ref[...] = acc[...]


def feed_kernel(
    middle_ref, grad_ref, gain_ref, wi_ref, wo_ref,
    out_ref, back_ref, gain_grad_ref, gi_ref, go_ref,
    x2_ref, x2t_ref, ob_ref, obt_ref, acc_out, acc_two,
):
    f = pl.program_id(0)

    @pl.when(f == 0)
    def _():
        x2 = rms_scaled(middle_ref[...], gain_ref[1:2, :]).astype(BF16)
        x2_ref[...] = x2
        x2t_ref[...] = x2.T
        ob = grad_ref[...].astype(BF16)
        ob_ref[...] = ob
        obt_ref[...] = ob.T
        acc_out[...] = jnp.zeros_like(acc_out)
        acc_two[...] = jnp.zeros_like(acc_two)

    inner = mm(x2_ref[...], wi_ref[...])
    active_back = mm(ob_ref[...], wo_ref[...])
    c = 0.7978845608028654
    sq = inner * inner
    th = jnp.tanh(c * (inner + 0.044715 * (sq * inner)))
    half = 0.5 * (1.0 + th)
    active = (inner * half).astype(BF16)
    slope = half + (0.5 * c) * inner * (1.0 - th * th) * (1.0 + (3 * 0.044715) * sq)
    inner_back = (slope * active_back).astype(BF16)
    acc_out[...] += mt(active, wo_ref[...])
    acc_two[...] += mt(inner_back, wi_ref[...])
    go_ref[...] = mm(obt_ref[...], active).astype(go_ref.dtype)
    gi_ref[...] = mm(x2t_ref[...], inner_back).astype(gi_ref.dtype)

    @pl.when(f == pl.num_programs(0) - 1)
    def _():
        out_ref[...] = middle_ref[...] + acc_out[...]
        result, gain_part = rms_back(middle_ref[...], gain_ref[1:2, :], acc_two[...])
        back_ref[...] = grad_ref[...] + result
        gain_grad_ref[...] = jnp.broadcast_to(gain_part, gain_grad_ref.shape)


def backward_kernel(
    x_ref, xo_ref, back_ref, w_ref, line_ref, qaug_ref, kaug_ref, own_ref, oth_ref, ctx_ref, lse_ref,
    ga_ref, one_own_ref, one_oth_ref, near_ref, sums_ref,
    xt_ref, xot_ref, ab_ref, abt_ref, acc_own, acc_oth,
):
    m = pl.program_id(0)
    tokens = x_ref.shape[0]
    nq = tokens // LANES

    @pl.when(m == 0)
    def _():
        xt_ref[...] = x_ref[...].T
        xot_ref[...] = xo_ref[...].T
        ab = back_ref[...].astype(BF16)
        ab_ref[...] = ab
        abt_ref[...] = ab.T
        acc_own[...] = jnp.zeros_like(acc_own)
        acc_oth[...] = jnp.zeros_like(acc_oth)

    ab = ab_ref[...]
    cb = {2: mm(ab, w_ref[:, 3 * LANES : 4 * LANES]).astype(BF16), 4: mm(ab, w_ref[:, 5 * LANES :]).astype(BF16)}
    ctx = {2: ctx_ref[0, :, :LANES], 4: ctx_ref[0, :, LANES:]}
    own = {c: own_ref[0, :, at * LANES : (at + 1) * LANES] for at, c in enumerate((0, 1, 2, 4, 5))}
    oth = {c: oth_ref[0, :, at * LANES : (at + 1) * LANES] for at, c in enumerate((1, 2, 4, 5))}
    masks = [half_rows(0), half_rows(1)]
    flags = (line_ref[0, 3:4, :LANES], line_ref[0, 4:5, :LANES])
    prod = {c: cb[c].astype(F32) * ctx[c].astype(F32) for c in (2, 4)}
    prod_hi = {c: prod[c].astype(BF16) for c in prod}
    prod_lo = {c: (prod[c] - prod_hi[c].astype(F32)).astype(BF16) for c in prod}
    dq_t = []
    dk = {}
    dv = {}
    for i, (qc, qh, kc, vc, vh) in enumerate(HEAD_AT):
        line = line_ref[0, i : i + 1, :]
        tile = bias_tile(line)
        qm = own[qc] * masks[qh]
        qa = qm + query_aug(qaug_ref[0], i, nq) * masks[1 - qh]
        om = cb[vc] * masks[vh]
        pick = jnp.broadcast_to(masks[vh], (8, LANES))
        center = (mt(pick, prod_hi[vc]) + mt(pick, prod_lo[vc]))[0:1, :]
        lse = lse_ref[0, i : i + 1, :]
        kaug = kaug_ref[...] * masks[1 - qh]
        dqt = None
        parts = near_parts(tile)
        corner = corner_parts(tile, line, flags)
        near = [None, None, None, None, None]
        for side, cols in enumerate((own, oth)):
            ka = cols[kc] * masks[qh] + kaug[side * tokens : (side + 1) * tokens]
            scores = mt(ka, qa)
            chance_back = mt(cols[vc], om)
            ps, ds = [], []
            for jb in range(nq):
                row_s, row_p, row_d = [], [], []
                for ib in range(nq):
                    at = (slice(jb * LANES, (jb + 1) * LANES), slice(ib * LANES, (ib + 1) * LANES))
                    block = scores[at]
                    kind = None
                    if side == 0 and abs(jb - ib) <= 1:
                        block = block + parts[jb - ib + 1]
                        kind = jb - ib + 1
                    elif side == 1 and jb == 0 and ib == nq - 1:
                        block = block + corner[0]
                        kind = 3
                    elif side == 1 and jb == nq - 1 and ib == 0:
                        block = block + corner[1]
                        kind = 4
                    p = jnp.exp(block - lse[:, at[1]])
                    d = p * (chance_back[at] - center[:, at[1]])
                    if kind is not None:
                        near[kind] = d if near[kind] is None else near[kind] + d
                    row_p.append(p.astype(BF16))
                    row_d.append(d.astype(BF16))
                ps.append(jnp.concatenate(row_p, axis=1))
                ds.append(jnp.concatenate(row_d, axis=1))
            pb = jnp.concatenate(ps, axis=0)
            db = jnp.concatenate(ds, axis=0)
            part_v = mm(pb, om)
            part_k = mm(db, qm)
            dv[vc, side] = part_v if (vc, side) not in dv else dv[vc, side] + part_v
            dk[kc, side] = part_k if (kc, side) not in dk else dk[kc, side] + part_k
            part_q = mm(ka.T, db)
            dqt = part_q if dqt is None else dqt + part_q
        at = HDIM if qh == 0 else 0
        sums_ref[0, i * 8 : (i + 1) * 8, :] = dqt[at + 8 : at + 16, :]
        dq_t.append(dqt[:HDIM] if qh == 0 else dqt[HDIM:])
        for kind in range(5):
            near_ref[0, i, kind] = near[kind]
    dq_a = jnp.concatenate([dq_t[0], dq_t[1]], axis=0).T
    dq_b = jnp.concatenate([dq_t[2], jnp.zeros_like(dq_t[2])], axis=0).T
    d_own = jnp.concatenate([dq_a, dk[1, 0], dv[2, 0], dq_b + dv[4, 0], dk[5, 0]], axis=1).astype(BF16)
    d_oth = jnp.concatenate([dk[1, 1], dv[2, 1], dv[4, 1], dk[5, 1]], axis=1).astype(BF16)
    xt, xot, abt = xt_ref[...], xot_ref[...], abt_ref[...]
    g_own = mm(xt, d_own)
    g_oth = mm(xot, d_oth)
    g_ctx = mm(abt, ctx_ref[0])
    ga_ref[:, :LANES] = g_own[:, :LANES].astype(ga_ref.dtype)
    ga_ref[:, LANES : 3 * LANES] = (g_own[:, LANES : 3 * LANES] + g_oth[:, : 2 * LANES]).astype(ga_ref.dtype)
    ga_ref[:, 3 * LANES : 4 * LANES] = g_ctx[:, :LANES].astype(ga_ref.dtype)
    ga_ref[:, 4 * LANES : 5 * LANES] = (g_own[:, 3 * LANES : 4 * LANES] + g_oth[:, 2 * LANES : 3 * LANES]).astype(ga_ref.dtype)
    ga_ref[:, 5 * LANES :] = (g_own[:, 4 * LANES :] + g_oth[:, 3 * LANES :] + g_ctx[:, LANES:]).astype(ga_ref.dtype)
    acc_own[...] += mt(d_own[:, : 3 * LANES], w_ref[:, : 3 * LANES]) + mt(d_own[:, 3 * LANES :], w_ref[:, 4 * LANES :])
    acc_oth[...] += mt(d_oth[:, : 2 * LANES], w_ref[:, LANES : 3 * LANES]) + mt(d_oth[:, 2 * LANES :], w_ref[:, 4 * LANES :])

    @pl.when(m == pl.num_programs(0) - 1)
    def _():
        one_own_ref[...] = acc_own[...]
        one_oth_ref[...] = acc_oth[...].astype(one_oth_ref.dtype)


def whole(shape):
    return pl.BlockSpec(shape, lambda m: (0,) * len(shape))


def params():
    return pltpu.CompilerParams(vmem_limit_bytes=60 * 2**20)


def run_forward(x, xo, wa, line, qaug, kaug, hidden, parts):
    t, d = x.shape
    return pl.pallas_call(
        forward_kernel,
        grid=(parts,),
        in_specs=[
            whole((t, d)), whole((t, d)),
            pl.BlockSpec((d, 6 * LANES), lambda m: (0, m)),
            pl.BlockSpec((1, 8, 4 * LANES), lambda m: (m, 0, 0)),
            pl.BlockSpec((1, 16, LANES), lambda m: (m, 0, 0)),
            whole((2 * t, LANES)), whole((t, d)),
        ],
        out_specs=[
            pl.BlockSpec((1, t, 5 * LANES), lambda m: (m, 0, 0)),
            pl.BlockSpec((1, t, 4 * LANES), lambda m: (m, 0, 0)),
            pl.BlockSpec((1, t, 2 * LANES), lambda m: (m, 0, 0)),
            pl.BlockSpec((1, 8, t), lambda m: (m, 0, 0)),
            whole((t, d)),
        ],
        out_shape=[
            jax.ShapeDtypeStruct((parts, t, 5 * LANES), BF16),
            jax.ShapeDtypeStruct((parts, t, 4 * LANES), BF16),
            jax.ShapeDtypeStruct((parts, t, 2 * LANES), BF16),
            jax.ShapeDtypeStruct((parts, 8, t), F32),
            jax.ShapeDtypeStruct((t, d), F32),
        ],
        scratch_shapes=[
            pltpu.VMEM((t, d), F32),
            pltpu.VMEM((3, 2 * t, t), F32),
            pltpu.VMEM((3, 2 * t, t), BF16),
        ],
        compiler_params=params(),
        name="attend_forward",
    )(x, xo, wa, line, qaug, kaug, hidden)


def run_feed(middle, grad, gains, wi, wo):
    t, d = middle.shape
    units = wi.shape[1]
    tile = min(512, units)
    return pl.pallas_call(
        feed_kernel,
        grid=(units // tile,),
        in_specs=[
            whole((t, d)), whole((t, d)), whole((2, d)),
            pl.BlockSpec((d, tile), lambda f: (0, f)),
            pl.BlockSpec((d, tile), lambda f: (0, f)),
        ],
        out_specs=[
            whole((t, d)), whole((t, d)), whole((8, d)),
            pl.BlockSpec((d, tile), lambda f: (0, f)),
            pl.BlockSpec((d, tile), lambda f: (0, f)),
        ],
        out_shape=[
            jax.ShapeDtypeStruct((t, d), F32),
            jax.ShapeDtypeStruct((t, d), F32),
            jax.ShapeDtypeStruct((8, d), F32),
            jax.ShapeDtypeStruct((d, units), BF16),
            jax.ShapeDtypeStruct((d, units), BF16),
        ],
        scratch_shapes=[
            pltpu.VMEM((t, d), BF16), pltpu.VMEM((d, t), BF16),
            pltpu.VMEM((t, d), BF16), pltpu.VMEM((d, t), BF16),
            pltpu.VMEM((t, d), F32), pltpu.VMEM((t, d), F32),
        ],
        compiler_params=params(),
        name="feed_both",
    )(middle, grad, gains, wi, wo)


def run_backward(x, xo, back, wa, line, qaug, kaug, own, oth, ctx, lse, parts):
    t, d = x.shape
    return pl.pallas_call(
        backward_kernel,
        grid=(parts,),
        in_specs=[
            whole((t, d)), whole((t, d)), whole((t, d)),
            pl.BlockSpec((d, 6 * LANES), lambda m: (0, m)),
            pl.BlockSpec((1, 8, 4 * LANES), lambda m: (m, 0, 0)),
            pl.BlockSpec((1, 16, LANES), lambda m: (m, 0, 0)),
            whole((2 * t, LANES)),
            pl.BlockSpec((1, t, 5 * LANES), lambda m: (m, 0, 0)),
            pl.BlockSpec((1, t, 4 * LANES), lambda m: (m, 0, 0)),
            pl.BlockSpec((1, t, 2 * LANES), lambda m: (m, 0, 0)),
            pl.BlockSpec((1, 8, t), lambda m: (m, 0, 0)),
        ],
        out_specs=[
            pl.BlockSpec((d, 6 * LANES), lambda m: (0, m)),
            whole((t, d)), whole((t, d)),
            pl.BlockSpec((1, 3, 5, LANES, LANES), lambda m: (m, 0, 0, 0, 0)),
            pl.BlockSpec((1, 24, t), lambda m: (m, 0, 0)),
        ],
        out_shape=[
            jax.ShapeDtypeStruct((d, parts * 6 * LANES), BF16),
            jax.ShapeDtypeStruct((t, d), F32),
            jax.ShapeDtypeStruct((t, d), BF16),
            jax.ShapeDtypeStruct((parts, 3, 5, LANES, LANES), F32),
            jax.ShapeDtypeStruct((parts, 24, t), F32),
        ],
        scratch_shapes=[
            pltpu.VMEM((d, t), BF16), pltpu.VMEM((d, t), BF16),
            pltpu.VMEM((t, d), BF16), pltpu.VMEM((d, t), BF16),
            pltpu.VMEM((t, d), F32), pltpu.VMEM((t, d), F32),
        ],
        compiler_params=params(),
        name="attend_backward",
    )(x, xo, back, wa, line, qaug, kaug, own, oth, ctx, lse)


def pack_attn(attn, out_t):
    cut = [[part[:, i * HDIM : (i + 1) * HDIM] for i in range(3)] for part in (attn[0], attn[1], attn[2], out_t)]
    q, k, v, o = cut
    return jnp.concatenate([q[0], q[1], k[0], k[1], v[0], v[1], o[0], o[1], q[2], v[2], k[2], o[2]], axis=1)


def unpack_attn(block):
    c = [block[:, i * HDIM : (i + 1) * HDIM] for i in range(12)]
    attn = jnp.stack(
        [
            jnp.concatenate([c[0], c[1], c[8]], axis=1),
            jnp.concatenate([c[2], c[3], c[10]], axis=1),
            jnp.concatenate([c[4], c[5], c[9]], axis=1),
        ]
    )
    return attn, jnp.concatenate([c[6], c[7], c[11]], axis=1)


def body(
    hidden_in, out_grad, attn_weight, out_weight, inner_weight, outer_weight, rel_bias, gains, lengths, table,
    attn_first, attn_second, out_first, out_second, inner_first, inner_second, outer_first, outer_second,
    rel_first, rel_second, gain_first, gain_second, *, parts,
):
    tokens = hidden_in.shape[0]
    nq = tokens // LANES
    heads = rel_bias.shape[1]
    per_seq = SEQLEN // tokens
    mp_index = lax.axis_index("mp")
    half = mp_index % per_seq
    length = lengths[mp_index // per_seq]

    shard = [
        pack_attn(attn_weight.astype(BF16), out_weight.astype(BF16).T),
        inner_weight.astype(BF16),
        outer_weight.astype(BF16).T,
    ]
    gathered = [lax.all_gather(lax.all_gather(s, "dp", axis=0, tiled=True), "mp", axis=1, tiled=True) for s in shard]
    wa, wi, wo = gathered

    x1 = rms_scaled(hidden_in, gains[0]).astype(BF16)
    swap = [(p, p ^ 1) for p in range(parts)]
    x1o = lax.ppermute(x1, "mp", swap)

    u = jnp.arange(4 * LANES)
    offset = jnp.where(u < 2 * LANES, -u, 4 * LANES - u)
    buckets = jnp.arange(rel_bias.shape[0], dtype=jnp.int32)
    line_hot = (jnp.take(table, offset + SEQLEN - 1)[:, None] == buckets[None, :]).astype(F32)
    line = jnp.dot(line_hot, rel_bias, precision=lax.Precision.HIGHEST).T.reshape(parts, heads // parts, 4 * LANES)
    first_flag = (half == 0).astype(F32)
    flags = jnp.stack([jnp.full((4 * LANES,), first_flag), jnp.full((4 * LANES,), 1.0 - first_flag)])
    line_in = jnp.concatenate(
        [line, jnp.broadcast_to(flags[None], (parts, 2, 4 * LANES)), jnp.zeros((parts, 3, 4 * LANES), F32)], axis=1
    )
    far_before, far_after = line[:, :, LANES], line[:, :, 3 * LANES]
    jb, ib = jnp.arange(nq)[None, :], jnp.arange(nq)[:, None]
    own_before, own_after = (jb < ib - 1).astype(F32), (jb > ib + 1).astype(F32)
    oth_before = jnp.full((nq, nq), 1.0 - first_flag)
    w_before = jnp.concatenate([own_before, oth_before], axis=1)
    w_after = jnp.concatenate([own_after, 1.0 - oth_before], axis=1)
    far = far_before[:, :, None, None] * w_before + far_after[:, :, None, None] * w_after
    far_hi = far.astype(BF16).astype(F32)
    far_lo = far - far_hi
    one = jnp.ones((parts, heads // parts, nq, 1), F32)
    blank = jnp.zeros((parts, heads // parts, nq, HDIM), F32)
    q64 = jnp.concatenate(
        [blank[..., :3], one, blank[..., :4], far_hi, far_lo, blank[..., : HDIM - 8 - 4 * nq]], axis=-1
    )
    qaug = jnp.concatenate([q64, q64], axis=-1).reshape(parts, 3 * nq, LANES)
    qaug = jnp.pad(qaug, ((0, 0), (0, 16 - 3 * nq), (0, 0))).astype(BF16)
    row = jnp.arange(2 * tokens)
    position = jnp.where(row < tokens, half * tokens + row, (1 - half) * tokens + row - tokens)
    masked = jnp.where(position < length, 0.0, NEG)
    col = jnp.arange(LANES) % HDIM
    block_of = row // LANES
    hot = ((col >= 8) & (col < 8 + 4 * nq))[None, :] & ((col[None, :] - 8) % (2 * nq) == block_of[:, None])
    kaug = jnp.where((col == 3)[None, :], masked[:, None], hot.astype(F32)).astype(BF16)

    own, oth, ctx, lse, middle = run_forward(x1, x1o, wa, line_in, qaug, kaug, hidden_in, parts)
    block_out, middle_back, gain_two, gi, go = run_feed(middle, out_grad, gains, wi, wo)
    ga, one_own, one_oth, near, sums = run_backward(
        x1, x1o, middle_back, wa, line_in, qaug, kaug, own, oth, ctx, lse, parts
    )
    one_back = one_own + lax.ppermute(one_oth, "mp", swap).astype(F32)
    input_grad, gain_one = rms_back(hidden_in, gains[0:1], one_back)
    input_grad = input_grad + middle_back

    nh = heads // parts
    near = near.reshape(heads, 5, LANES, LANES)
    first_w = first_flag
    blocks = jnp.stack(
        [near[:, 0] + near[:, 4] * (1.0 - first_w), near[:, 1], near[:, 2] + near[:, 3] * first_w], axis=1
    )
    r = jnp.arange(LANES)
    diff = r[None, :, None] - r[None, None, :] + (jnp.arange(3) - 1)[:, None, None] * LANES
    near_bucket = jnp.take(table, diff + SEQLEN - 1).reshape(1, -1)
    near_hot = (near_bucket == buckets[:, None]).astype(F32)
    near_grad = lax.dot_general(
        near_hot, blocks.reshape(heads, -1), (((1,), (1,)), ((), ())), precision=lax.Precision.HIGHEST
    )
    block_sums = jnp.sum(sums.reshape(heads, 2 * nq, nq, LANES), axis=-1)
    far_w = jnp.transpose(jnp.stack([w_before, w_after]), (0, 2, 1))
    corner = jnp.stack([jnp.sum(near[:, 4], (1, 2)) * (1.0 - first_w), jnp.sum(near[:, 3], (1, 2)) * first_w])
    far_grad = jnp.einsum("hji,sji->sh", block_sums, far_w, precision=lax.Precision.HIGHEST) - corner
    far_hot = (jnp.stack([table[0], table[2 * SEQLEN - 2]])[None, :] == buckets[:, None]).astype(F32)
    rel_part = near_grad + jnp.dot(far_hot, far_grad, precision=lax.Precision.HIGHEST)

    owned = [
        lax.psum_scatter(
            lax.psum_scatter(g, "mp", scatter_dimension=1, tiled=True), "dp", scatter_dimension=0, tiled=True
        ).astype(F32)
        for g in (ga, gi, go)
    ]
    g_attn, g_out_t = unpack_attn(owned[0])
    grads = (g_attn, g_out_t.T, owned[1], owned[2].T)
    square_part = sum(jnp.sum(g * g) for g in owned)
    gain_grad, rel_grad, square_total = lax.psum(
        (jnp.concatenate([gain_one, gain_two[:1]], axis=0), rel_part, square_part), ("dp", "mp")
    )
    grad_norm = jnp.sqrt(square_total + jnp.sum(gain_grad * gain_grad) + jnp.sum(rel_grad * rel_grad))
    factor = jnp.minimum(1.0, CLIP / (grad_norm + 1e-06))
    attn_new = adam_step(attn_weight, grads[0], attn_first, attn_second, factor, RATE_MATRIX)
    out_new = adam_step(out_weight, grads[1], out_first, out_second, factor, RATE_OUT)
    inner_new = adam_step(inner_weight, grads[2], inner_first, inner_second, factor, RATE_MATRIX)
    outer_new = adam_step(outer_weight, grads[3], outer_first, outer_second, factor, RATE_MATRIX)
    rel_new = adam_step(rel_bias, rel_grad, rel_first, rel_second, factor, RATE_SMALL)
    gain_new = adam_step(gains, gain_grad, gain_first, gain_second, factor, RATE_SMALL)
    return (block_out, input_grad, grad_norm, *attn_new, *out_new, *inner_new, *outer_new, *rel_new, *gain_new)


def solution(mesh):
    rows = P(("dp", "mp"), None)
    attn, up, down = P(None, "dp", "mp"), P("dp", "mp"), P("mp", "dp")
    in_specs = (
        rows, rows, attn, down, up, down, P(), P(), P("dp"), P(),
        attn, attn, down, down, up, up, down, down, P(), P(), P(), P(),
    )
    out_specs = (rows, rows, P()) + (attn,) * 3 + (down,) * 3 + (up,) * 3 + (down,) * 3 + (P(),) * 6
    return jax.shard_map(
        functools.partial(body, parts=mesh.shape["mp"]),
        mesh=mesh, in_specs=in_specs, out_specs=out_specs, check_vma=False,
    )
```

time: 1530 us -> 926 us (0.61); the launches traced: 1510 us -> 925 us
  local copies, waits for them, and re-layouts: 609 us -> 286 us
  matrix products: 139 us -> 6.13 us
  waiting for transfers between devices: 555 us -> 463 us
  Pallas kernels: 0 us -> 80.8 us
  other arithmetic: 90.3 us -> 26.2 us
  loops' own time: 27.7 us -> 0 us
  blocking collectives: 63.1 us -> 39.6 us
    gather x0 -> x2, local copies, waits for them, and re-layouts: none -> 274 us  [the longest x1 271 us: body(): near_bucket = jnp.take(table, diff + SEQLEN - 1).reshape(1, -1)]
    rev x6 -> x0, local copies, waits for them, and re-layouts: 223 us -> none  [the longest x4 126 us: diag_sums(): flipped = jnp.pad(matrix[:, ::-1, :], ((0, 0), (0, 0), (0, block)))]
    reduce_scatter x4 -> x6, waiting for transfers between devices: 300 us -> 133 us  [the longest x3 82.2 us: body(): lax.psum_scatter(g, 'mp', scatter_dimension=1, tiled=True)]
    while x60 -> x0, local copies, waits for them, and re-layouts: 148 us -> none
    all_gather x6, waiting for transfers between devices: 145 us -> 284 us  [the longest x3 206 us: body(): lax.all_gather(lax.all_gather(s, 'dp', axis=0, tiled=True), 'mp', axis=1,...]
    dot_general x42 -> x4, matrix products: 139 us -> 6.13 us  [the longest x1 5.47 us: body(): lax.dot_general(near_hot, blocks.reshape(heads, -1), (((1,), (1,)), ((),...]
    psum x1 -> x0, waiting for transfers between devices: 111 us -> none  [body(): lax.psum((partials[0], partials[1], partials[2], partials[3]), 'dp')]
    reshape x9 -> x1, local copies, waits for them, and re-layouts: 94.6 us -> 0.01 us  [body(): jnp.dot(line_hot, rel_bias, precision=lax.Precision.HIGHEST)]
  transfers between devices with their start and end apart: 11 -> 14, of which waited for: 8 -> 11; matrix products, arithmetic and copies ran while one was open for 18% -> 33% of each run, Pallas kernels for 0% -> 2%
where the time goes in v1:
time: 926 us; the launch traced here: 925 us
  waiting for transfers between devices  463 us (50%)
  local copies, waits for them, and re-layouts  286 us (31%)
  Pallas kernels  80.8 us (9%)
  blocking collectives  39.6 us (4%)
  other arithmetic  26.2 us (3%)
  between operations  20 us (2%)
    gather x1, local copies, waits for them, and re-layouts, body(): near_bucket = jnp.take(table, diff + SEQLEN - 1).reshape(1, -1)  271 us
    all_gather x3, waiting for transfers between devices, body(): lax.all_gather(lax.all_gather(s, 'dp', axis=0, tiled=True), 'mp', axis=1,...  206 us
    reduce_scatter x3, waiting for transfers between devices, body(): lax.psum_scatter(g, 'mp', scatter_dimension=1, tiled=True)  82.2 us
    all_gather x3, waiting for transfers between devices, body(): lax.all_gather(s, 'dp', axis=0, tiled=True)  78.5 us
    reduce_scatter x3, waiting for transfers between devices, body(): lax.psum_scatter(lax.psum_scatter(g, 'mp', scatter_dimension=1, tiled=Tru...  51.1 us
    psum x1, blocking collectives, body(): lax.psum((jnp.concatenate([gain_one, gain_two[:1]], axis=0), rel_part, sq...  39.6 us
    ppermute x1, waiting for transfers between devices, body(): x1o = lax.ppermute(x1, 'mp', swap)  38.9 us
    pallas_call x1, Pallas kernels, run_backward(): pl.pallas_call(backward_kernel, grid=(parts,), in_specs=[whole((t, d)), w...  36.3 us
  transfers between devices with their start and end apart: 14, of which 11 were waited for; matrix products, arithmetic and copies ran while one was open for 33% of the time, Pallas kernels for 2%

profile of v1, /device:TPU:0, one launch (start us, length us, event | category | flops | bytes accessed | tf_op | source)
XLA Modules:
  0.0 925.5 jit_solution(1455767434968190757)
XLA Ops:
  7.3 1.0 convert_element_type.63
  8.4 1.0 copy.59
  9.4 0.8 concatenate.39
  10.3 0.7 convert_element_type.72
  11.0 0.7 convert_bitcast_fusion
  11.8 25.5 %all-gather.7.cloned.1.call-done = bf16[768,768]{1,0:T(8,128)(2,1)} async-done(((bf16[96,768]{1,0:T(8,128)(2,1)}), bf16[768,768]{1,0:T(8,128)(2,1)}) %all-gather.7.cloned.1.call-update) | async-done | bytes 1179664 | tf_op jit(solution)/shard_map/all_gather | solution.py:487
  37.4 26.5 %all-gather.11.cloned.1.call-done = bf16[768,768]{1,0:T(8,128)(2,1)} async-done(((bf16[96,768]{1,0:T(8,128)(2,1)}), bf16[768,768]{1,0:T(8,128)(2,1)}) %all-gather.11.cloned.1.call-update) | async-done | bytes 1179664 | tf_op jit(solution)/shard_map/all_gather | solution.py:487
  63.9 26.5 %all-gather.15.cloned.1.call-done = bf16[768,768]{1,0:T(8,128)(2,1)} async-done(((bf16[96,768]{1,0:T(8,128)(2,1)}), bf16[768,768]{1,0:T(8,128)(2,1)}) %all-gather.15.cloned.1.call-update) | async-done | bytes 1179664 | tf_op jit(solution)/shard_map/all_gather | solution.py:487
  90.5 0.2 multiply_reduce_fusion.2
  90.7 0.2 multiply_convert_fusion.x_ref
  91.0 1.6 collective-permute-start
  92.7 3.1 gather_fusion
  95.9 0.3 convolution_bitcast_fusion
  96.8 0.1 concatenate.43
  97.0 0.6 pad.8.qaug_ref
  97.6 0.6 dynamic_slice.3
  98.3 0.7 fusion.27
  99.0 0.7 maximum_maximum_fusion.line_ref
  99.7 1.0 select_convert_fusion.kaug_ref
  100.8 38.9 %collective-permute-done.xo_ref = bf16[512,768]{1,0:T(8,128)(2,1)S(1)} collective-permute-done((bf16[512,768]{1,0:T(8,128)(2,1)S(1)}, bf16[512,768]{1,0:T(8,128)(2,1)S(1)}, u32[]{:S(2)}, u32[]{:S(2)}) %collective-permute-start) | collective-permute-done | bytes 786464 | tf_op jit(solution)/shard_map/ppermute | solution.py:492
  139.7 47.2 %all-gather.9.cloned.1.call-done.w_ref = bf16[768,3072]{1,0:T(8,128)(2,1)} async-done(((bf16[768,768]{1,0:T(8,128)(2,1)}), bf16[768,3072]{1,0:T(8,128)(2,1)}) %all-gather.9.cloned.1.call-update) | async-done | bytes 4718608 | tf_op jit(solution)/shard_map/all_gather | solution.py:487
  186.9 21.5 %attend_forward.1 = (bf16[4,512,640]{2,1,0:T(8,128)(2,1)}, bf16[4,512,512]{2,1,0:T(8,128)(2,1)}, bf16[4,512,256]{2,1,0:T(8,128)(2,1)}, f32[4,8,512]{2,1,0:T(8,128)}, f32[512,768]{1,0:T(8,128)}) custom-call(bf16[512,768]{1,0:T(8,128)(2,1)} %copy-done.3, bf16[512,768]{1,0:T(8,128)(2,1)} %copy-done.5, bf16[768,3072]{1,0:T(8,128)(2,1)} %all-gather.9.cloned.1.call-done.w_ref, ...), custom_call_target="tpu_custom_call" | custom-call | tf_op jit(solution)/shard_map/attend_forward/pallas_call | solution.py:344
  208.5 69.3 %all-gather.13.cloned.1.call-done.wi_ref = bf16[768,3072]{1,0:T(8,128)(2,1)} async-done(((bf16[768,768]{1,0:T(8,128)(2,1)}), bf16[768,3072]{1,0:T(8,128)(2,1)}) %all-gather.13.cloned.1.call-update) | async-done | bytes 4718608 | tf_op jit(solution)/shard_map/all_gather | solution.py:487
  277.8 89.3 %all-gather.17.cloned.1.call-done.wo_ref = bf16[768,3072]{1,0:T(8,128)(2,1)} async-done(((bf16[768,768]{1,0:T(8,128)(2,1)}), bf16[768,3072]{1,0:T(8,128)(2,1)}) %all-gather.17.cloned.1.call-update) | async-done | bytes 4718608 | tf_op jit(solution)/shard_map/all_gather | solution.py:487
  367.1 22.9 %feed_both.1 = (f32[512,768]{1,0:T(8,128)}, f32[512,768]{1,0:T(8,128)}, f32[8,768]{1,0:T(8,128)}, bf16[768,3072]{1,0:T(8,128)(2,1)}, bf16[768,3072]{1,0:T(8,128)(2,1)}) custom-call(f32[512,768]{1,0:T(8,128)} %get-tuple-element.36.middle_ref, f32[512,768]{1,0:T(8,128)} %grad_ref.1, f32[2,768]{1,0:T(2,128)} %gain_ref.1, ...), custom_call_target="tpu_custom_call" | custom-call | tf_op jit(solution)/shard_map/feed_both/pallas_call | solution.py:382
  390.0 36.3 %attend_backward.1 = (bf16[768,3072]{1,0:T(8,128)(2,1)}, f32[512,768]{1,0:T(8,128)}, bf16[512,768]{1,0:T(8,128)(2,1)}, f32[4,3,5,128,128]{4,3,2,1,0:T(8,128)}, f32[4,24,512]{2,1,0:T(8,128)}) custom-call(bf16[512,768]{1,0:T(8,128)(2,1)} %copy-done.3, bf16[512,768]{1,0:T(8,128)(2,1)} %copy-done.5, f32[512,768]{1,0:T(8,128)} %get-tuple-element.38.back_ref, ...), custom_call_target="tpu_custom_call" | custom-call | tf_op jit(solution)/shard_map/attend_backward/pallas_call | solution.py:414
  426.4 0.7 reduce-scatter.11.cloned.1.call-update
  427.2 0.7 reduce-scatter.15.cloned.1.call-update
  428.0 82.2 %reduce-scatter.7.cloned.1.call-done = bf16[768,768]{1,0:T(8,128)(2,1)} async-done(((bf16[768,3072]{1,0:T(8,128)(2,1)}), bf16[768,768]{1,0:T(8,128)(2,1)}) %reduce-scatter.7.cloned.1.call-update) | async-done | bytes 1179664 | tf_op jit(solution)/shard_map/reduce_scatter | solution.py:559
  510.3 270.5 %gather_fusion.1 = s32[49152]{0:T(1024)S(1)} fusion(s32[2047]{0:T(1024)S(1)} %copy-done, s32[49152]{0:T(1024)S(1)} %broadcast_clamp_fusion), kind=kCustom, calls=%fused_computation.1 | custom fusion | bytes 589824 | tf_op jit(solution)/shard_map/jit(_take)/gather | solution.py:545
  781.0 0.7 copy.64
  781.7 0.6 fusion.46
  782.3 1.4 pad_add_fusion
  783.8 0.3 reduce-scatter.17.cloned.1.call-start
  784.1 1.5 collective-permute-start.1
  785.7 2.4 slice_add_fusion.1
  788.1 0.2 pad_maximum_fusion
  788.3 0.3 pad.37
  788.6 3.5 copy.70
  792.0 0.1 reduce_sum.110
  792.2 0.7 slice.135
  792.9 0.1 fusion.3
  793.1 0.2 fusion.19
  793.3 5.5 fusion.2
  798.7 5.1 collective-permute-done.1
  803.9 1.7 multiply_reduce_fusion
  805.6 1.6 multiply_reduce_fusion.3
  807.2 14.0 %reduce-scatter.13.cloned.1.call-done = bf16[96,768]{1,0:T(8,128)(2,1)} async-done(((bf16[768,768]{1,0:T(8,128)(2,1)}), bf16[96,768]{1,0:T(8,128)(2,1)}) %reduce-scatter.13.cloned.1.call-update) | async-done | bytes 147472 | tf_op jit(solution)/shard_map/reduce_scatter | solution.py:558
  821.3 1.6 fusion.6
  824.2 37.0 %reduce-scatter.17.cloned.1.call-done = bf16[96,768]{1,0:T(8,128)(2,1)} async-done(((bf16[768,768]{1,0:T(8,128)(2,1)}), bf16[96,768]{1,0:T(8,128)(2,1)}) %reduce-scatter.17.cloned.1.call-update) | async-done | bytes 147472 | tf_op jit(solution)/shard_map/reduce_scatter | solution.py:558
  861.2 1.6 fusion.7
  863.4 3.2 multiply_add_fusion
  866.7 39.6 %all-reduce.4 = (f32[]{:T(128)}, f32[2,768]{1,0:T(2,128)S(1)}, f32[32,12]{0,1:T(8,128)S(1)}) all-reduce(f32[]{:T(128)S(6)} %add.413, f32[2,768]{1,0:T(2,128)S(1)} %pad_maximum_fusion.1, f32[32,12]{0,1:T(8,128)S(1)} %fusion.2), channel_id=1, replica_groups=mesh['dp'=8,'mp'=4] {'dp','mp'}, use_global_device_ids=true, to_apply=%region_11.12 | all-reduce | flops 1921 | bytes 15368 | tf_op jit(solution)/shard_map/psum | solution.py:566
  906.3 0.6 multiply_reduce_fusion.5
  906.9 0.6 multiply_reduce_fusion.4
  909.7 1.0 multiply_subtract_fusion.3
  910.7 0.7 copy.67
  911.4 0.7 copy.68
  912.2 0.7 copy.69
  912.9 0.6 add_subtract_fusion.1
  913.6 0.6 add_subtract_fusion
  914.3 1.1 multiply_subtract_fusion.2
  915.4 1.1 multiply_subtract_fusion
  916.5 1.1 multiply_subtract_fusion.1
  (147 shorter events, 2.4 us)
Async XLA Ops:
  7.2 3.1 copy-start.10
  7.2 3.8 copy-start.8
  7.2 30.1 %all-gather.7.cloned.1.call-start = ((), (), s32[]{:S(2)}) async-start(), calls=%async_computation.6 | async-start | bytes 1327104 | tf_op jit(solution)/shard_map/all_gather | solution.py:487
  10.2 53.6 %all-gather.11.cloned.1.call-start = ((), (), s32[]{:S(2)}) async-start(), calls=%async_computation.8 | async-start | bytes 1327104 | tf_op jit(solution)/shard_map/all_gather | solution.py:487
  11.0 79.4 %all-gather.15.cloned.1.call-start = ((), (), s32[]{:S(2)}) async-start(), calls=%async_computation.10 | async-start | bytes 1327104 | tf_op jit(solution)/shard_map/all_gather | solution.py:487
  11.7 175.2 %all-gather.9.cloned.1.call-start = ((), (), s32[]{:S(2)}) async-start(), calls=%async_computation.7 | async-start | bytes 5898240 | tf_op jit(solution)/shard_map/all_gather | solution.py:487
  37.3 53.2 %copy-start.23 = (f32[2,768]{1,0:T(2,128)S(1)}, f32[2,768]{1,0:T(2,128)}, u32[]{:S(2)}) copy-start(f32[2,768]{1,0:T(2,128)} %gain_ref.1) | copy-start | bytes 18436
  37.3 53.2 %copy-start.1 = (f32[512,768]{1,0:T(8,128)S(1)}, f32[512,768]{1,0:T(8,128)}, u32[]{:S(2)}) copy-start(f32[512,768]{1,0:T(8,128)} %hidden_ref.1) | copy-start | bytes 4718596
  37.3 240.5 %all-gather.13.cloned.1.call-start = ((), (), s32[]{:S(2)}) async-start(), calls=%async_computation.9 | async-start | bytes 5898240 | tf_op jit(solution)/shard_map/all_gather | solution.py:487
  63.9 303.2 %all-gather.17.cloned.1.call-start = ((), (), s32[]{:S(2)}) async-start(), calls=%async_computation.11 | async-start | bytes 5898240 | tf_op jit(solution)/shard_map/all_gather | solution.py:487
  90.4 419.8 %reduce-scatter.7.cloned.1.call-start = ((), (), s32[]{:S(2)}) async-start(), calls=%async_computation.12 | async-start | bytes 5898240 | tf_op jit(solution)/shard_map/reduce_scatter | solution.py:559
  90.7 2.0 copy-start
  90.9 9.8 %copy-start.3 = (bf16[512,768]{1,0:T(8,128)(2,1)}, bf16[512,768]{1,0:T(8,128)(2,1)S(1)}, u32[]{:S(2)}) copy-start(bf16[512,768]{1,0:T(8,128)(2,1)S(1)} %multiply_convert_fusion.x_ref) | copy-start | bytes 2359300
  90.9 5.0 copy-start.25
  90.9 6.6 copy-start.31
  91.0 48.7 %collective-permute-start = (bf16[512,768]{1,0:T(8,128)(2,1)S(1)}, bf16[512,768]{1,0:T(8,128)(2,1)S(1)}, u32[]{:S(2)}, u32[]{:S(2)}) collective-permute-start(bf16[512,768]{1,0:T(8,128)(2,1)S(1)} %multiply_convert_fusion.x_ref), channel_id=1, source_target_pairs={{0,1},{1,0},{2,3},{3,2},{4,5},{5,4},{6,7},{7,6},{8,9},{9,8},{10,11... | collective-permute-start | bytes 2359304 | tf_op jit(solution)/shard_map/ppermute | solution.py:492
  139.7 47.2 %copy-start.5 = (bf16[512,768]{1,0:T(8,128)(2,1)}, bf16[512,768]{1,0:T(8,128)(2,1)S(1)}, u32[]{:S(2)}) copy-start(bf16[512,768]{1,0:T(8,128)(2,1)S(1)} %collective-permute-done.xo_ref) | copy-start | bytes 2359300
  426.4 357.4 %reduce-scatter.11.cloned.1.call-start = ((), (), s32[]{:S(2)}) async-start(), calls=%async_computation.14 | async-start | bytes 5898240 | tf_op jit(solution)/shard_map/reduce_scatter | solution.py:559
  427.1 361.0 %reduce-scatter.15.cloned.1.call-start = ((), (), s32[]{:S(2)}) async-start(), calls=%async_computation.16 | async-start | bytes 5898240 | tf_op jit(solution)/shard_map/reduce_scatter | solution.py:559
  427.8 377.8 %reduce-scatter.9.cloned.1.call-start = ((), (), s32[]{:S(2)}) async-start(), calls=%async_computation.13 | async-start | bytes 1327104 | tf_op jit(solution)/shard_map/reduce_scatter | solution.py:558
  510.2 311.1 %reduce-scatter.13.cloned.1.call-start = ((), (), s32[]{:S(2)}) async-start(), calls=%async_computation.15 | async-start | bytes 1327104 | tf_op jit(solution)/shard_map/reduce_scatter | solution.py:558
  510.3 270.6 %copy-start.21 = (f32[192,96]{1,0:T(8,128)S(1)}, f32[192,96]{1,0:T(8,128)}, u32[]{:S(2)}) copy-start(f32[192,96]{1,0:T(8,128)} %param.34) | copy-start | bytes 221188
  510.3 270.7 %copy-start.22 = (f32[192,96]{1,0:T(8,128)S(1)}, f32[192,96]{1,0:T(8,128)}, u32[]{:S(2)}) copy-start(f32[192,96]{1,0:T(8,128)} %param.35) | copy-start | bytes 221188
  783.8 77.4 %reduce-scatter.17.cloned.1.call-start = ((), (), s32[]{:S(2)}) async-start(), calls=%async_computation.17 | async-start | bytes 1327104 | tf_op jit(solution)/shard_map/reduce_scatter | solution.py:558
  784.1 19.7 %collective-permute-start.1 = (bf16[512,768]{1,0:T(8,128)(2,1)}, bf16[512,768]{1,0:T(8,128)(2,1)}, u32[]{:S(2)}, u32[]{:S(2)}) collective-permute-start(bf16[512,768]{1,0:T(8,128)(2,1)} %get-tuple-element.44), channel_id=1, source_target_pairs={{0,1},{1,0},{2,3},{3,2},{4,5},{5,4},{6,7},{7,6},{8,9},{9,8},{10,11... | collective-permute-start | bytes 2359304 | tf_op jit(solution)/shard_map/ppermute | solution.py:533
  788.6 3.5 copy-start.20
  793.3 10.6 %copy-start.2 = (f32[512,768]{1,0:T(8,128)S(1)}, f32[512,768]{1,0:T(8,128)}, u32[]{:S(2)}) copy-start(f32[512,768]{1,0:T(8,128)} %hidden_ref.1) | copy-start | bytes 4718596
  793.3 10.6 %copy-start.4 = (f32[512,768]{1,0:T(8,128)S(1)}, f32[512,768]{1,0:T(8,128)}, u32[]{:S(2)}) copy-start(f32[512,768]{1,0:T(8,128)} %get-tuple-element.43) | copy-start | bytes 4718596
  863.4 46.1 %copy-start.6 = (bf16[96,768]{1,0:T(8,128)(2,1)S(1)}, bf16[96,768]{1,0:T(8,128)(2,1)}, u32[]{:S(2)}) copy-start(bf16[96,768]{1,0:T(8,128)(2,1)} %reduce-scatter.9.cloned.1.call-done) | copy-start | bytes 442372
  866.7 46.3 %copy-start.24 = (f32[2,768]{1,0:T(2,128)S(1)}, f32[2,768]{1,0:T(2,128)}, u32[]{:S(2)}) copy-start(f32[2,768]{1,0:T(2,128)} %gain_ref.1) | copy-start | bytes 18436
  866.7 46.3 %copy-start.29 = (f32[2,768]{1,0:T(2,128)S(1)}, f32[2,768]{1,0:T(2,128)}, u32[]{:S(2)}) copy-start(f32[2,768]{1,0:T(2,128)} %param.42) | copy-start | bytes 18436
  866.7 46.3 %copy-start.30 = (f32[2,768]{1,0:T(2,128)S(1)}, f32[2,768]{1,0:T(2,128)}, u32[]{:S(2)}) copy-start(f32[2,768]{1,0:T(2,128)} %param.43) | copy-start | bytes 18436
  866.7 46.9 %copy-start.26 = (f32[32,12]{0,1:T(8,128)S(1)}, f32[32,12]{0,1:T(8,128)}, u32[]{:S(2)}) copy-start(f32[32,12]{0,1:T(8,128)} %param.28) | copy-start | bytes 4612
  866.7 46.9 %copy-start.27 = (f32[32,12]{0,1:T(8,128)S(1)}, f32[32,12]{0,1:T(8,128)}, u32[]{:S(2)}) copy-start(f32[32,12]{0,1:T(8,128)} %param.40) | copy-start | bytes 4612
  866.7 46.9 %copy-start.28 = (f32[32,12]{0,1:T(8,128)S(1)}, f32[32,12]{0,1:T(8,128)}, u32[]{:S(2)}) copy-start(f32[32,12]{0,1:T(8,128)} %param.41) | copy-start | bytes 4612
  866.7 47.5 %copy-start.7 = (f32[3,96,192]{2,1,0:T(8,128)S(1)}, f32[3,96,192]{2,1,0:T(8,128)}, u32[]{:S(2)}) copy-start(f32[3,96,192]{2,1,0:T(8,128)} %param.24) | copy-start | bytes 663556
  866.7 47.5 %copy-start.14 = (f32[3,96,192]{2,1,0:T(8,128)S(1)}, f32[3,96,192]{2,1,0:T(8,128)}, u32[]{:S(2)}) copy-start(f32[3,96,192]{2,1,0:T(8,128)} %param.32) | copy-start | bytes 663556
  866.7 47.5 %copy-start.15 = (f32[3,96,192]{2,1,0:T(8,128)S(1)}, f32[3,96,192]{2,1,0:T(8,128)}, u32[]{:S(2)}) copy-start(f32[3,96,192]{2,1,0:T(8,128)} %param.33) | copy-start | bytes 663556
  911.4 3.9 copy-start.9
  911.4 3.9 copy-start.13
  911.4 3.9 copy-start.16
  911.4 4.0 copy-start.17
  914.3 2.2 copy-start.11
  914.3 2.2 copy-start.12
  914.3 2.2 copy-start.18
  914.3 2.2 copy-start.19
Sparse Core Ops, SparseCore 0:
  10.5 26.7 all-gather.6
  39.8 24.0 all-gather.10
  66.3 24.0 all-gather.14
  91.8 95.0 all-gather.8
  188.4 89.4 all-gather.12
  279.2 87.8 all-gather.16
  426.5 83.6 reduce-scatter.6
  512.5 85.7 reduce-scatter.10
  600.6 85.7 reduce-scatter.14
  689.5 37.2 reduce-scatter.8
  783.9 37.2 reduce-scatter.12
  824.4 36.7 reduce-scatter.16

commit v2 on v1

--- a/solution.py
+++ b/solution.py
@@ -24,6 +24,7 @@
 BF16 = jnp.bfloat16
 LANES = 128
 NEG = -1e30
+MESH = pl.DeviceIdType.MESH
 
 HEAD_AT = ((0, 0, 1, 2, 0), (0, 1, 1, 2, 1), (4, 0, 5, 4, 1))
 
@@ -105,6 +106,861 @@
     return jnp.concatenate(
         [jnp.broadcast_to(qaug[i * nq + ib : i * nq + ib + 1, :], (LANES, LANES)) for ib in range(nq)], axis=0
     )
+
+
+def peer(index, stride):
+    return index + stride - 2 * stride * ((index // stride) % 2)
+
+
+class Links:
+    def __init__(self):
+        self.dp = lax.axis_index("dp")
+        self.mp = lax.axis_index("mp")
+        self.core = self.dp % 2
+        self.chip = self.dp // 2
+        self.dp_x, self.dp_y, self.dp_s = peer(self.dp, 2), peer(self.dp, 4), peer(self.dp, 1)
+        self.dp_d = peer(self.dp_x, 4)
+        self.at_x, self.at_y, self.at_s = (self.dp_x, self.mp), (self.dp_y, self.mp), (self.dp_s, self.mp)
+        z1, z2 = peer(self.mp, 1), peer(self.mp, 2)
+        self.at_z = (None, (self.dp, z1), (self.dp, z2), (self.dp, peer(z1, 2)))
+
+    def meet(self):
+        barrier = pltpu.get_barrier_semaphore()
+        others = (self.at_x, self.at_y, self.at_s) + self.at_z[1:]
+        for other in others:
+            pl.semaphore_signal(barrier, inc=1, device_id=other, device_id_type=MESH)
+        pl.semaphore_wait(barrier, len(others))
+
+
+def remote(src, dst, send, recv, to):
+    return pltpu.make_async_remote_copy(
+        src_ref=src, dst_ref=dst, send_sem=send, recv_sem=recv, device_id=to, device_id_type=MESH
+    )
+
+
+class Gather:
+    def __init__(self, links, w, send, recv, zsend, zrecv):
+        self.k, self.w, self.send, self.recv, self.zsend, self.zrecv = links, w, send, recv, zsend, zrecv
+        self.rows = w.shape[2] // 8
+
+    def block(self, unit, dp, lo=0, n=None):
+        group, s = unit
+        n = self.rows if n is None else n
+        return self.w.at[group, s, pl.ds(pl.multiple_of(dp * self.rows + lo, 16), n), :]
+
+    def copy(self, unit, kind, ref, to):
+        at = unit[0] * 4 + unit[1]
+        return remote(ref, ref, self.send.at[at, kind], self.recv.at[at, kind], to)
+
+    def outgoing(self, unit, kind):
+        k, half = self.k, self.rows // 2
+        dp, lo, n, to = (
+            (k.dp, 0, None, k.at_x),
+            (k.dp, 0, None, k.at_y),
+            (k.dp, 0, None, k.at_s),
+            (k.dp_x, 0, half, k.at_y),
+            (k.dp_x, 0, None, k.at_s),
+            (k.dp_y, half, half, k.at_x),
+            (k.dp_y, 0, None, k.at_s),
+            (k.dp_d, 0, None, k.at_s),
+        )[kind]
+        return self.copy(unit, kind, self.block(unit, dp, lo, n), to)
+
+    def arrived(self, unit, kind):
+        k, half = self.k, self.rows // 2
+        sib = k.dp_s
+        dp, lo, n = {
+            0: (k.dp_x, 0, None),
+            1: (k.dp_y, 0, None),
+            2: (sib, 0, None),
+            3: (k.dp_d, 0, half),
+            4: (peer(sib, 2), 0, None),
+            5: (k.dp_d, half, half),
+            6: (peer(sib, 4), 0, None),
+            7: (peer(peer(sib, 2), 4), 0, None),
+        }[kind]
+        self.copy(unit, kind, self.block(unit, dp, lo, n), k.at_x).wait_recv()
+
+    def z_copy(self, group, s):
+        at = group * 3 + s - 1
+        src = self.block((group, 0), self.k.dp)
+        dst = self.block((group, s), self.k.dp)
+        return remote(src, dst, self.zsend.at[at], self.zrecv.at[at], self.k.at_z[s])
+
+    def z_arrived(self, unit):
+        at = unit[0] * 3 + unit[1] - 1
+        ref = self.block(unit, self.k.dp)
+        remote(ref, ref, self.zsend.at[at], self.zrecv.at[at], self.k.at_x).wait_recv()
+
+    def run(self, ops):
+        for op in ops:
+            (self.s1, self.s2, self.s3, self.s4)[op // 16 - 1](UNITS[op % 16])
+
+    def at(self, loop, step, place):
+        for number in range(4):
+            ops = GATHER_PLAN.get((loop, number), {}).get(place)
+            if ops:
+                pl.when(step == number)(functools.partial(self.run, ops))
+
+    def s1(self, unit):
+        if unit[1] > 0:
+            self.z_arrived(unit)
+        for kind in (0, 1, 2):
+            self.outgoing(unit, kind).start()
+
+    def s2(self, unit):
+        self.arrived(unit, 0)
+        for kind in (3, 4):
+            self.outgoing(unit, kind).start()
+        self.arrived(unit, 1)
+        for kind in (5, 6):
+            self.outgoing(unit, kind).start()
+
+    def s3(self, unit):
+        self.arrived(unit, 3)
+        self.arrived(unit, 5)
+        self.outgoing(unit, 7).start()
+
+    def s4(self, unit):
+        for kind in (2, 4, 6, 7):
+            self.arrived(unit, kind)
+
+    def finish(self):
+        def each(at, carry):
+            for kind in range(8):
+                self.outgoing((at // 4, at % 4), kind).wait_send()
+            return carry
+
+        lax.fori_loop(0, 12, each, 0)
+        for group in range(3):
+            for s in (1, 2, 3):
+                self.z_copy(group, s).wait_send()
+
+
+UNITS = ((0, 0), (0, 1), (0, 2), (1, 0), (2, 0), (0, 3), (1, 1), (2, 1), (1, 2), (2, 2), (1, 3), (2, 3))
+GATHER_AHEAD = (0x10, 0x11, 0x20, 0x12, 0x30, 0x21, 0x13, 0x40, 0x31, 0x22, 0x14, 0x41, 0x32)
+GATHER_PLAN = {
+    ("attend", 0): {0: (0x23, 0x15, 0x42), 2: (0x33,)},
+    ("attend", 1): {0: (0x24, 0x16), 1: (0x43,), 2: (0x34,)},
+    ("attend", 2): {0: (0x25, 0x17), 1: (0x44,), 2: (0x35,), 3: (0x45,)},
+    ("attend", 3): {0: (0x26, 0x18), 1: (0x36,), 2: (0x27, 0x19)},
+    ("feed", 0): {0: (0x46,), 1: (0x37,), 2: (0x28, 0x1a, 0x47)},
+    ("feed", 1): {1: (0x38,), 2: (0x29, 0x1b, 0x48)},
+    ("feed", 2): {0: (0x39, 0x49), 1: (0x2a,), 2: (0x3a, 0x2b)},
+    ("feed", 3): {0: (0x4a, 0x3b, 0x4b)},
+}
+
+
+def front_kernel(
+    x_ref, shard_ref, line_ref, qaug_ref, kaug_ref, gain_ref, hidden_hbm, grad_hbm,
+    own_hbm, oth_hbm, ctx_hbm, lse_ref, wa_hbm, xo_hbm, out_ref, back_ref, gain_grad_ref, gi_hbm, go_hbm,
+    w, xo, own, oth, ctx, s_ref, e_ref, middle, grad, x2_ref, x2t_ref, ob_ref, obt_ref, acc_out, acc_two, gi, go,
+    send, recv, zsend, zrecv, xsem, lsem, osem, gsem,
+):
+    tokens = x_ref.shape[0]
+    nq = tokens // LANES
+    links = Links()
+    net = Gather(links, w, send, recv, zsend, zrecv)
+    get_hidden = pltpu.make_async_copy(hidden_hbm, middle, lsem.at[0])
+    get_grad = pltpu.make_async_copy(grad_hbm, grad, lsem.at[1])
+    get_hidden.start()
+    get_grad.start()
+    place = [pltpu.make_async_copy(shard_ref.at[g], net.block((g, 0), links.dp), lsem.at[2 + g]) for g in range(3)]
+    for copy in place:
+        copy.start()
+    links.meet()
+    for copy in place:
+        copy.wait()
+    xcopy = remote(x_ref, xo, xsem.at[0], xsem.at[1], links.at_z[1])
+    net.z_copy(0, 1).start()
+    net.z_copy(0, 2).start()
+    xcopy.start()
+    net.z_copy(0, 3).start()
+    for step in (1, 2, 3):
+        net.z_copy(1, step).start()
+        net.z_copy(2, step).start()
+    net.run(GATHER_AHEAD)
+    get_grad.wait()
+    ob = grad[...].astype(BF16)
+    ob_ref[...] = ob
+    obt_ref[...] = ob.T
+    get_hidden.wait()
+    xcopy.wait_recv()
+
+    masks = [half_rows(0), half_rows(1)]
+    count = lax.broadcasted_iota(jnp.int32, (HDIM, 2 * tokens), 0)
+    ones = (count == 0).astype(F32).astype(BF16)
+
+    def attend(s, carry):
+        x, other = x_ref[...], xo[...]
+        p_a = mm(x, w[0, s, :, : 3 * LANES]).astype(BF16)
+        p_b = mm(x, w[0, s, :, 4 * LANES :]).astype(BF16)
+        o_a = mm(other, w[0, s, :, LANES : 3 * LANES]).astype(BF16)
+        o_b = mm(other, w[0, s, :, 4 * LANES :]).astype(BF16)
+        own[s, :, : 3 * LANES] = p_a
+        own[s, :, 3 * LANES :] = p_b
+        oth[s, :, : 2 * LANES] = o_a
+        oth[s, :, 2 * LANES :] = o_b
+        cols_own = {0: p_a[:, :LANES], 1: p_a[:, LANES : 2 * LANES], 2: p_a[:, 2 * LANES :], 4: p_b[:, :LANES], 5: p_b[:, LANES:]}
+        cols_oth = {1: o_a[:, :LANES], 2: o_a[:, LANES:], 4: o_b[:, :LANES], 5: o_b[:, LANES:]}
+        both = {c: jnp.concatenate([cols_own[c], cols_oth[c]], axis=0) for c in (1, 2, 4, 5)}
+        flags = (line_ref[s, 3:4, :LANES], line_ref[s, 4:5, :LANES])
+        v_t = {2: both[2].T, 4: both[4].T}
+        pieces = []
+        stats = []
+        for i, (qc, qh, kc, vc, vh) in enumerate(HEAD_AT):
+            net.at("attend", s, i)
+            line = line_ref[s, i : i + 1, :]
+            tile = bias_tile(line)
+            qa = cols_own[qc] * masks[qh] + query_aug(qaug_ref[s], i, nq) * masks[1 - qh]
+            ka = both[kc] * masks[qh] + kaug_ref[...] * masks[1 - qh]
+            scores = mt(ka, qa)
+            peak = None
+            for jb, row in enumerate(add_bias(scores, tile, line, flags, nq)):
+                s_ref[i % 2, jb * LANES : (jb + 1) * LANES, :] = row
+                top = jnp.max(row.reshape(LANES // 8, 8, tokens), axis=0)
+                peak = top if peak is None else jnp.maximum(peak, top)
+            peak = jnp.max(peak, axis=0, keepdims=True)
+            for jb in range(2 * nq):
+                rows = slice(jb * LANES, (jb + 1) * LANES)
+                e_ref[i % 2, rows, :] = jnp.exp(s_ref[i % 2, rows, :] - peak).astype(BF16)
+            if vh == 0:
+                va = jnp.concatenate([v_t[vc][:HDIM], ones], axis=0)
+            else:
+                va = jnp.concatenate([ones, v_t[vc][HDIM:]], axis=0)
+            ot = mm(va, e_ref[i % 2])
+            at = HDIM if vh == 0 else 0
+            total = ot[at : at + 1, :]
+            stats.append(peak + jnp.log(total))
+            real = ot[:HDIM] if vh == 0 else ot[HDIM:]
+            pieces.append(real / total)
+        zero = jnp.zeros((HDIM, tokens), F32)
+        ctx_a = jnp.concatenate([pieces[0], pieces[1]], axis=0).T.astype(BF16)
+        ctx_b = jnp.concatenate([zero, pieces[2]], axis=0).T.astype(BF16)
+        ctx[s, :, :LANES] = ctx_a
+        ctx[s, :, LANES:] = ctx_b
+        lse_ref[s] = jnp.concatenate(stats + [jnp.zeros((5, tokens), F32)], axis=0)
+        middle[...] += mt(ctx_a, w[0, s, :, 3 * LANES : 4 * LANES]) + mt(ctx_b, w[0, s, :, 5 * LANES :])
+        net.at("attend", s, 3)
+        return carry
+
+    lax.fori_loop(0, 4, attend, 0)
+    saves = [
+        pltpu.make_async_copy(a, b, osem.at[n])
+        for n, (a, b) in enumerate(((own, own_hbm), (oth, oth_hbm), (ctx, ctx_hbm), (w.at[0], wa_hbm), (xo, xo_hbm)))
+    ]
+    for copy in saves:
+        copy.start()
+
+    x2 = rms_scaled(middle[...], gain_ref[1:2, :]).astype(BF16)
+    x2_ref[...] = x2
+    x2t_ref[...] = x2.T
+    acc_out[...] = jnp.zeros_like(acc_out)
+    acc_two[...] = jnp.zeros_like(acc_two)
+    def g_copies(t):
+        slot = t % 2
+        return (
+            pltpu.make_async_copy(gi.at[slot], gi_hbm.at[t], gsem.at[slot, 0]),
+            pltpu.make_async_copy(go.at[slot], go_hbm.at[t], gsem.at[slot, 1]),
+        )
+
+    def feed(t, carry):
+        slot = t % 2
+        cols = w.shape[3]
+        tile = 2 * LANES
+
+        @pl.when(t >= 2)
+        def _():
+            for copy in g_copies(t - 2):
+                copy.wait()
+
+        for n in range(cols // tile):
+            net.at("feed", t, n)
+            at = slice(n * tile, (n + 1) * tile)
+            wi = w[1, t, :, at]
+            wo = w[2, t, :, at]
+            inner = mm(x2_ref[...], wi)
+            active_back = mm(ob_ref[...], wo)
+            c = 0.7978845608028654
+            sq = inner * inner
+            th = jnp.tanh(c * (inner + 0.044715 * (sq * inner)))
+            half = 0.5 * (1.0 + th)
+            active = (inner * half).astype(BF16)
+            slope = half + (0.5 * c) * inner * (1.0 - th * th) * (1.0 + (3 * 0.044715) * sq)
+            inner_back = (slope * active_back).astype(BF16)
+            acc_out[...] += mt(active, wo)
+            acc_two[...] += mt(inner_back, wi)
+            go[slot, :, at] = mm(obt_ref[...], active).astype(BF16)
+            gi[slot, :, at] = mm(x2t_ref[...], inner_back).astype(BF16)
+        for copy in g_copies(t):
+            copy.start()
+
+        return carry
+
+    lax.fori_loop(0, 4, feed, 0)
+    out_ref[...] = middle[...] + acc_out[...]
+    result, gain_part = rms_back(middle[...], gain_ref[1:2, :], acc_two[...])
+    back_ref[...] = grad[...] + result
+    gain_grad_ref[...] = jnp.broadcast_to(gain_part, gain_grad_ref.shape)
+    for t in (2, 3):
+        for copy in g_copies(t):
+            copy.wait()
+    for copy in saves:
+        copy.wait()
+    xcopy.wait_send()
+    net.finish()
+
+
+class Scatter:
+    def __init__(self, links, sources, sums, piece, diag, side, final, result, send, recv, psem):
+        self.k, self.sources, self.sums, self.piece = links, sources, sums, piece
+        self.diag, self.side, self.final, self.result = diag, side, final, result
+        self.send, self.recv, self.psem = send, recv, psem
+        self.rows = sums.shape[2]
+        chip = links.chip
+        self.chips = (chip, peer(chip, 1), peer(chip, 2), peer(peer(chip, 1), 2))
+
+    def outgoing(self, u, kind):
+        group, s = BACK_UNITS[u]
+        k, half = self.k, self.rows // 2
+        at, at_x, at_y, at_d = self.chips
+        if kind == 0:
+            src, dst, to = self.sources[group].at[s, :, 1 - k.core], self.sums.at[u], k.at_s
+        elif kind == 1:
+            src, dst, to = self.sums.at[u, at_d, pl.ds(0, half)], self.diag.at[u, 0], k.at_x
+        elif kind == 2:
+            src, dst, to = self.sums.at[u, at_d, pl.ds(half, half)], self.diag.at[u, 1], k.at_y
+        elif kind == 3:
+            src, dst, to = self.sums.at[u, at_x], self.side.at[u, 0], k.at_x
+        elif kind == 4:
+            src, dst, to = self.sums.at[u, at_y], self.side.at[u, 1], k.at_y
+        else:
+            src, dst, to = self.sums.at[u, at], self.final.at[group, s - 1], k.at_z[s]
+        return remote(src, dst, self.send.at[u, kind], self.recv.at[u, kind], to)
+
+    def local(self, u):
+        group, s = BACK_UNITS[u]
+        return pltpu.make_async_copy(self.sources[group].at[s, :, self.k.core], self.piece.at[u % 3], self.psem.at[u % 3])
+
+    def s1(self, u):
+        self.outgoing(u, 0).start()
+        self.local(u).start()
+
+    def s2(self, u):
+        self.local(u).wait()
+        self.outgoing(u, 0).wait_recv()
+        for chip in range(4):
+            self.sums[u, chip] = (self.sums[u, chip].astype(F32) + self.piece[u % 3, chip].astype(F32)).astype(BF16)
+        self.outgoing(u, 1).start()
+        self.outgoing(u, 2).start()
+
+    def s3(self, u):
+        half = self.rows // 2
+        self.outgoing(u, 1).wait_recv()
+        self.outgoing(u, 2).wait_recv()
+        for chip, lo, n in ((self.chips[2], 0, 0), (self.chips[1], half, 1)):
+            part = self.sums[u, chip, lo : lo + half].astype(F32) + self.diag[u, n].astype(F32)
+            self.sums[u, chip, lo : lo + half] = part.astype(BF16)
+        self.outgoing(u, 3).start()
+        self.outgoing(u, 4).start()
+
+    def s4(self, u):
+        group, s = BACK_UNITS[u]
+        self.outgoing(u, 3).wait_recv()
+        self.outgoing(u, 4).wait_recv()
+        at = self.chips[0]
+        total = self.sums[u, at].astype(F32) + (self.side[u, 0].astype(F32) + self.side[u, 1].astype(F32))
+        if s == 0:
+            self.result[group] = total
+        else:
+            self.sums[u, at] = total.astype(BF16)
+            self.outgoing(u, 5).start()
+
+    def last(self, group):
+        total = self.result[group]
+        for u, (other, s) in enumerate(BACK_UNITS):
+            if other == group and s > 0:
+                self.outgoing(u, 5).wait_recv()
+        for n in range(3):
+            total = total + self.final[group, n].astype(F32)
+        self.result[group] = total
+
+    def run(self, ops):
+        for op in ops:
+            (self.s1, self.s2, self.s3, self.s4)[op // 16 - 1](op % 16)
+
+    def at(self, loop, step, place):
+        for number in range(4):
+            ops = SCATTER_PLAN.get((loop, number), {}).get(place)
+            if ops:
+                pl.when(step == number)(functools.partial(self.run, ops))
+
+    def finish(self):
+        for u, (group, s) in enumerate(BACK_UNITS):
+            for kind in range(5 if s == 0 else 6):
+                self.outgoing(u, kind).wait_send()
+
+
+BACK_UNITS = ((1, 3), (2, 3), (1, 2), (2, 2), (1, 1), (2, 1), (1, 0), (2, 0), (0, 3), (0, 2), (0, 1), (0, 0))
+SCATTER_PLAN = {
+    ("other", 0): {0: (0x30, 0x12), 2: (0x21,)},
+    ("other", 1): {0: (0x31, 0x13), 1: (0x40,), 2: (0x22,)},
+    ("other", 2): {0: (0x32, 0x14), 1: (0x41,), 2: (0x23,)},
+    ("other", 3): {0: (0x33, 0x15), 1: (0x42,), 2: (0x24,)},
+    ("own", 0): {0: (0x34, 0x16), 1: (0x43,), 2: (0x25,)},
+    ("own", 1): {0: (0x35, 0x17), 1: (0x44,), 2: (0x26,)},
+    ("own", 2): {0: (0x36, 0x18), 1: (0x45,), 2: (0x27,)},
+    ("own", 3): {0: (0x37, 0x19), 1: (0x46,), 2: (0x28,)},
+}
+SCATTER_AFTER = ((0x1a, 0x1b, 0x38, 0x47, 0x29), (0x39, 0x48, 0x2a, 0x3a, 0x49, 0x2b, 0x3b, 0x4a, 0x4b))
+
+
+def back_kernel(
+    x_ref, line_ref, qaug_ref, kaug_ref, lse_ref, gain_ref,
+    xo_hbm, back_hbm, hidden_hbm, wa_hbm, own_hbm, oth_hbm, ctx_hbm, gi_hbm, go_hbm,
+    grad_ref, gain_grad_ref, line_grad_ref, sums_ref, result_ref,
+    xo, back, hidden, wa, own, oth, ctx, xt, xot, ab_ref, abt, acc_own, acc_oth, oth_out, oth_in,
+    dq_acc, d_oth, cb_ref, center_ref, near_ref, ga, sums, piece, diag, side, final,
+    lsem, ssem, osem, send, recv, psem,
+):
+    tokens = x_ref.shape[0]
+    nq = tokens // LANES
+    links = Links()
+    net = Scatter(links, (ga, gi_hbm, go_hbm), sums, piece, diag, side, final, result_ref, send, recv, psem)
+    loads = [
+        pltpu.make_async_copy(a, b, lsem.at[n])
+        for n, (a, b) in enumerate(((back_hbm, back), (xo_hbm, xo), (hidden_hbm, hidden)))
+    ]
+
+    def step_loads(s):
+        return [
+            pltpu.make_async_copy(a.at[s], b.at[s], ssem.at[s, n])
+            for n, (a, b) in enumerate(((wa_hbm, wa), (own_hbm, own), (oth_hbm, oth), (ctx_hbm, ctx)))
+        ]
+
+    loads[0].start()
+    for copy in step_loads(3):
+        copy.start()
+    loads[1].start()
+    for s in (2, 1, 0):
+        for copy in step_loads(s):
+            copy.start()
+    loads[2].start()
+    links.meet()
+    net.run((0x10, 0x11))
+    loads[0].wait()
+    ab = back[...].astype(BF16)
+    ab_ref[...] = ab
+    abt[...] = ab.T
+    net.run((0x20,))
+    xt[...] = x_ref[...].T
+    acc_own[...] = jnp.zeros_like(acc_own)
+    acc_oth[...] = jnp.zeros_like(acc_oth)
+    loads[1].wait()
+    xot[...] = xo[...].T
+    masks = [half_rows(0), half_rows(1)]
+    own_at = {c: slice(at * LANES, (at + 1) * LANES) for at, c in enumerate((0, 1, 2, 4, 5))}
+    oth_at = {c: slice(at * LANES, (at + 1) * LANES) for at, c in enumerate((1, 2, 4, 5))}
+    cb_at = {2: slice(0, LANES), 4: slice(LANES, 2 * LANES)}
+    at_row = lax.broadcasted_iota(jnp.int32, (LANES, LANES), 0) + lax.broadcasted_iota(jnp.int32, (LANES, LANES), 1)
+    mirror = (at_row == LANES - 1).astype(F32).astype(BF16)
+
+    def one_side(s, i, other):
+        qc, qh, kc, vc, vh = HEAD_AT[i]
+        line = line_ref[s, i : i + 1, :]
+        tile = bias_tile(line)
+        qm = own[s, :, own_at[qc]] * masks[qh]
+        qa = qm + query_aug(qaug_ref[s], i, nq) * masks[1 - qh]
+        om = cb_ref[s, :, cb_at[vc]] * masks[vh]
+        center = center_ref[s, i : i + 1, :]
+        lse = lse_ref[s, i : i + 1, :]
+        flags = (line_ref[s, 3:4, :LANES], line_ref[s, 4:5, :LANES])
+        parts = near_parts(tile)
+        corner = corner_parts(tile, line, flags)
+        side = 1 if other else 0
+        k_cols = oth[s, :, oth_at[kc]] if other else own[s, :, own_at[kc]]
+        v_cols = oth[s, :, oth_at[vc]] if other else own[s, :, own_at[vc]]
+        ka = k_cols * masks[qh] + kaug_ref[side * tokens : (side + 1) * tokens] * masks[1 - qh]
+        scores = mt(ka, qa)
+        chance_back = mt(v_cols, om)
+        near = [None] * 5
+        ps, ds = [], []
+        for jb in range(nq):
+            row_p, row_d = [], []
+            for ib in range(nq):
+                at = (slice(jb * LANES, (jb + 1) * LANES), slice(ib * LANES, (ib + 1) * LANES))
+                block = scores[at]
+                kind = None
+                if not other and abs(jb - ib) <= 1:
+                    kind = jb - ib + 1
+                    block = block + parts[kind]
+                elif other and jb == 0 and ib == nq - 1:
+                    kind = 3
+                    block = block + corner[0]
+                elif other and jb == nq - 1 and ib == 0:
+                    kind = 4
+                    block = block + corner[1]
+                p = jnp.exp(block - lse[:, at[1]])
+                d = p * (chance_back[at] - center[:, at[1]])
+                if kind is not None:
+                    near[kind] = d if near[kind] is None else near[kind] + d
+                row_p.append(p.astype(BF16))
+                row_d.append(d.astype(BF16))
+            ps.append(jnp.concatenate(row_p, axis=1))
+            ds.append(jnp.concatenate(row_d, axis=1))
+        pb = jnp.concatenate(ps, axis=0)
+        db = jnp.concatenate(ds, axis=0)
+        return mm(ka.T, db), mm(db, qm), mm(pb, om), near
+
+    def other_side(it, carry):
+        s = 3 - it
+        for copy in step_loads(s):
+            copy.wait()
+        cb = {
+            2: mm(ab_ref[...], wa[s, :, 3 * LANES : 4 * LANES]).astype(BF16),
+            4: mm(ab_ref[...], wa[s, :, 5 * LANES :]).astype(BF16),
+        }
+        centers = []
+        for i in range(3):
+            vc, vh = HEAD_AT[i][3:]
+            prod = cb[vc].astype(F32) * ctx[s, :, cb_at[vc]].astype(F32)
+            high = prod.astype(BF16)
+            low = (prod - high.astype(F32)).astype(BF16)
+            pick = jnp.broadcast_to(masks[vh], (8, LANES))
+            centers.append((mt(pick, high) + mt(pick, low))[0:1, :])
+        for c in cb:
+            cb_ref[s, :, cb_at[c]] = cb[c]
+        center_ref[s] = jnp.concatenate(centers + [jnp.zeros((5, tokens), F32)], axis=0)
+        dk, dv = {}, {}
+        for i, (qc, qh, kc, vc, vh) in enumerate(HEAD_AT):
+            net.at("other", it, i)
+            dq_acc[s, i], part_k, part_v, near = one_side(s, i, True)
+            dk[kc] = dk[kc] + part_k if kc in dk else part_k
+            dv[vc] = dv[vc] + part_v if vc in dv else part_v
+            near_ref[s, i, 0] = near[3]
+            near_ref[s, i, 1] = near[4]
+        d = jnp.concatenate([dk[1], dv[2], dv[4], dk[5]], axis=1).astype(BF16)
+        d_oth[s] = d
+        acc_oth[...] += mt(d[:, : 2 * LANES], wa[s, :, LANES : 3 * LANES]) + mt(d[:, 2 * LANES :], wa[s, :, 4 * LANES :])
+        return carry
+
+    lax.fori_loop(0, 4, other_side, 0)
+    oth_out[...] = acc_oth[...].astype(BF16)
+    swap = remote(oth_out, oth_in, osem.at[0], osem.at[1], links.at_z[1])
+    swap.start()
+
+    def own_side(it, carry):
+        s = 3 - it
+        dk, dv, dq = {}, {}, []
+        for i, (qc, qh, kc, vc, vh) in enumerate(HEAD_AT):
+            net.at("own", it, i)
+            part_q, part_k, part_v, near = one_side(s, i, False)
+            part_q = part_q + dq_acc[s, i]
+            dk[kc] = dk[kc] + part_k if kc in dk else part_k
+            dv[vc] = dv[vc] + part_v if vc in dv else part_v
+            at = HDIM if qh == 0 else 0
+            sums_ref[s, i * 8 : (i + 1) * 8, :] = part_q[at + 8 : at + 16, :]
+            dq.append(part_q[:HDIM] if qh == 0 else part_q[HDIM:])
+            flags = (line_ref[s, 3:4, :LANES], line_ref[s, 4:5, :LANES])
+            first, final_corner = near_ref[s, i, 0] * flags[0], near_ref[s, i, 1] * flags[1]
+            blank = jnp.zeros((LANES, LANES), F32)
+            tile = jnp.concatenate([near[1], near[0] + final_corner, blank, near[2] + first], axis=1)
+            high = tile.astype(BF16)
+            low = (tile - high.astype(F32)).astype(BF16)
+            turned = pltpu.roll(mm(mirror, high) + mm(mirror, low), 0, 1, stride=1, stride_axis=0)
+            line_grad_ref[s, i : i + 1, :] = jnp.sum(turned, axis=0, keepdims=True)
+            line_grad_ref[s, 3 + i : 4 + i, :] = jnp.concatenate(
+                [
+                    jnp.sum(first, axis=0, keepdims=True),
+                    jnp.sum(final_corner, axis=0, keepdims=True),
+                    jnp.zeros((1, 2 * LANES), F32),
+                ],
+                axis=1,
+            )
+        line_grad_ref[s, 6:8, :] = jnp.zeros((2, 4 * LANES), F32)
+        dq_a = jnp.concatenate([dq[0], dq[1]], axis=0).T
+        dq_b = jnp.concatenate([dq[2], jnp.zeros_like(dq[2])], axis=0).T
+        d_own = jnp.concatenate([dq_a, dk[1], dv[2], dq_b + dv[4], dk[5]], axis=1).astype(BF16)
+        g_own = mm(xt[...], d_own)
+        g_oth = mm(xot[...], d_oth[s])
+        g_ctx = mm(abt[...], ctx[s])
+        columns = [
+            g_own[:, :LANES],
+            g_own[:, LANES : 3 * LANES] + g_oth[:, : 2 * LANES],
+            g_ctx[:, :LANES],
+            g_own[:, 3 * LANES : 4 * LANES] + g_oth[:, 2 * LANES : 3 * LANES],
+            g_own[:, 4 * LANES :] + g_oth[:, 3 * LANES :] + g_ctx[:, LANES:],
+        ]
+        g = jnp.concatenate(columns, axis=1).astype(BF16)
+        rows = ga.shape[3]
+        for n in range(8):
+            ga[s, n // 2, n % 2] = g[n * rows : (n + 1) * rows, :]
+        acc_own[...] += mt(d_own[:, : 3 * LANES], wa[s, :, : 3 * LANES]) + mt(d_own[:, 3 * LANES :], wa[s, :, 4 * LANES :])
+        return carry
+
+    lax.fori_loop(0, 4, own_side, 0)
+    net.run(SCATTER_AFTER[0])
+    loads[2].wait()
+    swap.wait_recv()
+    one_back = acc_own[...] + oth_in[...].astype(F32)
+    grad, gain_part = rms_back(hidden[...], gain_ref[0:1, :], one_back)
+    grad_ref[...] = grad + back[...]
+    gain_grad_ref[...] = jnp.broadcast_to(gain_part, gain_grad_ref.shape)
+    net.run(SCATTER_AFTER[1])
+    for group in (1, 2, 0):
+        net.last(group)
+    swap.wait_send()
+    net.finish()
+
+
+def sum_kernel(x_ref, out_ref, held, other, send, recv):
+    links = Links()
+    near = []
+    for k in range(1, 8):
+        dp = links.dp
+        for stride in (1, 2, 4):
+            if k & stride:
+                dp = peer(dp, stride)
+        near.append((dp, links.mp))
+    barrier = pltpu.get_barrier_semaphore()
+    everyone = near + list(links.at_z[1:])
+    for to in everyone:
+        pl.semaphore_signal(barrier, inc=1, device_id=to, device_id_type=MESH)
+    pl.semaphore_wait(barrier, len(everyone))
+    first = [remote(x_ref, held.at[n], send.at[n], recv.at[n], to) for n, to in enumerate(near)]
+    for copy in first:
+        copy.start()
+    total = x_ref[...]
+    for copy in first:
+        copy.wait_recv()
+    for n in range(7):
+        total = total + held[n]
+    other[0] = total
+    second = [
+        remote(other.at[0], other.at[n], send.at[6 + n], recv.at[6 + n], links.at_z[n]) for n in (1, 2, 3)
+    ]
+    for copy in second:
+        copy.start()
+    for copy in second:
+        copy.wait_recv()
+    out_ref[...] = (other[0] + other[1]) + (other[2] + other[3])
+    for copy in first + second:
+        copy.wait_send()
+
+
+def sum_all(x):
+    dma = pltpu.SemaphoreType.DMA
+    vmem = pl.BlockSpec(memory_space=pltpu.VMEM)
+    return pl.pallas_call(
+        sum_kernel,
+        in_specs=[vmem],
+        out_specs=vmem,
+        out_shape=jax.ShapeDtypeStruct(x.shape, F32),
+        scratch_shapes=[pltpu.VMEM((7, *x.shape), F32), pltpu.VMEM((4, *x.shape), F32), dma((10,)), dma((10,))],
+        compiler_params=pltpu.CompilerParams(collective_id=2, has_side_effects=True),
+        name="finish_sums",
+    )(x)
+
+
+def run_front(x, shard, line, qaug, kaug, gains, hidden, grad):
+    t, d = x.shape
+    parts, cols = line.shape[0], shard.shape[2]
+    any_space = pl.BlockSpec(memory_space=pl.ANY)
+    vmem = pl.BlockSpec(memory_space=pltpu.VMEM)
+    dma = pltpu.SemaphoreType.DMA
+    return pl.pallas_call(
+        front_kernel,
+        in_specs=[vmem] * 6 + [any_space] * 2,
+        out_specs=[any_space] * 3 + [vmem] + [any_space] * 2 + [vmem] * 3 + [any_space] * 2,
+        out_shape=[
+            jax.ShapeDtypeStruct((parts, t, 5 * LANES), BF16),
+            jax.ShapeDtypeStruct((parts, t, 4 * LANES), BF16),
+            jax.ShapeDtypeStruct((parts, t, 2 * LANES), BF16),
+            jax.ShapeDtypeStruct((parts, 8, t), F32),
+            jax.ShapeDtypeStruct((parts, d, cols), BF16),
+            jax.ShapeDtypeStruct((t, d), BF16),
+            jax.ShapeDtypeStruct((t, d), F32),
+            jax.ShapeDtypeStruct((t, d), F32),
+            jax.ShapeDtypeStruct((8, d), F32),
+            jax.ShapeDtypeStruct((parts, d, cols), BF16),
+            jax.ShapeDtypeStruct((parts, d, cols), BF16),
+        ],
+        scratch_shapes=[
+            pltpu.VMEM((3, parts, d, cols), BF16),
+            pltpu.VMEM((t, d), BF16),
+            pltpu.VMEM((parts, t, 5 * LANES), BF16),
+            pltpu.VMEM((parts, t, 4 * LANES), BF16),
+            pltpu.VMEM((parts, t, 2 * LANES), BF16),
+            pltpu.VMEM((2, 2 * t, t), F32),
+            pltpu.VMEM((2, 2 * t, t), BF16),
+            pltpu.VMEM((t, d), F32),
+            pltpu.VMEM((t, d), F32),
+            pltpu.VMEM((t, d), BF16), pltpu.VMEM((d, t), BF16),
+            pltpu.VMEM((t, d), BF16), pltpu.VMEM((d, t), BF16),
+            pltpu.VMEM((t, d), F32), pltpu.VMEM((t, d), F32),
+            pltpu.VMEM((2, d, cols), BF16), pltpu.VMEM((2, d, cols), BF16),
+            dma((12, 8)), dma((12, 8)), dma((9,)), dma((9,)), dma((2,)), dma((5,)), dma((5,)), dma((2, 2)),
+        ],
+        compiler_params=pltpu.CompilerParams(
+            vmem_limit_bytes=62 * 2**20, collective_id=0, has_side_effects=True
+        ),
+        name="front",
+    )(x, shard, line, qaug, kaug, gains, hidden, grad)
+
+
+def run_back(x, xo, back, hidden, wa, line, qaug, kaug, own, oth, ctx, lse, gi, go, gains):
+    t, d = x.shape
+    parts, cols = wa.shape[0], wa.shape[2]
+    rows = d // 8
+    any_space = pl.BlockSpec(memory_space=pl.ANY)
+    vmem = pl.BlockSpec(memory_space=pltpu.VMEM)
+    dma = pltpu.SemaphoreType.DMA
+    split = (parts, 4, 2, rows, cols)
+    return pl.pallas_call(
+        back_kernel,
+        in_specs=[vmem] * 6 + [any_space] * 9,
+        out_specs=[vmem] * 5,
+        out_shape=[
+            jax.ShapeDtypeStruct((t, d), F32),
+            jax.ShapeDtypeStruct((8, d), F32),
+            jax.ShapeDtypeStruct((parts, 8, t), F32),
+            jax.ShapeDtypeStruct((parts, 24, t), F32),
+            jax.ShapeDtypeStruct((3, rows, cols), F32),
+        ],
+        scratch_shapes=[
+            pltpu.VMEM((t, d), BF16), pltpu.VMEM((t, d), F32), pltpu.VMEM((t, d), F32),
+            pltpu.VMEM(wa.shape, BF16), pltpu.VMEM(own.shape, BF16), pltpu.VMEM(oth.shape, BF16), pltpu.VMEM(ctx.shape, BF16),
+            pltpu.VMEM((d, t), BF16), pltpu.VMEM((d, t), BF16), pltpu.VMEM((t, d), BF16), pltpu.VMEM((d, t), BF16),
+            pltpu.VMEM((t, d), F32), pltpu.VMEM((t, d), F32), pltpu.VMEM((t, d), BF16), pltpu.VMEM((t, d), BF16),
+            pltpu.VMEM((parts, 3, LANES, t), F32), pltpu.VMEM((parts, t, 4 * LANES), BF16),
+            pltpu.VMEM((parts, t, 2 * LANES), BF16), pltpu.VMEM((parts, 8, t), F32), pltpu.VMEM((parts, 3, 2, LANES, LANES), F32),
+            pltpu.VMEM(split, BF16), pltpu.VMEM((12, 4, rows, cols), BF16), pltpu.VMEM((3, 4, rows, cols), BF16),
+            pltpu.VMEM((12, 2, rows // 2, cols), BF16), pltpu.VMEM((12, 2, rows, cols), BF16), pltpu.VMEM((3, 3, rows, cols), BF16),
+            dma((3,)), dma((parts, 4)), dma((2,)), dma((12, 6)), dma((12, 6)), dma((3,)),
+        ],
+        compiler_params=pltpu.CompilerParams(
+            vmem_limit_bytes=62 * 2**20, collective_id=1, has_side_effects=True
+        ),
+        name="back",
+    )(x, line, qaug, kaug, lse, gains, xo, back, hidden, wa, own, oth, ctx, gi.reshape(split), go.reshape(split))
+
+
+def pack_attn(attn, out_t):
+    cut = [[part[:, i * HDIM : (i + 1) * HDIM] for i in range(3)] for part in (attn[0], attn[1], attn[2], out_t)]
+    q, k, v, o = cut
+    return jnp.concatenate([q[0], q[1], k[0], k[1], v[0], v[1], o[0], o[1], q[2], v[2], k[2], o[2]], axis=1)
+
+
+def unpack_attn(block):
+    c = [block[:, i * HDIM : (i + 1) * HDIM] for i in range(12)]
+    attn = jnp.stack(
+        [
+            jnp.concatenate([c[0], c[1], c[8]], axis=1),
+            jnp.concatenate([c[2], c[3], c[10]], axis=1),
+            jnp.concatenate([c[4], c[5], c[9]], axis=1),
+        ]
+    )
+    return attn, jnp.concatenate([c[6], c[7], c[11]], axis=1)
+
+
+def body(
+    hidden_in, out_grad, attn_weight, out_weight, inner_weight, outer_weight, rel_bias, gains, lengths, table,
+    attn_first, attn_second, out_first, out_second, inner_first, inner_second, outer_first, outer_second,
+    rel_first, rel_second, gain_first, gain_second, *, parts,
+):
+    tokens = hidden_in.shape[0]
+    nq = tokens // LANES
+    heads = rel_bias.shape[1]
+    per_seq = SEQLEN // tokens
+    mp_index = lax.axis_index("mp")
+    half = mp_index % per_seq
+    length = lengths[mp_index // per_seq]
+
+    shard = [
+        pack_attn(attn_weight.astype(BF16), out_weight.astype(BF16).T),
+        inner_weight.astype(BF16),
+        outer_weight.astype(BF16).T,
+    ]
+    order = jnp.bitwise_xor(mp_index, jnp.arange(parts))
+
+    x1 = rms_scaled(hidden_in, gains[0]).astype(BF16)
+
+    u = jnp.arange(4 * LANES)
+    offset = jnp.where(u < 2 * LANES, -u, 4 * LANES - u)
+    buckets = jnp.arange(rel_bias.shape[0], dtype=jnp.int32)
+    line_hot = (jnp.take(table, offset + SEQLEN - 1)[:, None] == buckets[None, :]).astype(F32)
+    line = jnp.dot(line_hot, rel_bias, precision=lax.Precision.HIGHEST).T.reshape(parts, heads // parts, 4 * LANES)
+    first_flag = (half == 0).astype(F32)
+    flags = jnp.stack([jnp.full((4 * LANES,), first_flag), jnp.full((4 * LANES,), 1.0 - first_flag)])
+    line_in = jnp.concatenate(
+        [line, jnp.broadcast_to(flags[None], (parts, 2, 4 * LANES)), jnp.zeros((parts, 3, 4 * LANES), F32)], axis=1
+    )
+    far_before, far_after = line[:, :, LANES], line[:, :, 3 * LANES]
+    jb, ib = jnp.arange(nq)[None, :], jnp.arange(nq)[:, None]
+    own_before, own_after = (jb < ib - 1).astype(F32), (jb > ib + 1).astype(F32)
+    oth_before = jnp.full((nq, nq), 1.0 - first_flag)
+    w_before = jnp.concatenate([own_before, oth_before], axis=1)
+    w_after = jnp.concatenate([own_after, 1.0 - oth_before], axis=1)
+    far = far_before[:, :, None, None] * w_before + far_after[:, :, None, None] * w_after
+    far_hi = far.astype(BF16).astype(F32)
+    far_lo = far - far_hi
+    one = jnp.ones((parts, heads // parts, nq, 1), F32)
+    blank = jnp.zeros((parts, heads // parts, nq, HDIM), F32)
+    q64 = jnp.concatenate(
+        [blank[..., :3], one, blank[..., :4], far_hi, far_lo, blank[..., : HDIM - 8 - 4 * nq]], axis=-1
+    )
+    qaug = jnp.concatenate([q64, q64], axis=-1).reshape(parts, 3 * nq, LANES)
+    qaug = jnp.pad(qaug, ((0, 0), (0, 16 - 3 * nq), (0, 0))).astype(BF16)
+    row = jnp.arange(2 * tokens)
+    position = jnp.where(row < tokens, half * tokens + row, (1 - half) * tokens + row - tokens)
+    masked = jnp.where(position < length, 0.0, NEG)
+    col = jnp.arange(LANES) % HDIM
+    block_of = row // LANES
+    hot = ((col >= 8) & (col < 8 + 4 * nq))[None, :] & ((col[None, :] - 8) % (2 * nq) == block_of[:, None])
+    kaug = jnp.where((col == 3)[None, :], masked[:, None], hot.astype(F32)).astype(BF16)
+
+    line_in, qaug = jnp.take(line_in, order, axis=0), jnp.take(qaug, order, axis=0)
+    own, oth, ctx, lse, wa, x1o, block_out, middle_back, gain_two, gi, go = run_front(
+        x1, jnp.stack(shard), line_in, qaug, kaug, gains, hidden_in, out_grad
+    )
+    input_grad, gain_one, line_grad, sums, owned = run_back(
+        x1, x1o, middle_back, hidden_in, wa, line_in, qaug, kaug, own, oth, ctx, lse, gi, go, gains
+    )
+
+    line_grad = jnp.take(line_grad, order, axis=0)
+    near_line = jnp.roll(line_grad[:, :3], 1 - LANES, axis=2)
+    sums = jnp.take(sums, order, axis=0)
+    near_grad = jnp.einsum(
+        "ub,hu->bh", line_hot, near_line.reshape(heads, 4 * LANES), precision=lax.Precision.HIGHEST
+    )
+    corner = jnp.sum(line_grad[:, 3:6].reshape(heads, 4, LANES), axis=-1)
+    block_sums = jnp.sum(sums.reshape(heads, 2 * nq, nq, LANES), axis=-1)
+    far_w = jnp.transpose(jnp.stack([w_before, w_after]), (0, 2, 1))
+    far_grad = jnp.einsum("hji,sji->sh", block_sums, far_w, precision=lax.Precision.HIGHEST)
+    far_grad = far_grad - jnp.stack([corner[:, 1], corner[:, 0]])
+    far_hot = (jnp.stack([table[0], table[2 * SEQLEN - 2]])[None, :] == buckets[:, None]).astype(F32)
+    rel_part = near_grad + jnp.dot(far_hot, far_grad, precision=lax.Precision.HIGHEST)
+
+    g_attn, g_out_t = unpack_attn(owned[0])
+    grads = (g_attn, g_out_t.T, owned[1], owned[2].T)
+    square_part = jnp.sum(owned * owned)
+    width = gains.shape[1]
+    small = jnp.concatenate(
+        [gain_one[0], gain_two[0], rel_part.reshape(-1), jnp.full((LANES,), square_part)]
+    ).reshape(-1, LANES)
+    small = sum_all(jnp.pad(small, ((0, -small.shape[0] % 8), (0, 0)))).reshape(-1)
+    gain_grad = small[: 2 * width].reshape(2, width)
+    rel_grad = small[2 * width : 2 * width + rel_bias.size].reshape(rel_bias.shape)
+    square_total = small[2 * width + rel_bias.size]
+    grad_norm = jnp.sqrt(square_total + jnp.sum(gain_grad * gain_grad) + jnp.sum(rel_grad * rel_grad))
+    factor = jnp.minimum(1.0, CLIP / (grad_norm + 1e-06))
+    attn_new = adam_step(attn_weight, grads[0], attn_first, attn_second, factor, RATE_MATRIX)
+    out_new = adam_step(out_weight, grads[1], out_first, out_second, factor, RATE_OUT)
+    inner_new = adam_step(inner_weight, grads[2], inner_first, inner_second, factor, RATE_MATRIX)
+    outer_new = adam_step(outer_weight, grads[3], outer_first, outer_second, factor, RATE_MATRIX)
+    rel_new = adam_step(rel_bias, rel_grad, rel_first, rel_second, factor, RATE_SMALL)
+    gain_new = adam_step(gains, gain_grad, gain_first, gain_second, factor, RATE_SMALL)
+    return (block_out, input_grad, grad_norm, *attn_new, *out_new, *inner_new, *outer_new, *rel_new, *gain_new)
 
 
 def forward_kernel(
@@ -448,25 +1304,7 @@
     )(x, xo, back, wa, line, qaug, kaug, own, oth, ctx, lse)
 
 
-def pack_attn(attn, out_t):
-    cut = [[part[:, i * HDIM : (i + 1) * HDIM] for i in range(3)] for part in (attn[0], attn[1], attn[2], out_t)]
-    q, k, v, o = cut
-    return jnp.concatenate([q[0], q[1], k[0], k[1], v[0], v[1], o[0], o[1], q[2], v[2], k[2], o[2]], axis=1)
-
-
-def unpack_attn(block):
-    c = [block[:, i * HDIM : (i + 1) * HDIM] for i in range(12)]
-    attn = jnp.stack(
-        [
-            jnp.concatenate([c[0], c[1], c[8]], axis=1),
-            jnp.concatenate([c[2], c[3], c[10]], axis=1),
-            jnp.concatenate([c[4], c[5], c[9]], axis=1),
-        ]
-    )
-    return attn, jnp.concatenate([c[6], c[7], c[11]], axis=1)
-
-
-def body(
+def general_body(
     hidden_in, out_grad, attn_weight, out_weight, inner_weight, outer_weight, rel_bias, gains, lengths, table,
     attn_first, attn_second, out_first, out_second, inner_first, inner_second, outer_first, outer_second,
     rel_first, rel_second, gain_first, gain_second, *, parts,
@@ -585,7 +1423,8 @@
         attn, attn, down, down, up, up, down, down, P(), P(), P(), P(),
     )
     out_specs = (rows, rows, P()) + (attn,) * 3 + (down,) * 3 + (up,) * 3 + (down,) * 3 + (P(),) * 6
+    plan = body if (mesh.shape["dp"], mesh.shape["mp"]) == (8, 4) else general_body
     return jax.shard_map(
-        functools.partial(body, parts=mesh.shape["mp"]),
+        functools.partial(plan, parts=mesh.shape["mp"]),
         mesh=mesh, in_specs=in_specs, out_specs=out_specs, check_vma=False,
     )

time: 926 us -> 243 us (0.26)
  waiting for transfers between devices: 463 us -> 0 us
  local copies, waits for them, and re-layouts: 286 us -> 20.5 us
  Pallas kernels: 80.8 us -> 199 us
  blocking collectives: 39.6 us -> 0 us
  between operations: 20 us -> 4.55 us
    all_gather x6 -> x0, waiting for transfers between devices: 284 us -> none  [the longest x3 206 us: body(): lax.all_gather(lax.all_gather(s, 'dp', axis=0, tiled=True), 'mp', axis=1,...]
    gather x1 -> x4, local copies, waits for them, and re-layouts: 271 us -> 4.09 us  [the longest x1 1.58 us: body(): sums = jnp.take(sums, order, axis=0)]
    reduce_scatter x6 -> x0, waiting for transfers between devices: 133 us -> none  [the longest x3 82.2 us: body(): lax.psum_scatter(g, 'mp', scatter_dimension=1, tiled=True)]
    pallas_call x3, Pallas kernels: 80.8 us -> 199 us  [the longest x1 105 us: run_front(): pl.pallas_call(front_kernel, in_specs=[vmem] * 6 + [any_space] * 2, out_s...]
    ppermute x2 -> x0, waiting for transfers between devices: 44.1 us -> none  [the longest x1 38.9 us: body(): x1o = lax.ppermute(x1, 'mp', swap)]
    psum x1 -> x0, blocking collectives: 39.6 us -> none  [body(): lax.psum((jnp.concatenate([gain_one, gain_two[:1]], axis=0), rel_part, sq...]
  transfers between devices with their start and end apart: 14 -> 0, of which waited for: 11 -> 0; matrix products, arithmetic and copies ran while one was open for 33% -> 0% of each run, Pallas kernels for 2% -> 0%
where the time goes in v2:
time: 243 us
  Pallas kernels  199 us (82%)
  local copies, waits for them, and re-layouts  20.5 us (8%)
  other arithmetic  17.5 us (7%)
  between operations  4.55 us (2%)
    pallas_call x1, Pallas kernels, run_front(): pl.pallas_call(front_kernel, in_specs=[vmem] * 6 + [any_space] * 2, out_s...  105 us
    pallas_call x1, Pallas kernels, run_back(): pl.pallas_call(back_kernel, in_specs=[vmem] * 6 + [any_space] * 9, out_sp...  83.6 us
    pallas_call x1, Pallas kernels, sum_all(): pl.pallas_call(sum_kernel, in_specs=[vmem], out_specs=vmem, out_shape=jax...  10.4 us
    unnamed x60, local copies, waits for them, and re-layouts  5.9 us

profile of v2, /device:TPU:0, one launch (start us, length us, event | category | flops | bytes accessed | tf_op | source)
XLA Modules:
  0.0 242.7 jit_solution(855640231296583236)
XLA Ops:
  0.9 3.4 %gather_fusion = s32[512]{0:T(512)S(1)} fusion(s32[2047]{0:T(1024)} %param.33, s32[1024]{0:T(1024)S(1)} %pad_clamp_fusion.2), kind=kCustom, calls=%fused_computation.2 | custom fusion | bytes 6144 | tf_op jit(solution)/shard_map/jit(_take)/gather | solution.py:891
  4.4 0.3 convolution_bitcast_fusion
  4.7 0.1 slice_reduce_fusion.3
  4.9 0.1 mul.374
  5.1 0.1 mul.382
  5.2 0.1 subtract_convert_fusion
  5.3 0.1 concatenate.47
  5.5 0.6 gather_fusion.1
  6.1 0.7 pad_select_fusion.qaug_ref
  6.7 0.6 dynamic_slice.3
  7.3 0.7 fusion.20
  8.0 1.0 select_convert_fusion.kaug_ref
  9.3 0.6 gather_fusion.3
  9.9 0.7 broadcast_select_fusion.1.line_ref
  10.7 0.1 copy.128
  10.9 0.1 concatenate.43
  11.1 0.8 pad_maximum_fusion.shard_ref
  11.9 0.2 copy-done
  12.0 0.2 multiply_reduce_fusion
  12.2 1.1 multiply_convert_fusion.x_ref
  13.3 105.2 %front.1 = (bf16[4,512,640]{2,1,0:T(8,128)(2,1)}, bf16[4,512,512]{2,1,0:T(8,128)(2,1)}, bf16[4,512,256]{2,1,0:T(8,128)(2,1)}, f32[4,8,512]{2,1,0:T(8,128)}, bf16...) custom-call(bf16[512,768]{1,0:T(8,128)(2,1)} %multiply_convert_fusio, ...), custom_call_target="tpu_custom_call" | custom-call | tf_op jit(solution)/shard_map/front/pallas_call | solution.py:771
  118.5 83.6 %back.1 = (f32[512,768]{1,0:T(8,128)}, f32[8,768]{1,0:T(8,128)}, f32[4,8,512]{2,1,0:T(8,128)}, f32[4,24,512]{2,1,0:T(8,128)}, f32[3,96,768]{2,1,0:T(8,128)}) custom-call(bf16[512,768]{1,0:T(8,128)(2,1)} %multiply_convert_fusion.x_ref, f32[4,8,512]{2,1,0:T(8,128)} %broadcast_select_fusion.1.line_ref, bf16[4,16,128]{2,1,0:T(8,128)(2,1)} %pad_select_fusion.qaug_ref, ...), custom_call_target="tpu_custom_call" | custom-call | tf_op jit(solution)/shard_map/back/pallas_call | solution.py:819
  202.3 1.6 gather_fusion.2
  203.9 0.1 broadcast_in_dim.104
  204.0 0.2 select_reduce_fusion
  204.2 1.4 gather_fusion.4
  205.7 0.1 reduce_sum.56
  205.8 0.2 slice_reduce_fusion.1
  206.0 0.1 fusion
  206.2 0.1 slice.206
  206.3 0.1 pad_maximum_fusion.1
  206.4 0.3 fusion.6
  206.7 1.3 fusion.40
  208.0 1.4 pad_add_fusion
  209.3 0.2 convolution_add_fusion
  209.5 0.1 copy.132
  209.6 0.1 reshape.275
  209.7 0.8 slice_reduce_fusion.5
  210.5 0.8 multiply_reduce_fusion.1
  211.4 0.6 broadcast_in_dim.107
  212.0 0.8 slice_reduce_fusion.4
  212.8 0.6 maximum_bitcast_fusion.3.x_ref
  213.4 10.4 %finish_sums.1 = f32[16,128]{1,0:T(8,128)} custom-call(f32[16,128]{1,0:T(8,128)} %maximum_bitcast_fusion.3.x_ref), custom_call_target="tpu_custom_call" | custom-call | tf_op jit(solution)/shard_map/finish_sums/pallas_call | solution.py:754
  223.8 1.2 slice.211
  225.0 1.3 multiply_reduce_fusion.2
  227.6 1.3 multiply_reduce_fusion.3
  229.6 0.7 slice_multiply_fusion.2
  230.3 0.6 add_subtract_fusion.1
  230.9 0.7 slice_multiply_fusion.3
  231.6 0.1 mul.460
  231.8 0.6 add_subtract_fusion
  232.4 1.0 multiply_subtract_fusion
  233.5 1.1 multiply_subtract_fusion.1
  234.7 0.1 fusion.39
  234.8 0.1 copy.133
  234.9 0.1 copy.134
  235.0 0.1 multiply_subtract_fusion.3
  235.1 0.7 copy.140
  235.8 0.7 copy.141
  236.5 0.7 copy.142
  237.4 1.1 multiply_subtract_fusion.2
  238.4 1.1 copy.147
  239.6 0.8 copy-done.3
  240.4 1.1 copy.148
  (110 shorter events, 1.3 us)
Async XLA Ops:
  0.7 3.7 %copy-start.20 = (f32[32,12]{0,1:T(8,128)S(1)}, f32[32,12]{0,1:T(8,128)}, u32[]{:S(2)}) copy-start(f32[32,12]{0,1:T(8,128)} %param.30) | copy-start | bytes 4612
  0.7 6.1 %copy-start.25 = (s32[2]{0:T(128)S(1)}, s32[2]{0:T(128)}, u32[]{:S(2)}) copy-start(s32[2]{0:T(128)} %param.32) | copy-start | bytes 28
  0.9 9.7 %copy-start.7 = (f32[3,96,192]{2,1,0:T(8,128)S(1)}, f32[3,96,192]{2,1,0:T(8,128)}, u32[]{:S(2)}) copy-start(f32[3,96,192]{2,1,0:T(8,128)} %param.26) | copy-start | bytes 663556
  4.4 6.4 %copy-start.15 = (f32[192,96]{1,0:T(8,128)S(1)}, f32[192,96]{1,0:T(8,128)}, u32[]{:S(2)}) copy-start(f32[192,96]{1,0:T(8,128)} %param.27) | copy-start | bytes 221188
  4.4 6.6 %copy-start.4 = (f32[768,96]{0,1:T(8,128)S(1)}, f32[768,96]{0,1:T(8,128)}, u32[]{:S(2)}) copy-start(f32[768,96]{0,1:T(8,128)} %param.29) | copy-start | bytes 884740
  5.3 5.7 %copy-start.5 = (f32[96,768]{1,0:T(8,128)S(1)}, f32[96,768]{1,0:T(8,128)}, u32[]{:S(2)}) copy-start(f32[96,768]{1,0:T(8,128)} %param.28) | copy-start | bytes 884740
  10.6 1.4 copy-start
  11.0 1.2 copy-start.18
  202.2 8.3 %copy-start.1 = (f32[3,96,768]{2,1,0:T(8,128)S(1)}, f32[3,96,768]{2,1,0:T(8,128)}, u32[]{:S(2)}) copy-start(f32[3,96,768]{2,1,0:T(8,128)} %get-tuple-element.53) | copy-start | bytes 2654212
  202.2 28.1 %copy-start.19 = (f32[2,768]{1,0:T(2,128)S(1)}, f32[2,768]{1,0:T(2,128)}, u32[]{:S(2)}) copy-start(f32[2,768]{1,0:T(2,128)} %gain_ref.3) | copy-start | bytes 18436
  202.2 28.1 %copy-start.23 = (f32[2,768]{1,0:T(2,128)S(1)}, f32[2,768]{1,0:T(2,128)}, u32[]{:S(2)}) copy-start(f32[2,768]{1,0:T(2,128)} %param.44) | copy-start | bytes 18436
  202.2 28.1 %copy-start.24 = (f32[2,768]{1,0:T(2,128)S(1)}, f32[2,768]{1,0:T(2,128)}, u32[]{:S(2)}) copy-start(f32[2,768]{1,0:T(2,128)} %param.45) | copy-start | bytes 18436
  202.2 29.6 %copy-start.21 = (f32[32,12]{0,1:T(8,128)S(1)}, f32[32,12]{0,1:T(8,128)}, u32[]{:S(2)}) copy-start(f32[32,12]{0,1:T(8,128)} %param.42) | copy-start | bytes 4612
  202.2 29.6 %copy-start.22 = (f32[32,12]{0,1:T(8,128)S(1)}, f32[32,12]{0,1:T(8,128)}, u32[]{:S(2)}) copy-start(f32[32,12]{0,1:T(8,128)} %param.43) | copy-start | bytes 4612
  202.2 30.2 %copy-start.9 = (f32[768,96]{0,1:T(8,128)S(1)}, f32[768,96]{0,1:T(8,128)}, u32[]{:S(2)}) copy-start(f32[768,96]{0,1:T(8,128)} %param.40) | copy-start | bytes 884740
  202.2 30.2 %copy-start.10 = (f32[768,96]{0,1:T(8,128)S(1)}, f32[768,96]{0,1:T(8,128)}, u32[]{:S(2)}) copy-start(f32[768,96]{0,1:T(8,128)} %param.41) | copy-start | bytes 884740
  210.5 23.0 %copy-start.6 = (f32[96,768]{1,0:T(8,128)S(1)}, f32[96,768]{1,0:T(8,128)}, u32[]{:S(2)}) copy-start(f32[96,768]{1,0:T(8,128)} %param.28) | copy-start | bytes 884740
  210.5 23.0 %copy-start.11 = (f32[96,768]{1,0:T(8,128)S(1)}, f32[96,768]{1,0:T(8,128)}, u32[]{:S(2)}) copy-start(f32[96,768]{1,0:T(8,128)} %param.38) | copy-start | bytes 884740
  210.5 23.0 %copy-start.12 = (f32[96,768]{1,0:T(8,128)S(1)}, f32[96,768]{1,0:T(8,128)}, u32[]{:S(2)}) copy-start(f32[96,768]{1,0:T(8,128)} %param.39) | copy-start | bytes 884740
  233.5 1.3 copy-start.16
  233.5 1.3 copy-start.17
  234.6 2.7 %copy-start.8 = (f32[3,96,192]{2,1,0:T(8,128)S(1)}, f32[3,96,192]{2,1,0:T(8,128)}, u32[]{:S(2)}) copy-start(f32[3,96,192]{2,1,0:T(8,128)} %param.26) | copy-start | bytes 663556
  234.6 2.7 %copy-start.13 = (f32[3,96,192]{2,1,0:T(8,128)S(1)}, f32[3,96,192]{2,1,0:T(8,128)}, u32[]{:S(2)}) copy-start(f32[3,96,192]{2,1,0:T(8,128)} %param.34) | copy-start | bytes 663556
  234.6 2.7 %copy-start.14 = (f32[3,96,192]{2,1,0:T(8,128)S(1)}, f32[3,96,192]{2,1,0:T(8,128)}, u32[]{:S(2)}) copy-start(f32[3,96,192]{2,1,0:T(8,128)} %param.35) | copy-start | bytes 663556
  235.8 2.6 %copy-start.2 = (f32[512,768]{1,0:T(8,128)S(1)}, f32[512,768]{1,0:T(8,128)}, u32[]{:S(2)}) copy-start(f32[512,768]{1,0:T(8,128)} %get-tuple-element.240) | copy-start | bytes 4718596
  238.4 2.0 copy-start.3

commit v3 on v2

--- a/solution.py
+++ b/solution.py
@@ -77,8 +77,8 @@
 
 def corner_parts(tile, line, flags):
     before, same, after = near_parts(tile)
-    first = (after - line[:, 3 * LANES : 3 * LANES + 1]) * flags[0]
-    last = (before - line[:, LANES : LANES + 1]) * flags[1]
+    first = (after - line[:, 3 * LANES : 3 * LANES + 1]) * flags
+    last = (before - line[:, LANES : LANES + 1]) * (1.0 - flags)
     return first, last
 
 
@@ -101,11 +101,42 @@
     return rows
 
 
-def query_aug(qaug, i, nq):
-    rows = qaug.shape[0]
-    return jnp.concatenate(
-        [jnp.broadcast_to(qaug[i * nq + ib : i * nq + ib + 1, :], (LANES, LANES)) for ib in range(nq)], axis=0
-    )
+def far_masks(first, nq):
+    lane = lax.broadcasted_iota(jnp.int32, (8, LANES), 1) % HDIM
+    ib = lax.broadcasted_iota(jnp.int32, (8, LANES), 0)
+    jb = (lane - 8) % (2 * nq)
+    coded = (lane >= 8) & (lane < 8 + 4 * nq)
+    own_before = (coded & (jb < nq) & (jb < ib - 1)).astype(F32)
+    own_after = (coded & (jb < nq) & (jb > ib + 1)).astype(F32)
+    other = (coded & (jb >= nq)).astype(F32)
+    high = (lane < 8 + 2 * nq).astype(F32)
+    return own_before + other * (1.0 - first), own_after + other * first, high, (lane == 3).astype(F32)
+
+
+def query_aug(line, masks, nq):
+    before, after, high, one = masks
+    far = line[:, LANES : LANES + 1] * before + line[:, 3 * LANES : 3 * LANES + 1] * after
+    top = far.astype(BF16).astype(F32)
+    rows = (high * top + (1.0 - high) * (far - top) + one).astype(BF16)
+    return jnp.concatenate([jnp.broadcast_to(rows[ib : ib + 1, :], (LANES, LANES)) for ib in range(nq)], axis=0)
+
+
+def turned_hot(table, origin):
+    size = 4 * LANES
+    hot = (lax.broadcasted_iota(jnp.int32, (LANES, size), 0) == table).astype(F32).astype(BF16)
+    at = lax.broadcasted_iota(jnp.int32, (size, size), 0) + lax.broadcasted_iota(jnp.int32, (size, size), 1)
+    turn = ((at == origin) | (at == origin + size)).astype(F32).astype(BF16)
+    return mm(hot, turn).astype(BF16)
+
+
+def key_aug(half, length, tokens):
+    row = lax.broadcasted_iota(jnp.int32, (2 * tokens, LANES), 0)
+    lane = lax.broadcasted_iota(jnp.int32, (2 * tokens, LANES), 1) % HDIM
+    position = jnp.where(row < tokens, half * tokens + row, row - half * tokens)
+    blocks = 2 * tokens // LANES
+    hot = (lane >= 8) & (lane < 8 + 2 * blocks) & ((lane - 8) % blocks == row // LANES)
+    masked = (lane == 3) & (position >= length)
+    return jnp.where(masked, NEG, hot.astype(F32)).astype(BF16)
 
 
 def peer(index, stride):
@@ -122,11 +153,16 @@
         self.dp_d = peer(self.dp_x, 4)
         self.at_x, self.at_y, self.at_s = (self.dp_x, self.mp), (self.dp_y, self.mp), (self.dp_s, self.mp)
         z1, z2 = peer(self.mp, 1), peer(self.mp, 2)
+        self.half = self.mp % 2
+        self.first = (1 - self.half).astype(F32)
         self.at_z = (None, (self.dp, z1), (self.dp, z2), (self.dp, peer(z1, 2)))
 
-    def meet(self):
+    def column(self, s):
+        return (self.mp + s) % 2 + 2 * ((self.mp // 2 + s // 2) % 2)
+
+    def meet(self, more=()):
         barrier = pltpu.get_barrier_semaphore()
-        others = (self.at_x, self.at_y, self.at_s) + self.at_z[1:]
+        others = (self.at_x, self.at_y, self.at_s) + self.at_z[1:] + tuple(more)
         for other in others:
             pl.semaphore_signal(barrier, inc=1, device_id=other, device_id_type=MESH)
         pl.semaphore_wait(barrier, len(others))
@@ -238,23 +274,23 @@
 
 
 UNITS = ((0, 0), (0, 1), (0, 2), (1, 0), (2, 0), (0, 3), (1, 1), (2, 1), (1, 2), (2, 2), (1, 3), (2, 3))
-GATHER_AHEAD = (0x10, 0x11, 0x20, 0x12, 0x30, 0x21, 0x13, 0x40, 0x31, 0x22, 0x14, 0x41, 0x32)
+GATHER_AHEAD = (0x11, 0x20, 0x12, 0x30, 0x21, 0x13, 0x40, 0x31, 0x22, 0x14, 0x41, 0x32, 0x23, 0x42)
 GATHER_PLAN = {
-    ("attend", 0): {0: (0x23, 0x15, 0x42), 2: (0x33,)},
-    ("attend", 1): {0: (0x24, 0x16), 1: (0x43,), 2: (0x34,)},
-    ("attend", 2): {0: (0x25, 0x17), 1: (0x44,), 2: (0x35,), 3: (0x45,)},
-    ("attend", 3): {0: (0x26, 0x18), 1: (0x36,), 2: (0x27, 0x19)},
-    ("feed", 0): {0: (0x46,), 1: (0x37,), 2: (0x28, 0x1a, 0x47)},
-    ("feed", 1): {1: (0x38,), 2: (0x29, 0x1b, 0x48)},
-    ("feed", 2): {0: (0x39, 0x49), 1: (0x2a,), 2: (0x3a, 0x2b)},
-    ("feed", 3): {0: (0x4a, 0x3b, 0x4b)},
+    ("attend", 0): {0: (0x33,), 1: (0x24,), 2: (0x15, 0x43)},
+    ("attend", 1): {0: (0x34,), 1: (0x16, 0x25), 2: (0x44,)},
+    ("attend", 2): {0: (0x17, 0x35), 1: (0x26,), 2: (0x18,), 3: (0x45,)},
+    ("attend", 3): {0: (0x36,), 1: (0x19, 0x27), 2: (0x46,), 3: (0x1a, 0x37)},
+    ("feed", 0): {0: (0x28,), 1: (0x47,), 2: (0x1b, 0x38)},
+    ("feed", 1): {0: (0x29,), 1: (0x48,), 2: (0x39,)},
+    ("feed", 2): {0: (0x49, 0x2a), 1: (0x3a,), 2: (0x2b, 0x4a)},
+    ("feed", 3): {0: (0x3b, 0x4b)},
 }
 
 
 def front_kernel(
-    x_ref, shard_ref, line_ref, qaug_ref, kaug_ref, gain_ref, hidden_hbm, grad_hbm,
-    own_hbm, oth_hbm, ctx_hbm, lse_ref, wa_hbm, xo_hbm, out_ref, back_ref, gain_grad_ref, gi_hbm, go_hbm,
-    w, xo, own, oth, ctx, s_ref, e_ref, middle, grad, x2_ref, x2t_ref, ob_ref, obt_ref, acc_out, acc_two, gi, go,
+    lengths_ref, attn_ref, wout_ref, inner_ref, outer_ref, table_ref, rel_ref, gain_ref, hidden_hbm, grad_hbm,
+    own_hbm, oth_hbm, ctx_hbm, lse_ref, wa_hbm, x_hbm, xo_hbm, line_ref, out_ref, back_ref, gain_grad_ref, gi_hbm, go_hbm,
+    w, x_ref, xo, own, oth, ctx, s_ref, e_ref, middle, grad, x2_ref, x2t_ref, ob_ref, obt_ref, acc_out, acc_two, gi, go, kaug_ref,
     send, recv, zsend, zrecv, xsem, lsem, osem, gsem,
 ):
     tokens = x_ref.shape[0]
@@ -264,27 +300,41 @@
     get_hidden = pltpu.make_async_copy(hidden_hbm, middle, lsem.at[0])
     get_grad = pltpu.make_async_copy(grad_hbm, grad, lsem.at[1])
     get_hidden.start()
+    def own_block(group):
+        return (group, 0, pl.ds(pl.multiple_of(links.dp * net.rows, 16), net.rows), slice(None))
+
+    parts = [attn_ref[n].astype(BF16) for n in range(3)] + [wout_ref[...].T.astype(BF16)]
+    q, k, v, o = [(part[:, :LANES], part[:, LANES:]) for part in parts]
+    w[own_block(0)] = jnp.concatenate([q[0], k[0], v[0], o[0], q[1], v[1], k[1], o[1]], axis=1)
+    w[own_block(1)] = inner_ref[...].astype(BF16)
+    w[own_block(2)] = outer_ref[...].astype(BF16)
     get_grad.start()
-    place = [pltpu.make_async_copy(shard_ref.at[g], net.block((g, 0), links.dp), lsem.at[2 + g]) for g in range(3)]
-    for copy in place:
-        copy.start()
     links.meet()
-    for copy in place:
-        copy.wait()
+    net.z_copy(0, 1).start()
+    net.s1(UNITS[0])
+    get_hidden.wait()
+    x_ref[...] = rms_scaled(middle[...], gain_ref[0:1, :]).astype(BF16)
     xcopy = remote(x_ref, xo, xsem.at[0], xsem.at[1], links.at_z[1])
-    net.z_copy(0, 1).start()
     net.z_copy(0, 2).start()
     xcopy.start()
     net.z_copy(0, 3).start()
     for step in (1, 2, 3):
         net.z_copy(1, step).start()
         net.z_copy(2, step).start()
-    net.run(GATHER_AHEAD)
+    hot = turned_hot(table_ref[...], 2 * LANES - 1)[: rel_ref.shape[1]]
+    high = rel_ref[...].astype(BF16)
+    rest = rel_ref[...] - high.astype(F32)
+    mid = rest.astype(BF16)
+    low = (rest - mid.astype(F32)).astype(BF16)
+    line_ref[...] = mm(high, hot) + (mm(mid, hot) + mm(low, hot))
+    kaug_ref[...] = key_aug(links.half, lengths_ref[links.mp // 2], tokens)
+    far = far_masks(links.first, nq)
+    net.run(GATHER_AHEAD[:8])
     get_grad.wait()
     ob = grad[...].astype(BF16)
     ob_ref[...] = ob
     obt_ref[...] = ob.T
-    get_hidden.wait()
+    net.run(GATHER_AHEAD[8:])
     xcopy.wait_recv()
 
     masks = [half_rows(0), half_rows(1)]
@@ -304,19 +354,19 @@
         cols_own = {0: p_a[:, :LANES], 1: p_a[:, LANES : 2 * LANES], 2: p_a[:, 2 * LANES :], 4: p_b[:, :LANES], 5: p_b[:, LANES:]}
         cols_oth = {1: o_a[:, :LANES], 2: o_a[:, LANES:], 4: o_b[:, :LANES], 5: o_b[:, LANES:]}
         both = {c: jnp.concatenate([cols_own[c], cols_oth[c]], axis=0) for c in (1, 2, 4, 5)}
-        flags = (line_ref[s, 3:4, :LANES], line_ref[s, 4:5, :LANES])
+        m = links.column(s)
         v_t = {2: both[2].T, 4: both[4].T}
         pieces = []
         stats = []
         for i, (qc, qh, kc, vc, vh) in enumerate(HEAD_AT):
             net.at("attend", s, i)
-            line = line_ref[s, i : i + 1, :]
+            line = line_ref[pl.ds(3 * m + i, 1), :]
             tile = bias_tile(line)
-            qa = cols_own[qc] * masks[qh] + query_aug(qaug_ref[s], i, nq) * masks[1 - qh]
+            qa = cols_own[qc] * masks[qh] + query_aug(line, far, nq) * masks[1 - qh]
             ka = both[kc] * masks[qh] + kaug_ref[...] * masks[1 - qh]
             scores = mt(ka, qa)
             peak = None
-            for jb, row in enumerate(add_bias(scores, tile, line, flags, nq)):
+            for jb, row in enumerate(add_bias(scores, tile, line, links.first, nq)):
                 s_ref[i % 2, jb * LANES : (jb + 1) * LANES, :] = row
                 top = jnp.max(row.reshape(LANES // 8, 8, tokens), axis=0)
                 peak = top if peak is None else jnp.maximum(peak, top)
@@ -347,7 +397,7 @@
     lax.fori_loop(0, 4, attend, 0)
     saves = [
         pltpu.make_async_copy(a, b, osem.at[n])
-        for n, (a, b) in enumerate(((own, own_hbm), (oth, oth_hbm), (ctx, ctx_hbm), (w.at[0], wa_hbm), (xo, xo_hbm)))
+        for n, (a, b) in enumerate(((own, own_hbm), (oth, oth_hbm), (ctx, ctx_hbm), (w.at[0], wa_hbm), (xo, xo_hbm), (x_ref, x_hbm)))
     ]
     for copy in saves:
         copy.start()
@@ -449,18 +499,19 @@
     def s2(self, u):
         self.local(u).wait()
         self.outgoing(u, 0).wait_recv()
-        for chip in range(4):
-            self.sums[u, chip] = (self.sums[u, chip].astype(F32) + self.piece[u % 3, chip].astype(F32)).astype(BF16)
+        far = self.chips[3]
+        self.sums[u, far] = self.sums[u, far] + self.piece[u % 3, far]
         self.outgoing(u, 1).start()
         self.outgoing(u, 2).start()
+        for chip in self.chips[:3]:
+            self.sums[u, chip] = self.sums[u, chip] + self.piece[u % 3, chip]
 
     def s3(self, u):
         half = self.rows // 2
         self.outgoing(u, 1).wait_recv()
         self.outgoing(u, 2).wait_recv()
         for chip, lo, n in ((self.chips[2], 0, 0), (self.chips[1], half, 1)):
-            part = self.sums[u, chip, lo : lo + half].astype(F32) + self.diag[u, n].astype(F32)
-            self.sums[u, chip, lo : lo + half] = part.astype(BF16)
+            self.sums[u, chip, lo : lo + half] = self.sums[u, chip, lo : lo + half] + self.diag[u, n]
         self.outgoing(u, 3).start()
         self.outgoing(u, 4).start()
 
@@ -502,30 +553,39 @@
 
 
 BACK_UNITS = ((1, 3), (2, 3), (1, 2), (2, 2), (1, 1), (2, 1), (1, 0), (2, 0), (0, 3), (0, 2), (0, 1), (0, 0))
+SCATTER_AHEAD = ((0x10, 0x11, 0x12), (0x20,), (0x21,))
 SCATTER_PLAN = {
-    ("other", 0): {0: (0x30, 0x12), 2: (0x21,)},
-    ("other", 1): {0: (0x31, 0x13), 1: (0x40,), 2: (0x22,)},
-    ("other", 2): {0: (0x32, 0x14), 1: (0x41,), 2: (0x23,)},
-    ("other", 3): {0: (0x33, 0x15), 1: (0x42,), 2: (0x24,)},
-    ("own", 0): {0: (0x34, 0x16), 1: (0x43,), 2: (0x25,)},
-    ("own", 1): {0: (0x35, 0x17), 1: (0x44,), 2: (0x26,)},
-    ("own", 2): {0: (0x36, 0x18), 1: (0x45,), 2: (0x27,)},
-    ("own", 3): {0: (0x37, 0x19), 1: (0x46,), 2: (0x28,)},
+    ("other", 0): {0: (0x30, 0x22, 0x13), 2: (0x31, 0x23, 0x14, 0x40)},
+    ("other", 1): {1: (0x32, 0x24, 0x15, 0x41)},
+    ("other", 2): {1: (0x33, 0x25, 0x16, 0x42)},
+    ("other", 3): {0: (0x34, 0x26, 0x17, 0x43)},
+    ("own", 0): {0: (0x35, 0x27, 0x44), 2: (0x36, 0x45), 3: (0x18,)},
+    ("own", 1): {0: (0x37, 0x46), 1: (0x28,), 2: (0x47,), 3: (0x38, 0x19)},
+    ("own", 2): {1: (0x29,), 2: (0x48,), 3: (0x39, 0x1a)},
+    ("own", 3): {1: (0x2a,), 2: (0x49,), 3: (0x3a, 0x1b)},
 }
-SCATTER_AFTER = ((0x1a, 0x1b, 0x38, 0x47, 0x29), (0x39, 0x48, 0x2a, 0x3a, 0x49, 0x2b, 0x3b, 0x4a, 0x4b))
+SCATTER_AFTER = ((0x2b,), (0x4a, 0x3b), (0x4b,))
 
 
 def back_kernel(
-    x_ref, line_ref, qaug_ref, kaug_ref, lse_ref, gain_ref,
+    lengths_ref, x_ref, line_ref, table_ref, lse_ref, gain_ref, gain_two_ref,
     xo_hbm, back_hbm, hidden_hbm, wa_hbm, own_hbm, oth_hbm, ctx_hbm, gi_hbm, go_hbm,
-    grad_ref, gain_grad_ref, line_grad_ref, sums_ref, result_ref,
+    grad_ref, small_ref, result_ref,
     xo, back, hidden, wa, own, oth, ctx, xt, xot, ab_ref, abt, acc_own, acc_oth, oth_out, oth_in,
     dq_acc, d_oth, cb_ref, center_ref, near_ref, ga, sums, piece, diag, side, final,
-    lsem, ssem, osem, send, recv, psem,
+    kaug_ref, line_grad, far_grad, small, small_near, small_z,
+    lsem, ssem, osem, send, recv, psem, tsend, trecv,
 ):
     tokens = x_ref.shape[0]
     nq = tokens // LANES
     links = Links()
+    group = []
+    for n in range(1, 8):
+        dp = links.dp
+        for stride in (1, 2, 4):
+            if n & stride:
+                dp = peer(dp, stride)
+        group.append((dp, links.mp))
     net = Scatter(links, (ga, gi_hbm, go_hbm), sums, piece, diag, side, final, result_ref, send, recv, psem)
     loads = [
         pltpu.make_async_copy(a, b, lsem.at[n])
@@ -546,18 +606,30 @@
         for copy in step_loads(s):
             copy.start()
     loads[2].start()
-    links.meet()
-    net.run((0x10, 0x11))
+    links.meet([group[n] for n in (2, 4, 5, 6)])
+    net.run(SCATTER_AHEAD[0])
     loads[0].wait()
     ab = back[...].astype(BF16)
     ab_ref[...] = ab
     abt[...] = ab.T
-    net.run((0x20,))
+    net.run(SCATTER_AHEAD[1])
     xt[...] = x_ref[...].T
     acc_own[...] = jnp.zeros_like(acc_own)
     acc_oth[...] = jnp.zeros_like(acc_oth)
     loads[1].wait()
     xot[...] = xo[...].T
+    net.run(SCATTER_AHEAD[2])
+    kaug_ref[...] = key_aug(links.half, lengths_ref[links.mp // 2], tokens)
+    far = far_masks(links.first, nq)
+    line_grad[...] = jnp.zeros_like(line_grad)
+    far_grad[...] = jnp.zeros_like(far_grad)
+    jb = lax.broadcasted_iota(jnp.int32, (2 * nq, tokens), 0)
+    ib = lax.broadcasted_iota(jnp.int32, (2 * nq, tokens), 1) // LANES
+    edge_first = ((jb == nq) & (ib == nq - 1)).astype(F32)
+    edge_last = ((jb == 2 * nq - 1) & (ib == 0)).astype(F32)
+    other_key = (jb >= nq).astype(F32)
+    sum_before = ((jb < nq) & (jb < ib - 1)).astype(F32) + (other_key - edge_last) * (1.0 - links.first)
+    sum_after = ((jb < nq) & (jb > ib + 1)).astype(F32) + (other_key - edge_first) * links.first
     masks = [half_rows(0), half_rows(1)]
     own_at = {c: slice(at * LANES, (at + 1) * LANES) for at, c in enumerate((0, 1, 2, 4, 5))}
     oth_at = {c: slice(at * LANES, (at + 1) * LANES) for at, c in enumerate((1, 2, 4, 5))}
@@ -567,16 +639,15 @@
 
     def one_side(s, i, other):
         qc, qh, kc, vc, vh = HEAD_AT[i]
-        line = line_ref[s, i : i + 1, :]
+        line = line_ref[pl.ds(3 * links.column(s) + i, 1), :]
         tile = bias_tile(line)
         qm = own[s, :, own_at[qc]] * masks[qh]
-        qa = qm + query_aug(qaug_ref[s], i, nq) * masks[1 - qh]
+        qa = qm + query_aug(line, far, nq) * masks[1 - qh]
         om = cb_ref[s, :, cb_at[vc]] * masks[vh]
         center = center_ref[s, i : i + 1, :]
         lse = lse_ref[s, i : i + 1, :]
-        flags = (line_ref[s, 3:4, :LANES], line_ref[s, 4:5, :LANES])
         parts = near_parts(tile)
-        corner = corner_parts(tile, line, flags)
+        corner = corner_parts(tile, line, links.first)
         side = 1 if other else 0
         k_cols = oth[s, :, oth_at[kc]] if other else own[s, :, own_at[kc]]
         v_cols = oth[s, :, oth_at[vc]] if other else own[s, :, own_at[vc]]
@@ -651,6 +722,7 @@
 
     def own_side(it, carry):
         s = 3 - it
+        m = links.column(s)
         dk, dv, dq = {}, {}, []
         for i, (qc, qh, kc, vc, vh) in enumerate(HEAD_AT):
             net.at("own", it, i)
@@ -659,25 +731,18 @@
             dk[kc] = dk[kc] + part_k if kc in dk else part_k
             dv[vc] = dv[vc] + part_v if vc in dv else part_v
             at = HDIM if qh == 0 else 0
-            sums_ref[s, i * 8 : (i + 1) * 8, :] = part_q[at + 8 : at + 16, :]
+            block_sums = part_q[at + 8 : at + 8 + 2 * nq, :]
+            head = pl.ds(3 * m + i, 1)
+            far_grad[0, head, :] = jnp.sum(block_sums * sum_before, axis=0, keepdims=True)
+            far_grad[1, head, :] = jnp.sum(block_sums * sum_after, axis=0, keepdims=True)
             dq.append(part_q[:HDIM] if qh == 0 else part_q[HDIM:])
-            flags = (line_ref[s, 3:4, :LANES], line_ref[s, 4:5, :LANES])
-            first, final_corner = near_ref[s, i, 0] * flags[0], near_ref[s, i, 1] * flags[1]
+            first, final_corner = near_ref[s, i, 0] * links.first, near_ref[s, i, 1] * (1.0 - links.first)
             blank = jnp.zeros((LANES, LANES), F32)
             tile = jnp.concatenate([near[1], near[0] + final_corner, blank, near[2] + first], axis=1)
             high = tile.astype(BF16)
             low = (tile - high.astype(F32)).astype(BF16)
             turned = pltpu.roll(mm(mirror, high) + mm(mirror, low), 0, 1, stride=1, stride_axis=0)
-            line_grad_ref[s, i : i + 1, :] = jnp.sum(turned, axis=0, keepdims=True)
-            line_grad_ref[s, 3 + i : 4 + i, :] = jnp.concatenate(
-                [
-                    jnp.sum(first, axis=0, keepdims=True),
-                    jnp.sum(final_corner, axis=0, keepdims=True),
-                    jnp.zeros((1, 2 * LANES), F32),
-                ],
-                axis=1,
-            )
-        line_grad_ref[s, 6:8, :] = jnp.zeros((2, 4 * LANES), F32)
+            line_grad[head, :] = jnp.sum(turned, axis=0, keepdims=True)
         dq_a = jnp.concatenate([dq[0], dq[1]], axis=0).T
         dq_b = jnp.concatenate([dq[2], jnp.zeros_like(dq[2])], axis=0).T
         d_own = jnp.concatenate([dq_a, dk[1], dv[2], dq_b + dv[4], dk[5]], axis=1).astype(BF16)
@@ -695,6 +760,7 @@
         rows = ga.shape[3]
         for n in range(8):
             ga[s, n // 2, n % 2] = g[n * rows : (n + 1) * rows, :]
+        net.at("own", it, 3)
         acc_own[...] += mt(d_own[:, : 3 * LANES], wa[s, :, : 3 * LANES]) + mt(d_own[:, 3 * LANES :], wa[s, :, 4 * LANES :])
         return carry
 
@@ -705,73 +771,123 @@
     one_back = acc_own[...] + oth_in[...].astype(F32)
     grad, gain_part = rms_back(hidden[...], gain_ref[0:1, :], one_back)
     grad_ref[...] = grad + back[...]
-    gain_grad_ref[...] = jnp.broadcast_to(gain_part, gain_grad_ref.shape)
     net.run(SCATTER_AFTER[1])
-    for group in (1, 2, 0):
-        net.last(group)
+    lane = lax.broadcasted_iota(jnp.int32, (16, 4 * LANES), 1)
+    by_line = (
+        line_grad[...]
+        + jnp.sum(far_grad[0], axis=1, keepdims=True) * (lane == 2 * LANES - 1).astype(F32)
+        + jnp.sum(far_grad[1], axis=1, keepdims=True) * (lane == 4 * LANES - 1).astype(F32)
+    )
+    high = by_line.astype(BF16)
+    low = (by_line - high.astype(F32)).astype(BF16)
+    hot = turned_hot(table_ref[...], 3 * LANES - 2)
+    small[0:16, :] = mt(high, hot) + mt(low, hot)
+    for n in range(6):
+        at = slice(n * LANES, (n + 1) * LANES)
+        small[16 + n : 17 + n, :] = gain_part[:, at]
+        small[22 + n : 23 + n, :] = gain_two_ref[0:1, at]
+    net.run(SCATTER_AFTER[2])
+    squares = jnp.zeros((8, LANES), F32)
+    for weight in (1, 2, 0):
+        net.last(weight)
+        value = result_ref[weight]
+        value = value * value
+        for n in range(value.shape[1] // LANES):
+            piece_sum = value[:, n * LANES : (n + 1) * LANES]
+            squares = squares + jnp.sum(piece_sum.reshape(-1, 8, LANES), axis=0)
+    small[28:32, :] = squares[0:4] + squares[4:8]
+    near = [remote(small, small_near.at[n], tsend.at[n], trecv.at[n], to) for n, to in enumerate(group)]
+    for copy in near:
+        copy.start()
+    for copy in near:
+        copy.wait_recv()
+    total = small[...]
+    for n in range(7):
+        total = total + small_near[n]
+    small_z[0] = total
+    along = [remote(small_z.at[0], small_z.at[n], tsend.at[6 + n], trecv.at[6 + n], links.at_z[n]) for n in (1, 2, 3)]
+    for copy in along:
+        copy.start()
+    for copy in along:
+        copy.wait_recv()
+    small_ref[...] = (small_z[0] + small_z[1]) + (small_z[2] + small_z[3])
+    for copy in near + along:
+        copy.wait_send()
     swap.wait_send()
     net.finish()
 
 
-def sum_kernel(x_ref, out_ref, held, other, send, recv):
-    links = Links()
-    near = []
-    for k in range(1, 8):
-        dp = links.dp
-        for stride in (1, 2, 4):
-            if k & stride:
-                dp = peer(dp, stride)
-        near.append((dp, links.mp))
-    barrier = pltpu.get_barrier_semaphore()
-    everyone = near + list(links.at_z[1:])
-    for to in everyone:
-        pl.semaphore_signal(barrier, inc=1, device_id=to, device_id_type=MESH)
-    pl.semaphore_wait(barrier, len(everyone))
-    first = [remote(x_ref, held.at[n], send.at[n], recv.at[n], to) for n, to in enumerate(near)]
-    for copy in first:
+def update_kernel(small_ref, grad_hbm, block_hbm, input_hbm, *refs):
+    hbm, (block_out, input_out, norm_ref), new = refs[:18], refs[18:21], refs[21:39]
+    held, grad_ref, pass_ref, sem = refs[39:57], refs[57], refs[58], refs[59]
+    through = ((block_hbm, block_out), (input_hbm, input_out))
+    fetch = [pltpu.make_async_copy(a, pass_ref.at[n], sem.at[n]) for n, (a, b) in enumerate(through)]
+    store = [pltpu.make_async_copy(pass_ref.at[n], b, sem.at[21 + n]) for n, (a, b) in enumerate(through)]
+    loads = [pltpu.make_async_copy(a, b, sem.at[2 + n]) for n, (a, b) in enumerate(zip(hbm, held))]
+    loads.append(pltpu.make_async_copy(grad_hbm, grad_ref, sem.at[20]))
+    for copy in loads[::-1] + fetch:
         copy.start()
-    total = x_ref[...]
-    for copy in first:
-        copy.wait_recv()
-    for n in range(7):
-        total = total + held[n]
-    other[0] = total
-    second = [
-        remote(other.at[0], other.at[n], send.at[6 + n], recv.at[6 + n], links.at_z[n]) for n in (1, 2, 3)
-    ]
-    for copy in second:
-        copy.start()
-    for copy in second:
-        copy.wait_recv()
-    out_ref[...] = (other[0] + other[1]) + (other[2] + other[3])
-    for copy in first + second:
-        copy.wait_send()
-
-
-def sum_all(x):
-    dma = pltpu.SemaphoreType.DMA
-    vmem = pl.BlockSpec(memory_space=pltpu.VMEM)
-    return pl.pallas_call(
-        sum_kernel,
-        in_specs=[vmem],
-        out_specs=vmem,
-        out_shape=jax.ShapeDtypeStruct(x.shape, F32),
-        scratch_shapes=[pltpu.VMEM((7, *x.shape), F32), pltpu.VMEM((4, *x.shape), F32), dma((10,)), dma((10,))],
-        compiler_params=pltpu.CompilerParams(collective_id=2, has_side_effects=True),
-        name="finish_sums",
-    )(x)
-
-
-def run_front(x, shard, line, qaug, kaug, gains, hidden, grad):
-    t, d = x.shape
-    parts, cols = line.shape[0], shard.shape[2]
+    attn, out, inner, outer, rel, gain, attn_first, attn_second, out_first, out_second = held[:10]
+    inner_first, inner_second, outer_first, outer_second, rel_first, rel_second, gain_first, gain_second = held[10:]
+    small = small_ref[0:28, :]
+    squares = jnp.sum(small * small, axis=0, keepdims=True) + jnp.sum(small_ref[28:32, :], axis=0, keepdims=True)
+    norm = jnp.sqrt(jnp.sum(squares, axis=1, keepdims=True))
+    norm_ref[...] = norm
+    factor = jnp.minimum(1.0, CLIP / (norm + 1e-06))
+    for copy in loads:
+        copy.wait()
+    for a, b in zip(fetch, store):
+        a.wait()
+        b.start()
+
+    def step(at, grad, rate, master, first, second, outs):
+        for ref, value in zip(outs, adam_step(master[at], grad, first[at], second[at], factor, rate)):
+            ref[at] = value
+
+    def turned(column):
+        return pltpu.roll(column, HDIM, 1)[:, :HDIM]
+
+    g = [grad_ref[0, :, n * LANES : (n + 1) * LANES] for n in range(6)]
+    tails = (g[4][:, :HDIM], g[5][:, :HDIM], turned(g[4]))
+    for n in range(3):
+        step((n, slice(None), slice(0, LANES)), g[n], RATE_MATRIX, attn, attn_first, attn_second, new[0:3])
+        step((n, slice(None), slice(LANES, LANES + HDIM)), tails[n], RATE_MATRIX, attn, attn_first, attn_second, new[0:3])
+    rows = g[3].shape[0]
+    blank = jnp.zeros((LANES - rows, LANES), F32)
+    lower = pltpu.roll(g[5], HDIM, 1)
+    whole = slice(None)
+    step((slice(0, LANES), whole), jnp.concatenate([g[3], blank], axis=0).T[:, :rows], RATE_OUT, out, out_first, out_second, new[3:6])
+    step(
+        (slice(LANES, LANES + HDIM), whole),
+        jnp.concatenate([lower, blank], axis=0).T[:HDIM, :rows],
+        RATE_OUT, out, out_first, out_second, new[3:6],
+    )
+    step(whole, grad_ref[1], RATE_MATRIX, inner, inner_first, inner_second, new[6:9])
+    step(whole, grad_ref[2], RATE_MATRIX, outer, outer_first, outer_second, new[9:12])
+    heads, buckets = rel.shape
+    step(whole, small_ref[0:heads, 0:buckets], RATE_SMALL, rel, rel_first, rel_second, new[12:15])
+    gain_grad = jnp.concatenate(
+        [
+            jnp.concatenate([small_ref[at + n : at + n + 1, :] for n in range(6)], axis=1)
+            for at in (16, 22)
+        ],
+        axis=0,
+    )
+    step(whole, gain_grad, RATE_SMALL, gain, gain_first, gain_second, new[15:18])
+    for copy in store:
+        copy.wait()
+
+
+def run_front(lengths, attn, out, inner, outer, table, rel, gains, hidden, grad):
+    t, d = hidden.shape
+    parts, cols = rel.shape[0] // 3, inner.shape[1]
     any_space = pl.BlockSpec(memory_space=pl.ANY)
     vmem = pl.BlockSpec(memory_space=pltpu.VMEM)
     dma = pltpu.SemaphoreType.DMA
     return pl.pallas_call(
         front_kernel,
-        in_specs=[vmem] * 6 + [any_space] * 2,
-        out_specs=[any_space] * 3 + [vmem] + [any_space] * 2 + [vmem] * 3 + [any_space] * 2,
+        in_specs=[pl.BlockSpec(memory_space=pltpu.SMEM)] + [vmem] * 7 + [any_space] * 2,
+        out_specs=[any_space] * 3 + [vmem] + [any_space] * 3 + [vmem] * 4 + [any_space] * 2,
         out_shape=[
             jax.ShapeDtypeStruct((parts, t, 5 * LANES), BF16),
             jax.ShapeDtypeStruct((parts, t, 4 * LANES), BF16),
@@ -779,6 +895,8 @@
             jax.ShapeDtypeStruct((parts, 8, t), F32),
             jax.ShapeDtypeStruct((parts, d, cols), BF16),
             jax.ShapeDtypeStruct((t, d), BF16),
+            jax.ShapeDtypeStruct((t, d), BF16),
+            jax.ShapeDtypeStruct((rel.shape[0], 4 * LANES), F32),
             jax.ShapeDtypeStruct((t, d), F32),
             jax.ShapeDtypeStruct((t, d), F32),
             jax.ShapeDtypeStruct((8, d), F32),
@@ -787,6 +905,7 @@
         ],
         scratch_shapes=[
             pltpu.VMEM((3, parts, d, cols), BF16),
+            pltpu.VMEM((t, d), BF16),
             pltpu.VMEM((t, d), BF16),
             pltpu.VMEM((parts, t, 5 * LANES), BF16),
             pltpu.VMEM((parts, t, 4 * LANES), BF16),
@@ -799,16 +918,17 @@
             pltpu.VMEM((t, d), BF16), pltpu.VMEM((d, t), BF16),
             pltpu.VMEM((t, d), F32), pltpu.VMEM((t, d), F32),
             pltpu.VMEM((2, d, cols), BF16), pltpu.VMEM((2, d, cols), BF16),
-            dma((12, 8)), dma((12, 8)), dma((9,)), dma((9,)), dma((2,)), dma((5,)), dma((5,)), dma((2, 2)),
+            pltpu.VMEM((2 * t, LANES), BF16),
+            dma((12, 8)), dma((12, 8)), dma((9,)), dma((9,)), dma((2,)), dma((2,)), dma((6,)), dma((2, 2)),
         ],
         compiler_params=pltpu.CompilerParams(
             vmem_limit_bytes=62 * 2**20, collective_id=0, has_side_effects=True
         ),
         name="front",
-    )(x, shard, line, qaug, kaug, gains, hidden, grad)
-
-
-def run_back(x, xo, back, hidden, wa, line, qaug, kaug, own, oth, ctx, lse, gi, go, gains):
+    )(lengths, attn, out, inner, outer, table, rel, gains, hidden, grad)
+
+
+def run_back(lengths, x, line, table, lse, gains, gain_two, xo, back, hidden, wa, own, oth, ctx, gi, go):
     t, d = x.shape
     parts, cols = wa.shape[0], wa.shape[2]
     rows = d // 8
@@ -818,13 +938,11 @@
     split = (parts, 4, 2, rows, cols)
     return pl.pallas_call(
         back_kernel,
-        in_specs=[vmem] * 6 + [any_space] * 9,
-        out_specs=[vmem] * 5,
+        in_specs=[pl.BlockSpec(memory_space=pltpu.SMEM)] + [vmem] * 6 + [any_space] * 9,
+        out_specs=[vmem] * 3,
         out_shape=[
             jax.ShapeDtypeStruct((t, d), F32),
-            jax.ShapeDtypeStruct((8, d), F32),
-            jax.ShapeDtypeStruct((parts, 8, t), F32),
-            jax.ShapeDtypeStruct((parts, 24, t), F32),
+            jax.ShapeDtypeStruct((32, LANES), F32),
             jax.ShapeDtypeStruct((3, rows, cols), F32),
         ],
         scratch_shapes=[
@@ -836,31 +954,32 @@
             pltpu.VMEM((parts, t, 2 * LANES), BF16), pltpu.VMEM((parts, 8, t), F32), pltpu.VMEM((parts, 3, 2, LANES, LANES), F32),
             pltpu.VMEM(split, BF16), pltpu.VMEM((12, 4, rows, cols), BF16), pltpu.VMEM((3, 4, rows, cols), BF16),
             pltpu.VMEM((12, 2, rows // 2, cols), BF16), pltpu.VMEM((12, 2, rows, cols), BF16), pltpu.VMEM((3, 3, rows, cols), BF16),
-            dma((3,)), dma((parts, 4)), dma((2,)), dma((12, 6)), dma((12, 6)), dma((3,)),
+            pltpu.VMEM((2 * t, LANES), BF16), pltpu.VMEM((16, 4 * LANES), F32), pltpu.VMEM((2, 16, 4 * LANES), F32),
+            pltpu.VMEM((32, LANES), F32), pltpu.VMEM((7, 32, LANES), F32), pltpu.VMEM((4, 32, LANES), F32),
+            dma((3,)), dma((parts, 4)), dma((2,)), dma((12, 6)), dma((12, 6)), dma((3,)), dma((10,)), dma((10,)),
         ],
         compiler_params=pltpu.CompilerParams(
             vmem_limit_bytes=62 * 2**20, collective_id=1, has_side_effects=True
         ),
         name="back",
-    )(x, line, qaug, kaug, lse, gains, xo, back, hidden, wa, own, oth, ctx, gi.reshape(split), go.reshape(split))
-
-
-def pack_attn(attn, out_t):
-    cut = [[part[:, i * HDIM : (i + 1) * HDIM] for i in range(3)] for part in (attn[0], attn[1], attn[2], out_t)]
-    q, k, v, o = cut
-    return jnp.concatenate([q[0], q[1], k[0], k[1], v[0], v[1], o[0], o[1], q[2], v[2], k[2], o[2]], axis=1)
-
-
-def unpack_attn(block):
-    c = [block[:, i * HDIM : (i + 1) * HDIM] for i in range(12)]
-    attn = jnp.stack(
-        [
-            jnp.concatenate([c[0], c[1], c[8]], axis=1),
-            jnp.concatenate([c[2], c[3], c[10]], axis=1),
-            jnp.concatenate([c[4], c[5], c[9]], axis=1),
-        ]
-    )
-    return attn, jnp.concatenate([c[6], c[7], c[11]], axis=1)
+    )(lengths, x, line, table, lse, gains, gain_two, xo, back, hidden, wa, own, oth, ctx, gi.reshape(split), go.reshape(split))
+
+
+def run_update(small, grads, block_out, input_grad, masters, moments):
+    vmem = pl.BlockSpec(memory_space=pltpu.VMEM)
+    hbm = pl.BlockSpec(memory_space=pltpu.HBM)
+    like = lambda a: jax.ShapeDtypeStruct(a.shape, F32)
+    return pl.pallas_call(
+        update_kernel,
+        in_specs=[vmem] + [hbm] * 21,
+        out_specs=[hbm] * 2 + [vmem] * 19,
+        out_shape=[like(block_out), like(input_grad), jax.ShapeDtypeStruct((1, 1), F32)]
+        + [like(a) for a in masters for _ in range(3)],
+        scratch_shapes=[pltpu.VMEM(a.shape, F32) for a in (*masters, *moments, grads)]
+        + [pltpu.VMEM((2, *block_out.shape), F32), pltpu.SemaphoreType.DMA((23,))],
+        compiler_params=pltpu.CompilerParams(vmem_limit_bytes=62 * 2**20),
+        name="update",
+    )(small, grads, block_out, input_grad, *masters, *moments)
 
 
 def body(
@@ -868,99 +987,58 @@
     attn_first, attn_second, out_first, out_second, inner_first, inner_second, outer_first, outer_second,
     rel_first, rel_second, gain_first, gain_second, *, parts,
 ):
-    tokens = hidden_in.shape[0]
-    nq = tokens // LANES
-    heads = rel_bias.shape[1]
-    per_seq = SEQLEN // tokens
-    mp_index = lax.axis_index("mp")
-    half = mp_index % per_seq
-    length = lengths[mp_index // per_seq]
-
-    shard = [
-        pack_attn(attn_weight.astype(BF16), out_weight.astype(BF16).T),
-        inner_weight.astype(BF16),
-        outer_weight.astype(BF16).T,
-    ]
-    order = jnp.bitwise_xor(mp_index, jnp.arange(parts))
-
-    x1 = rms_scaled(hidden_in, gains[0]).astype(BF16)
-
-    u = jnp.arange(4 * LANES)
-    offset = jnp.where(u < 2 * LANES, -u, 4 * LANES - u)
-    buckets = jnp.arange(rel_bias.shape[0], dtype=jnp.int32)
-    line_hot = (jnp.take(table, offset + SEQLEN - 1)[:, None] == buckets[None, :]).astype(F32)
-    line = jnp.dot(line_hot, rel_bias, precision=lax.Precision.HIGHEST).T.reshape(parts, heads // parts, 4 * LANES)
-    first_flag = (half == 0).astype(F32)
-    flags = jnp.stack([jnp.full((4 * LANES,), first_flag), jnp.full((4 * LANES,), 1.0 - first_flag)])
-    line_in = jnp.concatenate(
-        [line, jnp.broadcast_to(flags[None], (parts, 2, 4 * LANES)), jnp.zeros((parts, 3, 4 * LANES), F32)], axis=1
-    )
-    far_before, far_after = line[:, :, LANES], line[:, :, 3 * LANES]
-    jb, ib = jnp.arange(nq)[None, :], jnp.arange(nq)[:, None]
-    own_before, own_after = (jb < ib - 1).astype(F32), (jb > ib + 1).astype(F32)
-    oth_before = jnp.full((nq, nq), 1.0 - first_flag)
-    w_before = jnp.concatenate([own_before, oth_before], axis=1)
-    w_after = jnp.concatenate([own_after, 1.0 - oth_before], axis=1)
-    far = far_before[:, :, None, None] * w_before + far_after[:, :, None, None] * w_after
-    far_hi = far.astype(BF16).astype(F32)
-    far_lo = far - far_hi
-    one = jnp.ones((parts, heads // parts, nq, 1), F32)
-    blank = jnp.zeros((parts, heads // parts, nq, HDIM), F32)
-    q64 = jnp.concatenate(
-        [blank[..., :3], one, blank[..., :4], far_hi, far_lo, blank[..., : HDIM - 8 - 4 * nq]], axis=-1
-    )
-    qaug = jnp.concatenate([q64, q64], axis=-1).reshape(parts, 3 * nq, LANES)
-    qaug = jnp.pad(qaug, ((0, 0), (0, 16 - 3 * nq), (0, 0))).astype(BF16)
-    row = jnp.arange(2 * tokens)
-    position = jnp.where(row < tokens, half * tokens + row, (1 - half) * tokens + row - tokens)
-    masked = jnp.where(position < length, 0.0, NEG)
-    col = jnp.arange(LANES) % HDIM
-    block_of = row // LANES
-    hot = ((col >= 8) & (col < 8 + 4 * nq))[None, :] & ((col[None, :] - 8) % (2 * nq) == block_of[:, None])
-    kaug = jnp.where((col == 3)[None, :], masked[:, None], hot.astype(F32)).astype(BF16)
-
-    line_in, qaug = jnp.take(line_in, order, axis=0), jnp.take(qaug, order, axis=0)
-    own, oth, ctx, lse, wa, x1o, block_out, middle_back, gain_two, gi, go = run_front(
-        x1, jnp.stack(shard), line_in, qaug, kaug, gains, hidden_in, out_grad
-    )
-    input_grad, gain_one, line_grad, sums, owned = run_back(
-        x1, x1o, middle_back, hidden_in, wa, line_in, qaug, kaug, own, oth, ctx, lse, gi, go, gains
-    )
-
-    line_grad = jnp.take(line_grad, order, axis=0)
-    near_line = jnp.roll(line_grad[:, :3], 1 - LANES, axis=2)
-    sums = jnp.take(sums, order, axis=0)
-    near_grad = jnp.einsum(
-        "ub,hu->bh", line_hot, near_line.reshape(heads, 4 * LANES), precision=lax.Precision.HIGHEST
-    )
-    corner = jnp.sum(line_grad[:, 3:6].reshape(heads, 4, LANES), axis=-1)
-    block_sums = jnp.sum(sums.reshape(heads, 2 * nq, nq, LANES), axis=-1)
-    far_w = jnp.transpose(jnp.stack([w_before, w_after]), (0, 2, 1))
-    far_grad = jnp.einsum("hji,sji->sh", block_sums, far_w, precision=lax.Precision.HIGHEST)
-    far_grad = far_grad - jnp.stack([corner[:, 1], corner[:, 0]])
-    far_hot = (jnp.stack([table[0], table[2 * SEQLEN - 2]])[None, :] == buckets[:, None]).astype(F32)
-    rel_part = near_grad + jnp.dot(far_hot, far_grad, precision=lax.Precision.HIGHEST)
-
-    g_attn, g_out_t = unpack_attn(owned[0])
-    grads = (g_attn, g_out_t.T, owned[1], owned[2].T)
-    square_part = jnp.sum(owned * owned)
-    width = gains.shape[1]
-    small = jnp.concatenate(
-        [gain_one[0], gain_two[0], rel_part.reshape(-1), jnp.full((LANES,), square_part)]
-    ).reshape(-1, LANES)
-    small = sum_all(jnp.pad(small, ((0, -small.shape[0] % 8), (0, 0)))).reshape(-1)
-    gain_grad = small[: 2 * width].reshape(2, width)
-    rel_grad = small[2 * width : 2 * width + rel_bias.size].reshape(rel_bias.shape)
-    square_total = small[2 * width + rel_bias.size]
-    grad_norm = jnp.sqrt(square_total + jnp.sum(gain_grad * gain_grad) + jnp.sum(rel_grad * rel_grad))
-    factor = jnp.minimum(1.0, CLIP / (grad_norm + 1e-06))
-    attn_new = adam_step(attn_weight, grads[0], attn_first, attn_second, factor, RATE_MATRIX)
-    out_new = adam_step(out_weight, grads[1], out_first, out_second, factor, RATE_OUT)
-    inner_new = adam_step(inner_weight, grads[2], inner_first, inner_second, factor, RATE_MATRIX)
-    outer_new = adam_step(outer_weight, grads[3], outer_first, outer_second, factor, RATE_MATRIX)
-    rel_new = adam_step(rel_bias, rel_grad, rel_first, rel_second, factor, RATE_SMALL)
-    gain_new = adam_step(gains, gain_grad, gain_first, gain_second, factor, RATE_SMALL)
-    return (block_out, input_grad, grad_norm, *attn_new, *out_new, *inner_new, *outer_new, *rel_new, *gain_new)
+    near_table = table[SEQLEN - 2 * LANES : SEQLEN + 2 * LANES].reshape(1, 4 * LANES)
+    own, oth, ctx, lse, wa, x1, x1o, line, block_out, middle_back, gain_two, gi, go = run_front(
+        lengths, attn_weight, out_weight, inner_weight, outer_weight.T, near_table, rel_bias.T, gains, hidden_in, out_grad
+    )
+    input_grad, small, owned = run_back(
+        lengths, x1, line, near_table, lse, gains, gain_two, x1o, middle_back, hidden_in, wa, own, oth, ctx, gi, go
+    )
+    new = run_update(
+        small, owned, block_out, input_grad,
+        (attn_weight, out_weight, inner_weight, outer_weight.T, rel_bias.T, gains),
+        (
+            attn_first, attn_second, out_first, out_second, inner_first, inner_second,
+            outer_first.T, outer_second.T, rel_first.T, rel_second.T, gain_first, gain_second,
+        ),
+    )
+    masters = new[3:]
+    return (
+        new[0], new[1], new[2].reshape(()), *masters[:9], *(a.T for a in masters[9:12]), *(a.T for a in masters[12:15]), *masters[15:],
+    )
+
+
+def plain_corner_parts(tile, line, flags):
+    before, same, after = near_parts(tile)
+    first = (after - line[:, 3 * LANES : 3 * LANES + 1]) * flags[0]
+    last = (before - line[:, LANES : LANES + 1]) * flags[1]
+    return first, last
+
+
+def plain_add_bias(scores, tile, line, flags, nq):
+    parts = near_parts(tile)
+    corner = plain_corner_parts(tile, line, flags)
+    rows = []
+    for jb in range(2 * nq):
+        row = []
+        for ib in range(nq):
+            block = scores[jb * LANES : (jb + 1) * LANES, ib * LANES : (ib + 1) * LANES]
+            if jb < nq and abs(jb - ib) <= 1:
+                block = block + parts[jb - ib + 1]
+            elif jb == nq and ib == nq - 1:
+                block = block + corner[0]
+            elif jb == 2 * nq - 1 and ib == 0:
+                block = block + corner[1]
+            row.append(block)
+        rows.append(jnp.concatenate(row, axis=1))
+    return rows
+
+
+def plain_query_aug(qaug, i, nq):
+    rows = qaug.shape[0]
+    return jnp.concatenate(
+        [jnp.broadcast_to(qaug[i * nq + ib : i * nq + ib + 1, :], (LANES, LANES)) for ib in range(nq)], axis=0
+    )
 
 
 def forward_kernel(
@@ -993,11 +1071,11 @@
     for i, (qc, qh, kc, vc, vh) in enumerate(HEAD_AT):
         line = line_ref[0, i : i + 1, :]
         tile = bias_tile(line)
-        qa = cols_own[qc] * masks[qh] + query_aug(qaug_ref[0], i, nq) * masks[1 - qh]
+        qa = cols_own[qc] * masks[qh] + plain_query_aug(qaug_ref[0], i, nq) * masks[1 - qh]
         ka = both[kc] * masks[qh] + kaug_ref[...] * masks[1 - qh]
         scores = mt(ka, qa)
         peak = None
-        for jb, row in enumerate(add_bias(scores, tile, line, flags, nq)):
+        for jb, row in enumerate(plain_add_bias(scores, tile, line, flags, nq)):
             s_ref[i, jb * LANES : (jb + 1) * LANES, :] = row
             top = jnp.max(row.reshape(LANES // 8, 8, tokens), axis=0)
             peak = top if peak is None else jnp.maximum(peak, top)
@@ -1114,7 +1192,7 @@
         line = line_ref[0, i : i + 1, :]
         tile = bias_tile(line)
         qm = own[qc] * masks[qh]
-        qa = qm + query_aug(qaug_ref[0], i, nq) * masks[1 - qh]
+        qa = qm + plain_query_aug(qaug_ref[0], i, nq) * masks[1 - qh]
         om = cb[vc] * masks[vh]
         pick = jnp.broadcast_to(masks[vh], (8, LANES))
         center = (mt(pick, prod_hi[vc]) + mt(pick, prod_lo[vc]))[0:1, :]
@@ -1122,7 +1200,7 @@
         kaug = kaug_ref[...] * masks[1 - qh]
         dqt = None
         parts = near_parts(tile)
-        corner = corner_parts(tile, line, flags)
+        corner = plain_corner_parts(tile, line, flags)
         near = [None, None, None, None, None]
         for side, cols in enumerate((own, oth)):
             ka = cols[kc] * masks[qh] + kaug[side * tokens : (side + 1) * tokens]
@@ -1304,6 +1382,24 @@
     )(x, xo, back, wa, line, qaug, kaug, own, oth, ctx, lse)
 
 
+def pack_attn(attn, out_t):
+    cut = [[part[:, i * HDIM : (i + 1) * HDIM] for i in range(3)] for part in (attn[0], attn[1], attn[2], out_t)]
+    q, k, v, o = cut
+    return jnp.concatenate([q[0], q[1], k[0], k[1], v[0], v[1], o[0], o[1], q[2], v[2], k[2], o[2]], axis=1)
+
+
+def unpack_attn(block):
+    c = [block[:, i * HDIM : (i + 1) * HDIM] for i in range(12)]
+    attn = jnp.stack(
+        [
+            jnp.concatenate([c[0], c[1], c[8]], axis=1),
+            jnp.concatenate([c[2], c[3], c[10]], axis=1),
+            jnp.concatenate([c[4], c[5], c[9]], axis=1),
+        ]
+    )
+    return attn, jnp.concatenate([c[6], c[7], c[11]], axis=1)
+
+
 def general_body(
     hidden_in, out_grad, attn_weight, out_weight, inner_weight, outer_weight, rel_bias, gains, lengths, table,
     attn_first, attn_second, out_first, out_second, inner_first, inner_second, outer_first, outer_second,

time: 243 us -> 198 us (0.81)
  local copies, waits for them, and re-layouts: 20.5 us -> 1.28 us
  other arithmetic: 17.5 us -> 0 us
  between operations: 4.55 us -> 0.86 us
  Pallas kernels: 199 us -> 196 us
    gather x5 -> x0, local copies, waits for them, and re-layouts: 7.51 us -> none  [the longest x1 3.43 us: body(): jnp.take(table, offset + SEQLEN - 1)[:, None] == buckets[None, :]]
    unnamed x60 -> x0, local copies, waits for them, and re-layouts: 5.9 us -> none
    sub x7 -> x0, other arithmetic: 4.52 us -> none  [the longest x6 4.51 us: adam_step(): master - rate * (first_hat / (jnp.sqrt(second_hat) + ADAM_EPS) + DECAY *...]
    reduce_sum x6 -> x0, other arithmetic: 3.89 us -> none  [the longest x1 1.3 us: body(): jnp.sum(gain_grad * gain_grad)]
    pallas_call x3, Pallas kernels: 199 us -> 196 us  [the longest x1 101 us: run_front(): pl.pallas_call(front_kernel, in_specs=[pl.BlockSpec(memory_space=pltpu.SM...]
    slice x23 -> x1, local copies, waits for them, and re-layouts: 4.54 us -> 1.28 us  [body(): table[SEQLEN - 2 * LANES:SEQLEN + 2 * LANES].reshape(1, 4 * LANES)]
where the time goes in v3:
time: 198 us
  Pallas kernels  196 us (99%)
    pallas_call x1, Pallas kernels, run_front(): pl.pallas_call(front_kernel, in_specs=[pl.BlockSpec(memory_space=pltpu.SM...  101 us
    pallas_call x1, Pallas kernels, run_back(): pl.pallas_call(back_kernel, in_specs=[pl.BlockSpec(memory_space=pltpu.SME...  88 us
    pallas_call x1, Pallas kernels, run_update(): pl.pallas_call(update_kernel, in_specs=[vmem] + [hbm] * 21, out_specs=[hb...  7.16 us

profile of v3, /device:TPU:0, one launch (start us, length us, event | category | flops | bytes accessed | tf_op | source)
XLA Modules:
  0.0 197.8 jit_solution(1865794302067559624)
XLA Ops:
  0.7 1.3 slice.3
  1.9 100.6 %front.1 = (bf16[4,512,640]{2,1,0:T(8,128)(2,1)}, bf16[4,512,512]{2,1,0:T(8,128)(2,1)}, bf16[4,512,256]{2,1,0:T(8,128)(2,1)}, f32[4,8,512]{2,1,0:T(8,128)}, bf16...) custom-call(s32[2]{0:T(128)} %lengths_ref.3, ...), custom_call_target="tpu_custom_call" | custom-call | tf_op jit(solution)/shard_map/front/pallas_call | solution.py:887
  102.5 88.0 %back.1 = (f32[512,768]{1,0:T(8,128)}, f32[32,128]{1,0:T(8,128)}, f32[3,96,768]{2,1,0:T(8,128)}) custom-call(s32[2]{0:T(128)} %lengths_ref.3, bf16[512,768]{1,0:T(8,128)(2,1)} %get-tuple-element.58.x_ref, f32[12,512]{1,0:T(8,128)} %get-tuple-element.59.line_ref, s32[1,512]{1,0:T(1,128)} %bitcast.25, f32[4,8,512]{2,1,0:T(8,128)} %get-tuple-element.60.lse_ref, ...), custom_call_target="tpu_custom_call" | custom-call | tf_op jit(solution)/shard_map/back/pallas_call | solution.py:939
  190.5 7.2 %update.1 = (f32[512,768]{1,0:T(8,128)}, f32[512,768]{1,0:T(8,128)}, f32[1,1]{1,0:T(1,128)}, f32[3,96,192]{2,1,0:T(8,128)}, f32[3,96,192]{2,1,0:T(8,128)}, /*ind...) custom-call(f32[32,128]{1,0:T(8,128)} %get-tuple-element.70.small_re, ...), custom_call_target="tpu_custom_call" | custom-call | tf_op jit(solution)/shard_map/update/pallas_call | solution.py:972

commit v4 on v3

--- a/solution.py
+++ b/solution.py
@@ -177,12 +177,11 @@
 class Gather:
     def __init__(self, links, w, send, recv, zsend, zrecv):
         self.k, self.w, self.send, self.recv, self.zsend, self.zrecv = links, w, send, recv, zsend, zrecv
-        self.rows = w.shape[2] // 8
+        self.rows = w.shape[3]
 
     def block(self, unit, dp, lo=0, n=None):
         group, s = unit
-        n = self.rows if n is None else n
-        return self.w.at[group, s, pl.ds(pl.multiple_of(dp * self.rows + lo, 16), n), :]
+        return self.w.at[group, s, dp] if n is None else self.w.at[group, s, dp, pl.ds(lo, n)]
 
     def copy(self, unit, kind, ref, to):
         at = unit[0] * 4 + unit[1]
@@ -268,40 +267,178 @@
             return carry
 
         lax.fori_loop(0, 12, each, 0)
-        for group in range(3):
+        for group in (1, 2):
             for s in (1, 2, 3):
                 self.z_copy(group, s).wait_send()
 
 
-UNITS = ((0, 0), (0, 1), (0, 2), (1, 0), (2, 0), (0, 3), (1, 1), (2, 1), (1, 2), (2, 2), (1, 3), (2, 3))
-GATHER_AHEAD = (0x11, 0x20, 0x12, 0x30, 0x21, 0x13, 0x40, 0x31, 0x22, 0x14, 0x41, 0x32, 0x23, 0x42)
+UNITS = ((0, 0), (1, 0), (2, 0), (0, 1), (0, 2), (0, 3), (1, 1), (2, 1), (1, 2), (2, 2), (1, 3), (2, 3))
+GATHER_AHEAD = (
+    (0x11, 0x12, 0x20, 0x13, 0x30),
+    (0x21, 0x14, 0x40, 0x31, 0x22, 0x15, 0x41, 0x32, 0x23, 0x42, 0x33, 0x24, 0x43),
+)
 GATHER_PLAN = {
-    ("attend", 0): {0: (0x33,), 1: (0x24,), 2: (0x15, 0x43)},
-    ("attend", 1): {0: (0x34,), 1: (0x16, 0x25), 2: (0x44,)},
-    ("attend", 2): {0: (0x17, 0x35), 1: (0x26,), 2: (0x18,), 3: (0x45,)},
-    ("attend", 3): {0: (0x36,), 1: (0x19, 0x27), 2: (0x46,), 3: (0x1a, 0x37)},
-    ("feed", 0): {0: (0x28,), 1: (0x47,), 2: (0x1b, 0x38)},
-    ("feed", 1): {0: (0x29,), 1: (0x48,), 2: (0x39,)},
-    ("feed", 2): {0: (0x49, 0x2a), 1: (0x3a,), 2: (0x2b, 0x4a)},
+    ("attend", 0): {0: (0x34, 0x25), 2: (0x44,), 3: (0x16,)},
+    ("attend", 1): {0: (0x35, 0x17), 3: (0x45, 0x26)},
+    ("attend", 2): {0: (0x18,), 1: (0x36,), 3: (0x27, 0x46, 0x19)},
+    ("attend", 3): {0: (0x37, 0x28, 0x1a), 3: (0x47,)},
+    ("feed", 0): {0: (0x38,), 1: (0x29,), 2: (0x1b, 0x48)},
+    ("feed", 1): {0: (0x39,), 1: (0x2a,), 2: (0x49,)},
+    ("feed", 2): {0: (0x3a,), 1: (0x2b,), 2: (0x4a,)},
     ("feed", 3): {0: (0x3b, 0x4b)},
 }
 
 
-def front_kernel(
+class Scatter:
+    def __init__(self, links, sources, w, sums, piece, diag, side, final, result, send, recv, psem):
+        self.k, self.sources, self.w, self.piece, self.final, self.result = links, sources, w, piece, final, result
+        self.sums_room, self.diag_room, self.side_room = sums, diag, side
+        self.send, self.recv, self.psem = send, recv, psem
+        self.rows = w.shape[3]
+        chip = links.chip
+        self.chips = (chip, peer(chip, 1), peer(chip, 2), peer(peer(chip, 1), 2))
+
+    def sums(self, u):
+        return self.sums_room.at[u] if u < 8 else self.w.at[1, u - 8, pl.ds(0, 4)]
+
+    def side(self, u, n):
+        return self.side_room.at[u, n] if u < 8 else self.w.at[1, u - 8, 4 + n]
+
+    def diag(self, u, n):
+        half = self.rows // 2
+        return self.diag_room.at[u, n] if u < 8 else self.w.at[1, u - 8, 6, pl.ds(n * half, half)]
+
+    def outgoing(self, u, kind):
+        group, s = BACK_UNITS[u]
+        k, half = self.k, self.rows // 2
+        at, at_x, at_y, at_d = self.chips
+        sums = self.sums(u)
+        if kind == 0:
+            src, dst, to = self.sources[group].at[s, :, 1 - k.core], sums, k.at_s
+        elif kind == 1:
+            src, dst, to = sums.at[at_d, pl.ds(0, half)], self.diag(u, 0), k.at_x
+        elif kind == 2:
+            src, dst, to = sums.at[at_d, pl.ds(half, half)], self.diag(u, 1), k.at_y
+        elif kind == 3:
+            src, dst, to = sums.at[at_x], self.side(u, 0), k.at_x
+        elif kind == 4:
+            src, dst, to = sums.at[at_y], self.side(u, 1), k.at_y
+        else:
+            src, dst, to = sums.at[at], self.final.at[group, s - 1], k.at_z[s]
+        return remote(src, dst, self.send.at[u, kind], self.recv.at[u, kind], to)
+
+    def local(self, u):
+        group, s = BACK_UNITS[u]
+        return pltpu.make_async_copy(self.sources[group].at[s, :, self.k.core], self.piece.at[u % 3], self.psem.at[u % 3])
+
+    def s1(self, u):
+        self.outgoing(u, 0).start()
+        self.local(u).start()
+
+    def s2(self, u):
+        self.local(u).wait()
+        self.outgoing(u, 0).wait_recv()
+        sums, far = self.sums(u), self.chips[3]
+        sums[far] = sums[far] + self.piece[u % 3, far]
+        self.outgoing(u, 1).start()
+        self.outgoing(u, 2).start()
+        for chip in self.chips[:3]:
+            sums[chip] = sums[chip] + self.piece[u % 3, chip]
+
+    def s3(self, u):
+        half, sums = self.rows // 2, self.sums(u)
+        self.outgoing(u, 1).wait_recv()
+        self.outgoing(u, 2).wait_recv()
+        for chip, lo, n in ((self.chips[2], 0, 0), (self.chips[1], half, 1)):
+            sums[chip, lo : lo + half] = sums[chip, lo : lo + half] + self.diag(u, n)[...]
+        self.outgoing(u, 3).start()
+        self.outgoing(u, 4).start()
+
+    def s4(self, u):
+        group, s = BACK_UNITS[u]
+        self.outgoing(u, 3).wait_recv()
+        self.outgoing(u, 4).wait_recv()
+        at, sums = self.chips[0], self.sums(u)
+        total = sums[at].astype(F32) + (self.side(u, 0)[...].astype(F32) + self.side(u, 1)[...].astype(F32))
+        if s == 0:
+            self.result[group] = total
+        else:
+            sums[at] = total.astype(BF16)
+            self.outgoing(u, 5).start()
+
+    def last(self, group):
+        total = self.result[group]
+        for u, (other, s) in enumerate(BACK_UNITS):
+            if other == group and s > 0:
+                self.outgoing(u, 5).wait_recv()
+        for n in range(3):
+            total = total + self.final[group, n].astype(F32)
+        self.result[group] = total
+
+    def run(self, ops):
+        for op in ops:
+            (self.s1, self.s2, self.s3, self.s4)[op // 16 - 1](op % 16)
+
+    def at(self, loop, step, place):
+        for number in range(4):
+            ops = SCATTER_PLAN.get((loop, number), {}).get(place)
+            if ops:
+                pl.when(step == number)(functools.partial(self.run, ops))
+
+    def finish(self):
+        for u, (group, s) in enumerate(BACK_UNITS):
+            for kind in range(5 if s == 0 else 6):
+                self.outgoing(u, kind).wait_send()
+
+
+BACK_UNITS = ((1, 0), (2, 0), (1, 1), (2, 1), (1, 2), (2, 2), (1, 3), (2, 3), (0, 3), (0, 2), (0, 1), (0, 0))
+SCATTER_PLAN = {
+    ("feed", 2): {1: (0x10, 0x11)},
+    ("feed", 3): {0: (0x20,), 1: (0x12, 0x13, 0x21), 2: (0x30, 0x22, 0x14)},
+    ("other", 0): {0: (0x40,), 2: (0x32, 0x25, 0x17)},
+    ("other", 1): {0: (0x41,), 2: (0x33, 0x26, 0x42)},
+    ("other", 2): {1: (0x34, 0x27, 0x43)},
+    ("other", 3): {0: (0x35, 0x44)},
+    ("own", 0): {0: (0x36,), 1: (0x45,), 3: (0x37, 0x46, 0x18)},
+    ("own", 1): {0: (0x28,), 1: (0x47,), 2: (0x38,), 3: (0x19,)},
+    ("own", 2): {0: (0x29, 0x48), 2: (0x39,), 3: (0x1a,)},
+    ("own", 3): {0: (0x2a, 0x49), 2: (0x3a,), 3: (0x1b,)},
+}
+SCATTER_BETWEEN = ((0x23, 0x15), (0x31, 0x24, 0x16))
+SCATTER_AFTER = ((0x4a, 0x2b), (0x3b,), (0x4b,))
+
+
+def layer_kernel(
     lengths_ref, attn_ref, wout_ref, inner_ref, outer_ref, table_ref, rel_ref, gain_ref, hidden_hbm, grad_hbm,
-    own_hbm, oth_hbm, ctx_hbm, lse_ref, wa_hbm, x_hbm, xo_hbm, line_ref, out_ref, back_ref, gain_grad_ref, gi_hbm, go_hbm,
-    w, x_ref, xo, own, oth, ctx, s_ref, e_ref, middle, grad, x2_ref, x2t_ref, ob_ref, obt_ref, acc_out, acc_two, gi, go, kaug_ref,
-    send, recv, zsend, zrecv, xsem, lsem, osem, gsem,
+    out_hbm, input_hbm, small_ref, result_ref, gi_hbm, go_hbm,
+    w, x_ref, xo, own, oth, ctx, s_ref, e_ref, middle, grad, x2_ref, x2t_ref, ob_ref, obt_ref, acc_out, acc_two, g_all, kaug_ref,
+    lse_ref, line_ref, center_ref, near_ref, oth_in, sums, piece, diag, side, final,
+    line_grad, far_grad, small, small_near, small_z,
+    send, recv, zsend, zrecv, xsem, lsem, gsem, osem, bsend, brecv, psem, tsend, trecv,
 ):
     tokens = x_ref.shape[0]
     nq = tokens // LANES
     links = Links()
     net = Gather(links, w, send, recv, zsend, zrecv)
+    group = []
+    for n in range(1, 8):
+        dp = links.dp
+        for stride in (1, 2, 4):
+            if n & stride:
+                dp = peer(dp, stride)
+        group.append((dp, links.mp))
+    back = Scatter(links, (g_all, gi_hbm, go_hbm), w, sums, piece, diag, side, final, result_ref, bsend, brecv, psem)
+    width = w.shape[2] * w.shape[3]
+
+    def weights(kind, s, lo=0, hi=None):
+        part = w[kind, s, :, :, lo:] if hi is None else w[kind, s, :, :, lo:hi]
+        return part.reshape(width, part.shape[2])
+
     get_hidden = pltpu.make_async_copy(hidden_hbm, middle, lsem.at[0])
     get_grad = pltpu.make_async_copy(grad_hbm, grad, lsem.at[1])
     get_hidden.start()
     def own_block(group):
-        return (group, 0, pl.ds(pl.multiple_of(links.dp * net.rows, 16), net.rows), slice(None))
+        return (group, 0, links.dp)
 
     parts = [attn_ref[n].astype(BF16) for n in range(3)] + [wout_ref[...].T.astype(BF16)]
     q, k, v, o = [(part[:, :LANES], part[:, LANES:]) for part in parts]
@@ -309,18 +446,13 @@
     w[own_block(1)] = inner_ref[...].astype(BF16)
     w[own_block(2)] = outer_ref[...].astype(BF16)
     get_grad.start()
-    links.meet()
-    net.z_copy(0, 1).start()
+    links.meet([group[n] for n in (2, 4, 5, 6)])
+    for step in (1, 2, 3):
+        net.z_copy(0, step).start()
     net.s1(UNITS[0])
     get_hidden.wait()
     x_ref[...] = rms_scaled(middle[...], gain_ref[0:1, :]).astype(BF16)
     xcopy = remote(x_ref, xo, xsem.at[0], xsem.at[1], links.at_z[1])
-    net.z_copy(0, 2).start()
-    xcopy.start()
-    net.z_copy(0, 3).start()
-    for step in (1, 2, 3):
-        net.z_copy(1, step).start()
-        net.z_copy(2, step).start()
     hot = turned_hot(table_ref[...], 2 * LANES - 1)[: rel_ref.shape[1]]
     high = rel_ref[...].astype(BF16)
     rest = rel_ref[...] - high.astype(F32)
@@ -329,12 +461,19 @@
     line_ref[...] = mm(high, hot) + (mm(mid, hot) + mm(low, hot))
     kaug_ref[...] = key_aug(links.half, lengths_ref[links.mp // 2], tokens)
     far = far_masks(links.first, nq)
-    net.run(GATHER_AHEAD[:8])
+    net.run(GATHER_AHEAD[0])
+    for step in (1, 2, 3):
+        net.z_copy(0, step).wait_send()
+    xcopy.start()
     get_grad.wait()
     ob = grad[...].astype(BF16)
     ob_ref[...] = ob
     obt_ref[...] = ob.T
-    net.run(GATHER_AHEAD[8:])
+    net.run(GATHER_AHEAD[1])
+    xcopy.wait_send()
+    for step in (1, 2, 3):
+        net.z_copy(1, step).start()
+        net.z_copy(2, step).start()
     xcopy.wait_recv()
 
     masks = [half_rows(0), half_rows(1)]
@@ -343,10 +482,10 @@
 
     def attend(s, carry):
         x, other = x_ref[...], xo[...]
-        p_a = mm(x, w[0, s, :, : 3 * LANES]).astype(BF16)
-        p_b = mm(x, w[0, s, :, 4 * LANES :]).astype(BF16)
-        o_a = mm(other, w[0, s, :, LANES : 3 * LANES]).astype(BF16)
-        o_b = mm(other, w[0, s, :, 4 * LANES :]).astype(BF16)
+        p_a = mm(x, weights(0, s, 0, 3 * LANES)).astype(BF16)
+        p_b = mm(x, weights(0, s, 4 * LANES)).astype(BF16)
+        o_a = mm(other, weights(0, s, LANES, 3 * LANES)).astype(BF16)
+        o_b = mm(other, weights(0, s, 4 * LANES)).astype(BF16)
         own[s, :, : 3 * LANES] = p_a
         own[s, :, 3 * LANES :] = p_b
         oth[s, :, : 2 * LANES] = o_a
@@ -367,18 +506,18 @@
             scores = mt(ka, qa)
             peak = None
             for jb, row in enumerate(add_bias(scores, tile, line, links.first, nq)):
-                s_ref[i % 2, jb * LANES : (jb + 1) * LANES, :] = row
+                s_ref[i % 2 * 2 * nq + jb] = row
                 top = jnp.max(row.reshape(LANES // 8, 8, tokens), axis=0)
                 peak = top if peak is None else jnp.maximum(peak, top)
             peak = jnp.max(peak, axis=0, keepdims=True)
             for jb in range(2 * nq):
-                rows = slice(jb * LANES, (jb + 1) * LANES)
-                e_ref[i % 2, rows, :] = jnp.exp(s_ref[i % 2, rows, :] - peak).astype(BF16)
+                rows = slice(jb % nq * LANES, (jb % nq + 1) * LANES)
+                e_ref[i % 2 * 2 + jb // nq, rows, :] = jnp.exp(s_ref[i % 2 * 2 * nq + jb] - peak).astype(BF16)
             if vh == 0:
                 va = jnp.concatenate([v_t[vc][:HDIM], ones], axis=0)
             else:
                 va = jnp.concatenate([ones, v_t[vc][HDIM:]], axis=0)
-            ot = mm(va, e_ref[i % 2])
+            ot = mm(va, e_ref[i % 2 * 2 : i % 2 * 2 + 2].reshape(2 * tokens, tokens))
             at = HDIM if vh == 0 else 0
             total = ot[at : at + 1, :]
             stats.append(peak + jnp.log(total))
@@ -390,45 +529,38 @@
         ctx[s, :, :LANES] = ctx_a
         ctx[s, :, LANES:] = ctx_b
         lse_ref[s] = jnp.concatenate(stats + [jnp.zeros((5, tokens), F32)], axis=0)
-        middle[...] += mt(ctx_a, w[0, s, :, 3 * LANES : 4 * LANES]) + mt(ctx_b, w[0, s, :, 5 * LANES :])
+        middle[...] += mt(ctx_a, weights(0, s, 3 * LANES, 4 * LANES)) + mt(ctx_b, weights(0, s, 5 * LANES))
         net.at("attend", s, 3)
         return carry
 
     lax.fori_loop(0, 4, attend, 0)
-    saves = [
-        pltpu.make_async_copy(a, b, osem.at[n])
-        for n, (a, b) in enumerate(((own, own_hbm), (oth, oth_hbm), (ctx, ctx_hbm), (w.at[0], wa_hbm), (xo, xo_hbm), (x_ref, x_hbm)))
-    ]
-    for copy in saves:
-        copy.start()
 
     x2 = rms_scaled(middle[...], gain_ref[1:2, :]).astype(BF16)
     x2_ref[...] = x2
     x2t_ref[...] = x2.T
     acc_out[...] = jnp.zeros_like(acc_out)
     acc_two[...] = jnp.zeros_like(acc_two)
+
     def g_copies(t):
-        slot = t % 2
         return (
-            pltpu.make_async_copy(gi.at[slot], gi_hbm.at[t], gsem.at[slot, 0]),
-            pltpu.make_async_copy(go.at[slot], go_hbm.at[t], gsem.at[slot, 1]),
+            pltpu.make_async_copy(g_all.at[t % 2 * 2], gi_hbm.at[t], gsem.at[t % 2, 0]),
+            pltpu.make_async_copy(g_all.at[t % 2 * 2 + 1], go_hbm.at[t], gsem.at[t % 2, 1]),
         )
 
     def feed(t, carry):
-        slot = t % 2
-        cols = w.shape[3]
         tile = 2 * LANES
-
-        @pl.when(t >= 2)
-        def _():
-            for copy in g_copies(t - 2):
-                copy.wait()
-
-        for n in range(cols // tile):
+        for n in range(w.shape[4] // tile):
             net.at("feed", t, n)
-            at = slice(n * tile, (n + 1) * tile)
-            wi = w[1, t, :, at]
-            wo = w[2, t, :, at]
+            if n == 1:
+
+                @pl.when(t >= 1)
+                def _():
+                    for copy in g_copies(t - 1):
+                        copy.wait()
+
+            back.at("feed", t, n)
+            wi = weights(1, t, n * tile, (n + 1) * tile)
+            wo = weights(2, t, n * tile, (n + 1) * tile)
             inner = mm(x2_ref[...], wi)
             active_back = mm(ob_ref[...], wo)
             c = 0.7978845608028654
@@ -440,187 +572,35 @@
             inner_back = (slope * active_back).astype(BF16)
             acc_out[...] += mt(active, wo)
             acc_two[...] += mt(inner_back, wi)
-            go[slot, :, at] = mm(obt_ref[...], active).astype(BF16)
-            gi[slot, :, at] = mm(x2t_ref[...], inner_back).astype(BF16)
+            at = slice(n * tile, (n + 1) * tile)
+            shape = (*w.shape[2:4], tile)
+            split = (shape[0] // 2, 2, *shape[1:])
+            g_all[t % 2 * 2, :, :, :, at] = mm(x2t_ref[...], inner_back).astype(BF16).reshape(split)
+            g_all[t % 2 * 2 + 1, :, :, :, at] = mm(obt_ref[...], active).astype(BF16).reshape(split)
         for copy in g_copies(t):
             copy.start()
-
         return carry
 
     lax.fori_loop(0, 4, feed, 0)
-    out_ref[...] = middle[...] + acc_out[...]
-    result, gain_part = rms_back(middle[...], gain_ref[1:2, :], acc_two[...])
-    back_ref[...] = grad[...] + result
-    gain_grad_ref[...] = jnp.broadcast_to(gain_part, gain_grad_ref.shape)
-    for t in (2, 3):
-        for copy in g_copies(t):
-            copy.wait()
-    for copy in saves:
+    back.run(SCATTER_BETWEEN[0])
+    acc_out[...] += middle[...]
+    put_out = pltpu.make_async_copy(acc_out, out_hbm, lsem.at[2])
+    put_out.start()
+    result, gain_two = rms_back(middle[...], gain_ref[1:2, :], acc_two[...])
+    get_hidden = pltpu.make_async_copy(hidden_hbm, middle, lsem.at[0])
+    get_hidden.start()
+    grad[...] += result
+    net.finish()
+    for copy in g_copies(3):
         copy.wait()
-    xcopy.wait_send()
-    net.finish()
-
-
-class Scatter:
-    def __init__(self, links, sources, sums, piece, diag, side, final, result, send, recv, psem):
-        self.k, self.sources, self.sums, self.piece = links, sources, sums, piece
-        self.diag, self.side, self.final, self.result = diag, side, final, result
-        self.send, self.recv, self.psem = send, recv, psem
-        self.rows = sums.shape[2]
-        chip = links.chip
-        self.chips = (chip, peer(chip, 1), peer(chip, 2), peer(peer(chip, 1), 2))
-
-    def outgoing(self, u, kind):
-        group, s = BACK_UNITS[u]
-        k, half = self.k, self.rows // 2
-        at, at_x, at_y, at_d = self.chips
-        if kind == 0:
-            src, dst, to = self.sources[group].at[s, :, 1 - k.core], self.sums.at[u], k.at_s
-        elif kind == 1:
-            src, dst, to = self.sums.at[u, at_d, pl.ds(0, half)], self.diag.at[u, 0], k.at_x
-        elif kind == 2:
-            src, dst, to = self.sums.at[u, at_d, pl.ds(half, half)], self.diag.at[u, 1], k.at_y
-        elif kind == 3:
-            src, dst, to = self.sums.at[u, at_x], self.side.at[u, 0], k.at_x
-        elif kind == 4:
-            src, dst, to = self.sums.at[u, at_y], self.side.at[u, 1], k.at_y
-        else:
-            src, dst, to = self.sums.at[u, at], self.final.at[group, s - 1], k.at_z[s]
-        return remote(src, dst, self.send.at[u, kind], self.recv.at[u, kind], to)
-
-    def local(self, u):
-        group, s = BACK_UNITS[u]
-        return pltpu.make_async_copy(self.sources[group].at[s, :, self.k.core], self.piece.at[u % 3], self.psem.at[u % 3])
-
-    def s1(self, u):
-        self.outgoing(u, 0).start()
-        self.local(u).start()
-
-    def s2(self, u):
-        self.local(u).wait()
-        self.outgoing(u, 0).wait_recv()
-        far = self.chips[3]
-        self.sums[u, far] = self.sums[u, far] + self.piece[u % 3, far]
-        self.outgoing(u, 1).start()
-        self.outgoing(u, 2).start()
-        for chip in self.chips[:3]:
-            self.sums[u, chip] = self.sums[u, chip] + self.piece[u % 3, chip]
-
-    def s3(self, u):
-        half = self.rows // 2
-        self.outgoing(u, 1).wait_recv()
-        self.outgoing(u, 2).wait_recv()
-        for chip, lo, n in ((self.chips[2], 0, 0), (self.chips[1], half, 1)):
-            self.sums[u, chip, lo : lo + half] = self.sums[u, chip, lo : lo + half] + self.diag[u, n]
-        self.outgoing(u, 3).start()
-        self.outgoing(u, 4).start()
-
-    def s4(self, u):
-        group, s = BACK_UNITS[u]
-        self.outgoing(u, 3).wait_recv()
-        self.outgoing(u, 4).wait_recv()
-        at = self.chips[0]
-        total = self.sums[u, at].astype(F32) + (self.side[u, 0].astype(F32) + self.side[u, 1].astype(F32))
-        if s == 0:
-            self.result[group] = total
-        else:
-            self.sums[u, at] = total.astype(BF16)
-            self.outgoing(u, 5).start()
-
-    def last(self, group):
-        total = self.result[group]
-        for u, (other, s) in enumerate(BACK_UNITS):
-            if other == group and s > 0:
-                self.outgoing(u, 5).wait_recv()
-        for n in range(3):
-            total = total + self.final[group, n].astype(F32)
-        self.result[group] = total
-
-    def run(self, ops):
-        for op in ops:
-            (self.s1, self.s2, self.s3, self.s4)[op // 16 - 1](op % 16)
-
-    def at(self, loop, step, place):
-        for number in range(4):
-            ops = SCATTER_PLAN.get((loop, number), {}).get(place)
-            if ops:
-                pl.when(step == number)(functools.partial(self.run, ops))
-
-    def finish(self):
-        for u, (group, s) in enumerate(BACK_UNITS):
-            for kind in range(5 if s == 0 else 6):
-                self.outgoing(u, kind).wait_send()
-
-
-BACK_UNITS = ((1, 3), (2, 3), (1, 2), (2, 2), (1, 1), (2, 1), (1, 0), (2, 0), (0, 3), (0, 2), (0, 1), (0, 0))
-SCATTER_AHEAD = ((0x10, 0x11, 0x12), (0x20,), (0x21,))
-SCATTER_PLAN = {
-    ("other", 0): {0: (0x30, 0x22, 0x13), 2: (0x31, 0x23, 0x14, 0x40)},
-    ("other", 1): {1: (0x32, 0x24, 0x15, 0x41)},
-    ("other", 2): {1: (0x33, 0x25, 0x16, 0x42)},
-    ("other", 3): {0: (0x34, 0x26, 0x17, 0x43)},
-    ("own", 0): {0: (0x35, 0x27, 0x44), 2: (0x36, 0x45), 3: (0x18,)},
-    ("own", 1): {0: (0x37, 0x46), 1: (0x28,), 2: (0x47,), 3: (0x38, 0x19)},
-    ("own", 2): {1: (0x29,), 2: (0x48,), 3: (0x39, 0x1a)},
-    ("own", 3): {1: (0x2a,), 2: (0x49,), 3: (0x3a, 0x1b)},
-}
-SCATTER_AFTER = ((0x2b,), (0x4a, 0x3b), (0x4b,))
-
-
-def back_kernel(
-    lengths_ref, x_ref, line_ref, table_ref, lse_ref, gain_ref, gain_two_ref,
-    xo_hbm, back_hbm, hidden_hbm, wa_hbm, own_hbm, oth_hbm, ctx_hbm, gi_hbm, go_hbm,
-    grad_ref, small_ref, result_ref,
-    xo, back, hidden, wa, own, oth, ctx, xt, xot, ab_ref, abt, acc_own, acc_oth, oth_out, oth_in,
-    dq_acc, d_oth, cb_ref, center_ref, near_ref, ga, sums, piece, diag, side, final,
-    kaug_ref, line_grad, far_grad, small, small_near, small_z,
-    lsem, ssem, osem, send, recv, psem, tsend, trecv,
-):
-    tokens = x_ref.shape[0]
-    nq = tokens // LANES
-    links = Links()
-    group = []
-    for n in range(1, 8):
-        dp = links.dp
-        for stride in (1, 2, 4):
-            if n & stride:
-                dp = peer(dp, stride)
-        group.append((dp, links.mp))
-    net = Scatter(links, (ga, gi_hbm, go_hbm), sums, piece, diag, side, final, result_ref, send, recv, psem)
-    loads = [
-        pltpu.make_async_copy(a, b, lsem.at[n])
-        for n, (a, b) in enumerate(((back_hbm, back), (xo_hbm, xo), (hidden_hbm, hidden)))
-    ]
-
-    def step_loads(s):
-        return [
-            pltpu.make_async_copy(a.at[s], b.at[s], ssem.at[s, n])
-            for n, (a, b) in enumerate(((wa_hbm, wa), (own_hbm, own), (oth_hbm, oth), (ctx_hbm, ctx)))
-        ]
-
-    loads[0].start()
-    for copy in step_loads(3):
-        copy.start()
-    loads[1].start()
-    for s in (2, 1, 0):
-        for copy in step_loads(s):
-            copy.start()
-    loads[2].start()
-    links.meet([group[n] for n in (2, 4, 5, 6)])
-    net.run(SCATTER_AHEAD[0])
-    loads[0].wait()
-    ab = back[...].astype(BF16)
+    back.run(SCATTER_BETWEEN[1])
+    ab_ref, abt, xt, acc_own, acc_oth, oth_out = x2_ref, x2t_ref, obt_ref, acc_out, acc_two, ob_ref
+    ab = grad[...].astype(BF16)
     ab_ref[...] = ab
     abt[...] = ab.T
-    net.run(SCATTER_AHEAD[1])
     xt[...] = x_ref[...].T
-    acc_own[...] = jnp.zeros_like(acc_own)
+    w[2, 0, :, :, : tokens] = xo[...].T.reshape(*w.shape[2:4], tokens)
     acc_oth[...] = jnp.zeros_like(acc_oth)
-    loads[1].wait()
-    xot[...] = xo[...].T
-    net.run(SCATTER_AHEAD[2])
-    kaug_ref[...] = key_aug(links.half, lengths_ref[links.mp // 2], tokens)
-    far = far_masks(links.first, nq)
     line_grad[...] = jnp.zeros_like(line_grad)
     far_grad[...] = jnp.zeros_like(far_grad)
     jb = lax.broadcasted_iota(jnp.int32, (2 * nq, tokens), 0)
@@ -630,20 +610,25 @@
     other_key = (jb >= nq).astype(F32)
     sum_before = ((jb < nq) & (jb < ib - 1)).astype(F32) + (other_key - edge_last) * (1.0 - links.first)
     sum_after = ((jb < nq) & (jb > ib + 1)).astype(F32) + (other_key - edge_first) * links.first
-    masks = [half_rows(0), half_rows(1)]
     own_at = {c: slice(at * LANES, (at + 1) * LANES) for at, c in enumerate((0, 1, 2, 4, 5))}
     oth_at = {c: slice(at * LANES, (at + 1) * LANES) for at, c in enumerate((1, 2, 4, 5))}
     cb_at = {2: slice(0, LANES), 4: slice(LANES, 2 * LANES)}
     at_row = lax.broadcasted_iota(jnp.int32, (LANES, LANES), 0) + lax.broadcasted_iota(jnp.int32, (LANES, LANES), 1)
     mirror = (at_row == LANES - 1).astype(F32).astype(BF16)
 
-    def one_side(s, i, other):
+    def context_back(s):
+        return {
+            2: mm(ab_ref[...], weights(0, s, 3 * LANES, 4 * LANES)).astype(BF16),
+            4: mm(ab_ref[...], weights(0, s, 5 * LANES)).astype(BF16),
+        }
+
+    def one_side(s, i, other, cb):
         qc, qh, kc, vc, vh = HEAD_AT[i]
         line = line_ref[pl.ds(3 * links.column(s) + i, 1), :]
         tile = bias_tile(line)
         qm = own[s, :, own_at[qc]] * masks[qh]
         qa = qm + query_aug(line, far, nq) * masks[1 - qh]
-        om = cb_ref[s, :, cb_at[vc]] * masks[vh]
+        om = cb[vc] * masks[vh]
         center = center_ref[s, i : i + 1, :]
         lse = lse_ref[s, i : i + 1, :]
         parts = near_parts(tile)
@@ -685,12 +670,7 @@
 
     def other_side(it, carry):
         s = 3 - it
-        for copy in step_loads(s):
-            copy.wait()
-        cb = {
-            2: mm(ab_ref[...], wa[s, :, 3 * LANES : 4 * LANES]).astype(BF16),
-            4: mm(ab_ref[...], wa[s, :, 5 * LANES :]).astype(BF16),
-        }
+        cb = context_back(s)
         centers = []
         for i in range(3):
             vc, vh = HEAD_AT[i][3:]
@@ -699,20 +679,17 @@
             low = (prod - high.astype(F32)).astype(BF16)
             pick = jnp.broadcast_to(masks[vh], (8, LANES))
             centers.append((mt(pick, high) + mt(pick, low))[0:1, :])
-        for c in cb:
-            cb_ref[s, :, cb_at[c]] = cb[c]
         center_ref[s] = jnp.concatenate(centers + [jnp.zeros((5, tokens), F32)], axis=0)
         dk, dv = {}, {}
         for i, (qc, qh, kc, vc, vh) in enumerate(HEAD_AT):
-            net.at("other", it, i)
-            dq_acc[s, i], part_k, part_v, near = one_side(s, i, True)
+            back.at("other", it, i)
+            s_ref[3 * s + i], part_k, part_v, near = one_side(s, i, True, cb)
             dk[kc] = dk[kc] + part_k if kc in dk else part_k
             dv[vc] = dv[vc] + part_v if vc in dv else part_v
-            near_ref[s, i, 0] = near[3]
-            near_ref[s, i, 1] = near[4]
+            near_ref[s, i] = near[3] * links.first + near[4] * (1.0 - links.first)
         d = jnp.concatenate([dk[1], dv[2], dv[4], dk[5]], axis=1).astype(BF16)
-        d_oth[s] = d
-        acc_oth[...] += mt(d[:, : 2 * LANES], wa[s, :, LANES : 3 * LANES]) + mt(d[:, 2 * LANES :], wa[s, :, 4 * LANES :])
+        e_ref[s] = d
+        acc_oth[...] += mt(d[:, : 2 * LANES], weights(0, s, LANES, 3 * LANES)) + mt(d[:, 2 * LANES :], weights(0, s, 4 * LANES))
         return carry
 
     lax.fori_loop(0, 4, other_side, 0)
@@ -723,11 +700,12 @@
     def own_side(it, carry):
         s = 3 - it
         m = links.column(s)
+        cb = context_back(s)
         dk, dv, dq = {}, {}, []
         for i, (qc, qh, kc, vc, vh) in enumerate(HEAD_AT):
-            net.at("own", it, i)
-            part_q, part_k, part_v, near = one_side(s, i, False)
-            part_q = part_q + dq_acc[s, i]
+            back.at("own", it, i)
+            part_q, part_k, part_v, near = one_side(s, i, False, cb)
+            part_q = part_q + s_ref[3 * s + i]
             dk[kc] = dk[kc] + part_k if kc in dk else part_k
             dv[vc] = dv[vc] + part_v if vc in dv else part_v
             at = HDIM if qh == 0 else 0
@@ -736,7 +714,7 @@
             far_grad[0, head, :] = jnp.sum(block_sums * sum_before, axis=0, keepdims=True)
             far_grad[1, head, :] = jnp.sum(block_sums * sum_after, axis=0, keepdims=True)
             dq.append(part_q[:HDIM] if qh == 0 else part_q[HDIM:])
-            first, final_corner = near_ref[s, i, 0] * links.first, near_ref[s, i, 1] * (1.0 - links.first)
+            first, final_corner = near_ref[s, i] * links.first, near_ref[s, i] * (1.0 - links.first)
             blank = jnp.zeros((LANES, LANES), F32)
             tile = jnp.concatenate([near[1], near[0] + final_corner, blank, near[2] + first], axis=1)
             high = tile.astype(BF16)
@@ -747,7 +725,7 @@
         dq_b = jnp.concatenate([dq[2], jnp.zeros_like(dq[2])], axis=0).T
         d_own = jnp.concatenate([dq_a, dk[1], dv[2], dq_b + dv[4], dk[5]], axis=1).astype(BF16)
         g_own = mm(xt[...], d_own)
-        g_oth = mm(xot[...], d_oth[s])
+        g_oth = mm(w[2, 0, :, :, :tokens].reshape(width, tokens), e_ref[s])
         g_ctx = mm(abt[...], ctx[s])
         columns = [
             g_own[:, :LANES],
@@ -757,21 +735,25 @@
             g_own[:, 4 * LANES :] + g_oth[:, 3 * LANES :] + g_ctx[:, LANES:],
         ]
         g = jnp.concatenate(columns, axis=1).astype(BF16)
-        rows = ga.shape[3]
+        rows = w.shape[3]
         for n in range(8):
-            ga[s, n // 2, n % 2] = g[n * rows : (n + 1) * rows, :]
-        net.at("own", it, 3)
-        acc_own[...] += mt(d_own[:, : 3 * LANES], wa[s, :, : 3 * LANES]) + mt(d_own[:, 3 * LANES :], wa[s, :, 4 * LANES :])
+            g_all[s, n // 2, n % 2] = g[n * rows : (n + 1) * rows, :]
+        back.at("own", it, 3)
+        acc_own[...] += mt(d_own[:, : 3 * LANES], weights(0, s, 0, 3 * LANES)) + mt(d_own[:, 3 * LANES :], weights(0, s, 4 * LANES))
         return carry
 
+    put_out.wait()
+    acc_own[...] = jnp.zeros_like(acc_own)
     lax.fori_loop(0, 4, own_side, 0)
-    net.run(SCATTER_AFTER[0])
-    loads[2].wait()
+    back.run(SCATTER_AFTER[0])
+    get_hidden.wait()
     swap.wait_recv()
     one_back = acc_own[...] + oth_in[...].astype(F32)
-    grad, gain_part = rms_back(hidden[...], gain_ref[0:1, :], one_back)
-    grad_ref[...] = grad + back[...]
-    net.run(SCATTER_AFTER[1])
+    value, gain_part = rms_back(middle[...], gain_ref[0:1, :], one_back)
+    acc_own[...] = value + grad[...]
+    put_grad = pltpu.make_async_copy(acc_own, input_hbm, lsem.at[2])
+    put_grad.start()
+    back.run(SCATTER_AFTER[1])
     lane = lax.broadcasted_iota(jnp.int32, (16, 4 * LANES), 1)
     by_line = (
         line_grad[...]
@@ -785,11 +767,11 @@
     for n in range(6):
         at = slice(n * LANES, (n + 1) * LANES)
         small[16 + n : 17 + n, :] = gain_part[:, at]
-        small[22 + n : 23 + n, :] = gain_two_ref[0:1, at]
-    net.run(SCATTER_AFTER[2])
+        small[22 + n : 23 + n, :] = gain_two[:, at]
+    back.run(SCATTER_AFTER[2])
     squares = jnp.zeros((8, LANES), F32)
     for weight in (1, 2, 0):
-        net.last(weight)
+        back.last(weight)
         value = result_ref[weight]
         value = value * value
         for n in range(value.shape[1] // LANES):
@@ -813,8 +795,9 @@
     small_ref[...] = (small_z[0] + small_z[1]) + (small_z[2] + small_z[3])
     for copy in near + along:
         copy.wait_send()
+    put_grad.wait()
     swap.wait_send()
-    net.finish()
+    back.finish()
 
 
 def update_kernel(small_ref, grad_hbm, block_hbm, input_hbm, *refs):
@@ -878,91 +861,43 @@
         copy.wait()
 
 
-def run_front(lengths, attn, out, inner, outer, table, rel, gains, hidden, grad):
+def run_layer(lengths, attn, out, inner, outer, table, rel, gains, hidden, grad):
     t, d = hidden.shape
-    parts, cols = rel.shape[0] // 3, inner.shape[1]
-    any_space = pl.BlockSpec(memory_space=pl.ANY)
-    vmem = pl.BlockSpec(memory_space=pltpu.VMEM)
-    dma = pltpu.SemaphoreType.DMA
-    return pl.pallas_call(
-        front_kernel,
-        in_specs=[pl.BlockSpec(memory_space=pltpu.SMEM)] + [vmem] * 7 + [any_space] * 2,
-        out_specs=[any_space] * 3 + [vmem] + [any_space] * 3 + [vmem] * 4 + [any_space] * 2,
-        out_shape=[
-            jax.ShapeDtypeStruct((parts, t, 5 * LANES), BF16),
-            jax.ShapeDtypeStruct((parts, t, 4 * LANES), BF16),
-            jax.ShapeDtypeStruct((parts, t, 2 * LANES), BF16),
-            jax.ShapeDtypeStruct((parts, 8, t), F32),
-            jax.ShapeDtypeStruct((parts, d, cols), BF16),
-            jax.ShapeDtypeStruct((t, d), BF16),
-            jax.ShapeDtypeStruct((t, d), BF16),
-            jax.ShapeDtypeStruct((rel.shape[0], 4 * LANES), F32),
-            jax.ShapeDtypeStruct((t, d), F32),
-            jax.ShapeDtypeStruct((t, d), F32),
-            jax.ShapeDtypeStruct((8, d), F32),
-            jax.ShapeDtypeStruct((parts, d, cols), BF16),
-            jax.ShapeDtypeStruct((parts, d, cols), BF16),
-        ],
-        scratch_shapes=[
-            pltpu.VMEM((3, parts, d, cols), BF16),
-            pltpu.VMEM((t, d), BF16),
-            pltpu.VMEM((t, d), BF16),
-            pltpu.VMEM((parts, t, 5 * LANES), BF16),
-            pltpu.VMEM((parts, t, 4 * LANES), BF16),
-            pltpu.VMEM((parts, t, 2 * LANES), BF16),
-            pltpu.VMEM((2, 2 * t, t), F32),
-            pltpu.VMEM((2, 2 * t, t), BF16),
-            pltpu.VMEM((t, d), F32),
-            pltpu.VMEM((t, d), F32),
-            pltpu.VMEM((t, d), BF16), pltpu.VMEM((d, t), BF16),
-            pltpu.VMEM((t, d), BF16), pltpu.VMEM((d, t), BF16),
-            pltpu.VMEM((t, d), F32), pltpu.VMEM((t, d), F32),
-            pltpu.VMEM((2, d, cols), BF16), pltpu.VMEM((2, d, cols), BF16),
-            pltpu.VMEM((2 * t, LANES), BF16),
-            dma((12, 8)), dma((12, 8)), dma((9,)), dma((9,)), dma((2,)), dma((2,)), dma((6,)), dma((2, 2)),
-        ],
-        compiler_params=pltpu.CompilerParams(
-            vmem_limit_bytes=62 * 2**20, collective_id=0, has_side_effects=True
-        ),
-        name="front",
-    )(lengths, attn, out, inner, outer, table, rel, gains, hidden, grad)
-
-
-def run_back(lengths, x, line, table, lse, gains, gain_two, xo, back, hidden, wa, own, oth, ctx, gi, go):
-    t, d = x.shape
-    parts, cols = wa.shape[0], wa.shape[2]
-    rows = d // 8
+    parts, (rows, cols) = rel.shape[0] // 3, inner.shape
     any_space = pl.BlockSpec(memory_space=pl.ANY)
     vmem = pl.BlockSpec(memory_space=pltpu.VMEM)
     dma = pltpu.SemaphoreType.DMA
     split = (parts, 4, 2, rows, cols)
+    low = lambda *shape: pltpu.VMEM(shape, BF16)
+    full = lambda *shape: pltpu.VMEM(shape, F32)
     return pl.pallas_call(
-        back_kernel,
-        in_specs=[pl.BlockSpec(memory_space=pltpu.SMEM)] + [vmem] * 6 + [any_space] * 9,
-        out_specs=[vmem] * 3,
+        layer_kernel,
+        in_specs=[pl.BlockSpec(memory_space=pltpu.SMEM)] + [vmem] * 7 + [any_space] * 2,
+        out_specs=[any_space] * 2 + [vmem] * 2 + [any_space] * 2,
         out_shape=[
+            jax.ShapeDtypeStruct((t, d), F32),
             jax.ShapeDtypeStruct((t, d), F32),
             jax.ShapeDtypeStruct((32, LANES), F32),
             jax.ShapeDtypeStruct((3, rows, cols), F32),
+            jax.ShapeDtypeStruct(split, BF16),
+            jax.ShapeDtypeStruct(split, BF16),
         ],
         scratch_shapes=[
-            pltpu.VMEM((t, d), BF16), pltpu.VMEM((t, d), F32), pltpu.VMEM((t, d), F32),
-            pltpu.VMEM(wa.shape, BF16), pltpu.VMEM(own.shape, BF16), pltpu.VMEM(oth.shape, BF16), pltpu.VMEM(ctx.shape, BF16),
-            pltpu.VMEM((d, t), BF16), pltpu.VMEM((d, t), BF16), pltpu.VMEM((t, d), BF16), pltpu.VMEM((d, t), BF16),
-            pltpu.VMEM((t, d), F32), pltpu.VMEM((t, d), F32), pltpu.VMEM((t, d), BF16), pltpu.VMEM((t, d), BF16),
-            pltpu.VMEM((parts, 3, LANES, t), F32), pltpu.VMEM((parts, t, 4 * LANES), BF16),
-            pltpu.VMEM((parts, t, 2 * LANES), BF16), pltpu.VMEM((parts, 8, t), F32), pltpu.VMEM((parts, 3, 2, LANES, LANES), F32),
-            pltpu.VMEM(split, BF16), pltpu.VMEM((12, 4, rows, cols), BF16), pltpu.VMEM((3, 4, rows, cols), BF16),
-            pltpu.VMEM((12, 2, rows // 2, cols), BF16), pltpu.VMEM((12, 2, rows, cols), BF16), pltpu.VMEM((3, 3, rows, cols), BF16),
-            pltpu.VMEM((2 * t, LANES), BF16), pltpu.VMEM((16, 4 * LANES), F32), pltpu.VMEM((2, 16, 4 * LANES), F32),
-            pltpu.VMEM((32, LANES), F32), pltpu.VMEM((7, 32, LANES), F32), pltpu.VMEM((4, 32, LANES), F32),
-            dma((3,)), dma((parts, 4)), dma((2,)), dma((12, 6)), dma((12, 6)), dma((3,)), dma((10,)), dma((10,)),
+            low(3, parts, 8, rows, cols), low(t, d), low(t, d),
+            low(parts, t, 5 * LANES), low(parts, t, 4 * LANES), low(parts, t, 2 * LANES),
+            full(4 * t // LANES, LANES, t), low(4, t, t), full(t, d), full(t, d),
+            low(t, d), low(d, t), low(t, d), low(d, t), full(t, d), full(t, d), low(*split), low(2 * t, LANES),
+            full(parts, 8, t), full(rel.shape[0], 4 * LANES), full(parts, 8, t), full(parts, 3, LANES, LANES), low(t, d),
+            low(8, 4, rows, cols), low(3, 4, rows, cols), low(8, 2, rows // 2, cols), low(8, 2, rows, cols), low(3, 3, rows, cols),
+            full(16, 4 * LANES), full(2, 16, 4 * LANES), full(32, LANES), full(7, 32, LANES), full(4, 32, LANES),
+            dma((12, 8)), dma((12, 8)), dma((9,)), dma((9,)), dma((2,)), dma((3,)), dma((2, 2)), dma((2,)),
+            dma((12, 6)), dma((12, 6)), dma((3,)), dma((10,)), dma((10,)),
         ],
         compiler_params=pltpu.CompilerParams(
-            vmem_limit_bytes=62 * 2**20, collective_id=1, has_side_effects=True
+            vmem_limit_bytes=63 * 2**20, collective_id=0, has_side_effects=True
         ),
-        name="back",
-    )(lengths, x, line, table, lse, gains, gain_two, xo, back, hidden, wa, own, oth, ctx, gi.reshape(split), go.reshape(split))
+        name="layer",
+    )(lengths, attn, out, inner, outer, table, rel, gains, hidden, grad)
 
 
 def run_update(small, grads, block_out, input_grad, masters, moments):
@@ -988,11 +923,8 @@
     rel_first, rel_second, gain_first, gain_second, *, parts,
 ):
     near_table = table[SEQLEN - 2 * LANES : SEQLEN + 2 * LANES].reshape(1, 4 * LANES)
-    own, oth, ctx, lse, wa, x1, x1o, line, block_out, middle_back, gain_two, gi, go = run_front(
+    block_out, input_grad, small, owned, _, _ = run_layer(
         lengths, attn_weight, out_weight, inner_weight, outer_weight.T, near_table, rel_bias.T, gains, hidden_in, out_grad
-    )
-    input_grad, small, owned = run_back(
-        lengths, x1, line, near_table, lse, gains, gain_two, x1o, middle_back, hidden_in, wa, own, oth, ctx, gi, go
     )
     new = run_update(
         small, owned, block_out, input_grad,

time: 198 us -> 184 us (0.929)
  Pallas kernels: 196 us -> 182 us
    pallas_call x2 -> x1, Pallas kernels: 189 us -> 175 us  [run_layer(): pl.pallas_call(layer_kernel, in_specs=[pl.BlockSpec(memory_space=pltpu.SM...]
where the time goes in v4:
time: 184 us
  Pallas kernels  182 us (99%)
    pallas_call x1, Pallas kernels, run_layer(): pl.pallas_call(layer_kernel, in_specs=[pl.BlockSpec(memory_space=pltpu.SM...  175 us
    pallas_call x1, Pallas kernels, run_update(): pl.pallas_call(update_kernel, in_specs=[vmem] + [hbm] * 21, out_specs=[hb...  7.16 us

profile of v4, /device:TPU:0, one launch (start us, length us, event | category | flops | bytes accessed | tf_op | source)
XLA Modules:
  0.0 183.9 jit_solution(14252932712407294107)
XLA Ops:
  0.7 1.3 slice.3
  1.9 174.6 %layer.1 = (f32[512,768]{1,0:T(8,128)}, f32[512,768]{1,0:T(8,128)}, f32[32,128]{1,0:T(8,128)}, f32[3,96,768]{2,1,0:T(8,128)}, bf16[4,4,2,96,768]{4,3,2,1,0:T(8,128)(2,1)}, /*index=5*/bf16[4,4,2,96,768]{4,3,2,1,0:T(8,128)(2,1)}) custom-call(s32[2]{0:T(128)} %lengths_ref.1, f32[3,96,192]{2,1,0:T(8,128)} %refs_0_.1, f32[192,96]{1,0:T(8,128)} %refs_1_.1, ...), custom_call_target="tpu_custom_call" | custom-call | tf_op jit(solution)/shard_map/layer/pallas_call | solution.py:873
  176.6 7.2 %update.1 = (f32[512,768]{1,0:T(8,128)}, f32[512,768]{1,0:T(8,128)}, f32[1,1]{1,0:T(1,128)}, f32[3,96,192]{2,1,0:T(8,128)}, f32[3,96,192]{2,1,0:T(8,128)}, /*ind...) custom-call(f32[32,128]{1,0:T(8,128)} %get-tuple-element.46.small_re, ...), custom_call_target="tpu_custom_call" | custom-call | tf_op jit(solution)/shard_map/update/pallas_call | solution.py:907

commit v5 on v4

--- a/solution.py
+++ b/solution.py
@@ -285,7 +285,7 @@
     ("feed", 0): {0: (0x38,), 1: (0x29,), 2: (0x1b, 0x48)},
     ("feed", 1): {0: (0x39,), 1: (0x2a,), 2: (0x49,)},
     ("feed", 2): {0: (0x3a,), 1: (0x2b,), 2: (0x4a,)},
-    ("feed", 3): {0: (0x3b, 0x4b)},
+    ("feed", 3): {0: (0x3b,), 3: (0x4b,)},
 }
 
 
@@ -393,19 +393,20 @@
 
 BACK_UNITS = ((1, 0), (2, 0), (1, 1), (2, 1), (1, 2), (2, 2), (1, 3), (2, 3), (0, 3), (0, 2), (0, 1), (0, 0))
 SCATTER_PLAN = {
-    ("feed", 2): {1: (0x10, 0x11)},
-    ("feed", 3): {0: (0x20,), 1: (0x12, 0x13, 0x21), 2: (0x30, 0x22, 0x14)},
-    ("other", 0): {0: (0x40,), 2: (0x32, 0x25, 0x17)},
-    ("other", 1): {0: (0x41,), 2: (0x33, 0x26, 0x42)},
-    ("other", 2): {1: (0x34, 0x27, 0x43)},
-    ("other", 3): {0: (0x35, 0x44)},
-    ("own", 0): {0: (0x36,), 1: (0x45,), 3: (0x37, 0x46, 0x18)},
-    ("own", 1): {0: (0x28,), 1: (0x47,), 2: (0x38,), 3: (0x19,)},
-    ("own", 2): {0: (0x29, 0x48), 2: (0x39,), 3: (0x1a,)},
-    ("own", 3): {0: (0x2a, 0x49), 2: (0x3a,), 3: (0x1b,)},
+    ("feed", 1): {1: (0x10, 0x11)},
+    ("feed", 2): {0: (0x20, 0x21), 1: (0x12, 0x13)},
+    ("feed", 3): {0: (0x30, 0x31, 0x22, 0x23), 1: (0x14, 0x15)},
+    ("other", 0): {0: (0x32, 0x33, 0x24, 0x25, 0x41, 0x17)},
+    ("other", 1): {0: (0x42,)},
+    ("other", 2): {0: (0x34, 0x35, 0x26, 0x27, 0x43)},
+    ("other", 3): {0: (0x44,)},
+    ("own", 0): {0: (0x36, 0x45), 1: (0x37,), 3: (0x18,)},
+    ("own", 1): {0: (0x46,), 2: (0x28, 0x47), 3: (0x19,)},
+    ("own", 2): {0: (0x38,), 2: (0x29,), 3: (0x1a,)},
+    ("own", 3): {0: (0x48,), 1: (0x39,), 2: (0x2a,), 3: (0x1b,)},
 }
-SCATTER_BETWEEN = ((0x23, 0x15), (0x31, 0x24, 0x16))
-SCATTER_AFTER = ((0x4a, 0x2b), (0x3b,), (0x4b,))
+SCATTER_BETWEEN = ((0x40,), (0x16,))
+SCATTER_AFTER = ((0x49,), (0x3a, 0x2b), (0x4a, 0x3b, 0x4b))
 
 
 def layer_kernel(
@@ -453,7 +454,8 @@
     get_hidden.wait()
     x_ref[...] = rms_scaled(middle[...], gain_ref[0:1, :]).astype(BF16)
     xcopy = remote(x_ref, xo, xsem.at[0], xsem.at[1], links.at_z[1])
-    hot = turned_hot(table_ref[...], 2 * LANES - 1)[: rel_ref.shape[1]]
+    near_table = table_ref[SEQLEN - 2 * LANES : SEQLEN + 2 * LANES].reshape(1, 4 * LANES)
+    hot = turned_hot(near_table, 2 * LANES - 1)[: rel_ref.shape[1]]
     high = rel_ref[...].astype(BF16)
     rest = rel_ref[...] - high.astype(F32)
     mid = rest.astype(BF16)
@@ -559,6 +561,8 @@
                         copy.wait()
 
             back.at("feed", t, n)
+            if n == 0:
+                net.at("feed", t, 3)
             wi = weights(1, t, n * tile, (n + 1) * tile)
             wo = weights(2, t, n * tile, (n + 1) * tile)
             inner = mm(x2_ref[...], wi)
@@ -753,7 +757,6 @@
     acc_own[...] = value + grad[...]
     put_grad = pltpu.make_async_copy(acc_own, input_hbm, lsem.at[2])
     put_grad.start()
-    back.run(SCATTER_AFTER[1])
     lane = lax.broadcasted_iota(jnp.int32, (16, 4 * LANES), 1)
     by_line = (
         line_grad[...]
@@ -762,12 +765,34 @@
     )
     high = by_line.astype(BF16)
     low = (by_line - high.astype(F32)).astype(BF16)
-    hot = turned_hot(table_ref[...], 3 * LANES - 2)
+    hot = turned_hot(near_table, 3 * LANES - 2)
     small[0:16, :] = mt(high, hot) + mt(low, hot)
     for n in range(6):
         at = slice(n * LANES, (n + 1) * LANES)
         small[16 + n : 17 + n, :] = gain_part[:, at]
         small[22 + n : 23 + n, :] = gain_two[:, at]
+    small[28:32, :] = jnp.zeros((4, LANES), F32)
+
+    def to_group(lo, n, at):
+        here = small.at[pl.ds(lo, n)]
+        return [remote(here, small_near.at[k, pl.ds(lo, n)], tsend.at[at + k], trecv.at[at + k], to) for k, to in enumerate(group)]
+
+    def along_z(lo, n, at):
+        here = small_z.at[0, pl.ds(lo, n)]
+        return [
+            remote(here, small_z.at[k, pl.ds(lo, n)], tsend.at[at + k], trecv.at[at + k], links.at_z[k]) for k in (1, 2, 3)
+        ]
+
+    def total(lo, n):
+        value = small[lo : lo + n, :]
+        for k in range(7):
+            value = value + small_near[k, lo : lo + n, :]
+        return value
+
+    early = to_group(0, 32, 0)
+    for copy in early:
+        copy.start()
+    back.run(SCATTER_AFTER[1])
     back.run(SCATTER_AFTER[2])
     squares = jnp.zeros((8, LANES), F32)
     for weight in (1, 2, 0):
@@ -777,32 +802,33 @@
         for n in range(value.shape[1] // LANES):
             piece_sum = value[:, n * LANES : (n + 1) * LANES]
             squares = squares + jnp.sum(piece_sum.reshape(-1, 8, LANES), axis=0)
-    small[28:32, :] = squares[0:4] + squares[4:8]
-    near = [remote(small, small_near.at[n], tsend.at[n], trecv.at[n], to) for n, to in enumerate(group)]
-    for copy in near:
+    small[32:40, :] = squares
+    late = to_group(32, 8, 11)
+    for copy in late:
         copy.start()
-    for copy in near:
+    for copy in early:
         copy.wait_recv()
-    total = small[...]
-    for n in range(7):
-        total = total + small_near[n]
-    small_z[0] = total
-    along = [remote(small_z.at[0], small_z.at[n], tsend.at[6 + n], trecv.at[6 + n], links.at_z[n]) for n in (1, 2, 3)]
-    for copy in along:
+    small_z[0, 0:32, :] = total(0, 32)
+    for copy in late:
+        copy.wait_recv()
+    small_z[0, 32:40, :] = total(32, 8)
+    late_z = along_z(0, 40, 18)
+    for copy in late_z:
         copy.start()
-    for copy in along:
+    back.finish()
+    for copy in late_z:
         copy.wait_recv()
     small_ref[...] = (small_z[0] + small_z[1]) + (small_z[2] + small_z[3])
-    for copy in near + along:
+    for copy in early + late + late_z:
         copy.wait_send()
     put_grad.wait()
     swap.wait_send()
-    back.finish()
 
 
 def update_kernel(small_ref, grad_hbm, block_hbm, input_hbm, *refs):
-    hbm, (block_out, input_out, norm_ref), new = refs[:18], refs[18:21], refs[21:39]
-    held, grad_ref, pass_ref, sem = refs[39:57], refs[57], refs[58], refs[59]
+    hbm, (block_out, input_out, norm_ref), new_hbm = refs[:18], refs[18:21], refs[21:39]
+    held, new, grad_ref, pass_ref, sem = refs[39:57], refs[57:75], refs[75], refs[76], refs[77]
+    results = [pltpu.make_async_copy(a, b, sem.at[23 + n]) for n, (a, b) in enumerate(zip(new, new_hbm))]
     through = ((block_hbm, block_out), (input_hbm, input_out))
     fetch = [pltpu.make_async_copy(a, pass_ref.at[n], sem.at[n]) for n, (a, b) in enumerate(through)]
     store = [pltpu.make_async_copy(pass_ref.at[n], b, sem.at[21 + n]) for n, (a, b) in enumerate(through)]
@@ -813,40 +839,57 @@
     attn, out, inner, outer, rel, gain, attn_first, attn_second, out_first, out_second = held[:10]
     inner_first, inner_second, outer_first, outer_second, rel_first, rel_second, gain_first, gain_second = held[10:]
     small = small_ref[0:28, :]
-    squares = jnp.sum(small * small, axis=0, keepdims=True) + jnp.sum(small_ref[28:32, :], axis=0, keepdims=True)
+    squares = jnp.sum(small * small, axis=0, keepdims=True) + jnp.sum(small_ref[32:40, :], axis=0, keepdims=True)
     norm = jnp.sqrt(jnp.sum(squares, axis=1, keepdims=True))
     norm_ref[...] = norm
     factor = jnp.minimum(1.0, CLIP / (norm + 1e-06))
-    for copy in loads:
-        copy.wait()
+    loads[18].wait()
+
+    def ready(*which):
+        for n in which:
+            loads[n].wait()
+
+    def put(*which):
+        for n in which:
+            results[n].start()
+
+    def step(at, grad, rate, master, first, second, outs):
+        for ref, value in zip(outs, adam_step(master[at], grad, first[at], second[at], factor, rate)):
+            ref[at] = value
+
+    whole = slice(None)
+
+    def turned(column):
+        return pltpu.roll(column, HDIM, 1)[:, :HDIM]
+
+    ready(2, 10, 11)
+    step(whole, grad_ref[1], RATE_MATRIX, inner, inner_first, inner_second, new[6:9])
+    put(6, 7, 8)
+    ready(3, 12, 13)
+    step(whole, grad_ref[2], RATE_MATRIX, outer, outer_first, outer_second, new[9:12])
+    put(9, 10, 11)
     for a, b in zip(fetch, store):
         a.wait()
         b.start()
-
-    def step(at, grad, rate, master, first, second, outs):
-        for ref, value in zip(outs, adam_step(master[at], grad, first[at], second[at], factor, rate)):
-            ref[at] = value
-
-    def turned(column):
-        return pltpu.roll(column, HDIM, 1)[:, :HDIM]
-
+    ready(0, 6, 7)
     g = [grad_ref[0, :, n * LANES : (n + 1) * LANES] for n in range(6)]
     tails = (g[4][:, :HDIM], g[5][:, :HDIM], turned(g[4]))
     for n in range(3):
         step((n, slice(None), slice(0, LANES)), g[n], RATE_MATRIX, attn, attn_first, attn_second, new[0:3])
         step((n, slice(None), slice(LANES, LANES + HDIM)), tails[n], RATE_MATRIX, attn, attn_first, attn_second, new[0:3])
+    put(0, 1, 2)
+    ready(1, 8, 9)
     rows = g[3].shape[0]
     blank = jnp.zeros((LANES - rows, LANES), F32)
     lower = pltpu.roll(g[5], HDIM, 1)
-    whole = slice(None)
     step((slice(0, LANES), whole), jnp.concatenate([g[3], blank], axis=0).T[:, :rows], RATE_OUT, out, out_first, out_second, new[3:6])
     step(
         (slice(LANES, LANES + HDIM), whole),
         jnp.concatenate([lower, blank], axis=0).T[:HDIM, :rows],
         RATE_OUT, out, out_first, out_second, new[3:6],
     )
-    step(whole, grad_ref[1], RATE_MATRIX, inner, inner_first, inner_second, new[6:9])
-    step(whole, grad_ref[2], RATE_MATRIX, outer, outer_first, outer_second, new[9:12])
+    put(3, 4, 5)
+    ready(4, 5, 14, 15, 16, 17)
     heads, buckets = rel.shape
     step(whole, small_ref[0:heads, 0:buckets], RATE_SMALL, rel, rel_first, rel_second, new[12:15])
     gain_grad = jnp.concatenate(
@@ -857,7 +900,8 @@
         axis=0,
     )
     step(whole, gain_grad, RATE_SMALL, gain, gain_first, gain_second, new[15:18])
-    for copy in store:
+    put(*range(12, 18))
+    for copy in store + results:
         copy.wait()
 
 
@@ -877,7 +921,7 @@
         out_shape=[
             jax.ShapeDtypeStruct((t, d), F32),
             jax.ShapeDtypeStruct((t, d), F32),
-            jax.ShapeDtypeStruct((32, LANES), F32),
+            jax.ShapeDtypeStruct((40, LANES), F32),
             jax.ShapeDtypeStruct((3, rows, cols), F32),
             jax.ShapeDtypeStruct(split, BF16),
             jax.ShapeDtypeStruct(split, BF16),
@@ -889,9 +933,9 @@
             low(t, d), low(d, t), low(t, d), low(d, t), full(t, d), full(t, d), low(*split), low(2 * t, LANES),
             full(parts, 8, t), full(rel.shape[0], 4 * LANES), full(parts, 8, t), full(parts, 3, LANES, LANES), low(t, d),
             low(8, 4, rows, cols), low(3, 4, rows, cols), low(8, 2, rows // 2, cols), low(8, 2, rows, cols), low(3, 3, rows, cols),
-            full(16, 4 * LANES), full(2, 16, 4 * LANES), full(32, LANES), full(7, 32, LANES), full(4, 32, LANES),
+            full(16, 4 * LANES), full(2, 16, 4 * LANES), full(40, LANES), full(7, 40, LANES), full(4, 40, LANES),
             dma((12, 8)), dma((12, 8)), dma((9,)), dma((9,)), dma((2,)), dma((3,)), dma((2, 2)), dma((2,)),
-            dma((12, 6)), dma((12, 6)), dma((3,)), dma((10,)), dma((10,)),
+            dma((12, 6)), dma((12, 6)), dma((3,)), dma((22,)), dma((22,)),
         ],
         compiler_params=pltpu.CompilerParams(
             vmem_limit_bytes=63 * 2**20, collective_id=0, has_side_effects=True
@@ -907,11 +951,13 @@
     return pl.pallas_call(
         update_kernel,
         in_specs=[vmem] + [hbm] * 21,
-        out_specs=[hbm] * 2 + [vmem] * 19,
+        out_specs=[hbm] * 2 + [vmem] + [hbm] * 18,
         out_shape=[like(block_out), like(input_grad), jax.ShapeDtypeStruct((1, 1), F32)]
         + [like(a) for a in masters for _ in range(3)],
-        scratch_shapes=[pltpu.VMEM(a.shape, F32) for a in (*masters, *moments, grads)]
-        + [pltpu.VMEM((2, *block_out.shape), F32), pltpu.SemaphoreType.DMA((23,))],
+        scratch_shapes=[pltpu.VMEM(a.shape, F32) for a in (*masters, *moments)]
+        + [pltpu.VMEM(a.shape, F32) for a in masters for _ in range(3)]
+        + [pltpu.VMEM(grads.shape, F32)]
+        + [pltpu.VMEM((2, *block_out.shape), F32), pltpu.SemaphoreType.DMA((41,))],
         compiler_params=pltpu.CompilerParams(vmem_limit_bytes=62 * 2**20),
         name="update",
     )(small, grads, block_out, input_grad, *masters, *moments)
@@ -922,9 +968,8 @@
     attn_first, attn_second, out_first, out_second, inner_first, inner_second, outer_first, outer_second,
     rel_first, rel_second, gain_first, gain_second, *, parts,
 ):
-    near_table = table[SEQLEN - 2 * LANES : SEQLEN + 2 * LANES].reshape(1, 4 * LANES)
     block_out, input_grad, small, owned, _, _ = run_layer(
-        lengths, attn_weight, out_weight, inner_weight, outer_weight.T, near_table, rel_bias.T, gains, hidden_in, out_grad
+        lengths, attn_weight, out_weight, inner_weight, outer_weight.T, table, rel_bias.T, gains, hidden_in, out_grad
     )
     new = run_update(
         small, owned, block_out, input_grad,

time: 184 us -> 177 us (0.962)
  Pallas kernels: 182 us -> 176 us
    pallas_call x1, Pallas kernels: 175 us -> 169 us  [run_layer(): pl.pallas_call(layer_kernel, in_specs=[pl.BlockSpec(memory_space=pltpu.SM...]
where the time goes in v5:
time: 177 us
  Pallas kernels  176 us (99%)
    pallas_call x1, Pallas kernels, run_layer(): pl.pallas_call(layer_kernel, in_specs=[pl.BlockSpec(memory_space=pltpu.SM...  169 us
    pallas_call x1, Pallas kernels, run_update(): pl.pallas_call(update_kernel, in_specs=[vmem] + [hbm] * 21, out_specs=[hb...  6.55 us

profile of v5, /device:TPU:0, one launch (start us, length us, event | category | flops | bytes accessed | tf_op | source)
XLA Modules:
  0.0 176.8 jit_solution(15115176858797174369)
XLA Ops:
  0.7 169.5 %layer.1 = (f32[512,768]{1,0:T(8,128)}, f32[512,768]{1,0:T(8,128)}, f32[40,128]{1,0:T(8,128)}, f32[3,96,768]{2,1,0:T(8,128)}, bf16[4,4,2,96,768]{4,3,2,1,0:T(8,128)(2,1)}, /*index=5*/bf16[4,4,2,96,768]{4,3,2,1,0:T(8,128)(2,1)}) custom-call(s32[2]{0:T(128)} %lengths_ref.1, f32[3,96,192]{2,1,0:T(8,128)} %refs_0_.1, f32[192,96]{1,0:T(8,128)} %refs_1_.1, ...), custom_call_target="tpu_custom_call" | custom-call | tf_op jit(solution)/shard_map/layer/pallas_call | solution.py:917
  170.1 6.5 %update.1 = (f32[512,768]{1,0:T(8,128)}, f32[512,768]{1,0:T(8,128)}, f32[1,1]{1,0:T(1,128)}, f32[3,96,192]{2,1,0:T(8,128)}, f32[3,96,192]{2,1,0:T(8,128)}, /*ind...) custom-call(f32[40,128]{1,0:T(8,128)} %get-tuple-element.46.small_re, ...), custom_call_target="tpu_custom_call" | custom-call | tf_op jit(solution)/shard_map/update/pallas_call | solution.py:951

commit v6 on v5

--- a/solution.py
+++ b/solution.py
@@ -267,25 +267,25 @@
             return carry
 
         lax.fori_loop(0, 12, each, 0)
-        for group in (1, 2):
+        for group in range(3):
             for s in (1, 2, 3):
                 self.z_copy(group, s).wait_send()
 
 
 UNITS = ((0, 0), (1, 0), (2, 0), (0, 1), (0, 2), (0, 3), (1, 1), (2, 1), (1, 2), (2, 2), (1, 3), (2, 3))
 GATHER_AHEAD = (
-    (0x11, 0x12, 0x20, 0x13, 0x30),
-    (0x21, 0x14, 0x40, 0x31, 0x22, 0x15, 0x41, 0x32, 0x23, 0x42, 0x33, 0x24, 0x43),
+    (),
+    (0x11, 0x20, 0x12, 0x21, 0x13, 0x30, 0x40, 0x22, 0x31, 0x41, 0x23, 0x32, 0x42, 0x33),
 )
 GATHER_PLAN = {
-    ("attend", 0): {0: (0x34, 0x25), 2: (0x44,), 3: (0x16,)},
-    ("attend", 1): {0: (0x35, 0x17), 3: (0x45, 0x26)},
-    ("attend", 2): {0: (0x18,), 1: (0x36,), 3: (0x27, 0x46, 0x19)},
-    ("attend", 3): {0: (0x37, 0x28, 0x1a), 3: (0x47,)},
-    ("feed", 0): {0: (0x38,), 1: (0x29,), 2: (0x1b, 0x48)},
-    ("feed", 1): {0: (0x39,), 1: (0x2a,), 2: (0x49,)},
-    ("feed", 2): {0: (0x3a,), 1: (0x2b,), 2: (0x4a,)},
-    ("feed", 3): {0: (0x3b,), 3: (0x4b,)},
+    ("attend", 0): {0: (0x43,)},
+    ("attend", 1): {0: (0x14,), 2: (0x15,), 3: (0x24, 0x16, 0x25, 0x17, 0x34, 0x44)},
+    ("attend", 2): {0: (0x26, 0x18), 1: (0x35,), 3: (0x45,)},
+    ("attend", 3): {0: (0x27, 0x36, 0x19), 2: (0x46,), 3: (0x28, 0x1a)},
+    ("feed", 0): {1: (0x37,)},
+    ("feed", 1): {0: (0x47,), 1: (0x29, 0x1b), 2: (0x38,)},
+    ("feed", 2): {0: (0x2a, 0x48, 0x39, 0x49), 2: (0x2b,)},
+    ("feed", 3): {0: (0x3a, 0x4a, 0x3b, 0x4b)},
 }
 
 
@@ -406,7 +406,7 @@
     ("own", 3): {0: (0x48,), 1: (0x39,), 2: (0x2a,), 3: (0x1b,)},
 }
 SCATTER_BETWEEN = ((0x40,), (0x16,))
-SCATTER_AFTER = ((0x49,), (0x3a, 0x2b), (0x4a, 0x3b, 0x4b))
+SCATTER_AFTER = ((0x49,), (0x3a, 0x2b), (0x4a, 0x3b), (0x4b,))
 
 
 def layer_kernel(
@@ -448,12 +448,19 @@
     w[own_block(2)] = outer_ref[...].astype(BF16)
     get_grad.start()
     links.meet([group[n] for n in (2, 4, 5, 6)])
-    for step in (1, 2, 3):
-        net.z_copy(0, step).start()
+    net.z_copy(0, 1).start()
+    inner_z = links.mp % 3 != 0
+
+    @pl.when(inner_z)
+    def _():
+        for kind in range(3):
+            net.z_copy(kind, 3).start()
+
     net.s1(UNITS[0])
     get_hidden.wait()
     x_ref[...] = rms_scaled(middle[...], gain_ref[0:1, :]).astype(BF16)
     xcopy = remote(x_ref, xo, xsem.at[0], xsem.at[1], links.at_z[1])
+    xcopy.start()
     near_table = table_ref[SEQLEN - 2 * LANES : SEQLEN + 2 * LANES].reshape(1, 4 * LANES)
     hot = turned_hot(near_table, 2 * LANES - 1)[: rel_ref.shape[1]]
     high = rel_ref[...].astype(BF16)
@@ -464,18 +471,27 @@
     kaug_ref[...] = key_aug(links.half, lengths_ref[links.mp // 2], tokens)
     far = far_masks(links.first, nq)
     net.run(GATHER_AHEAD[0])
-    for step in (1, 2, 3):
-        net.z_copy(0, step).wait_send()
-    xcopy.start()
     get_grad.wait()
     ob = grad[...].astype(BF16)
     ob_ref[...] = ob
     obt_ref[...] = ob.T
     net.run(GATHER_AHEAD[1])
     xcopy.wait_send()
-    for step in (1, 2, 3):
+    net.z_copy(0, 2).start()
+
+    @pl.when(jnp.logical_not(inner_z))
+    def _():
+        net.z_copy(0, 3).start()
+
+    for step in (1, 2):
         net.z_copy(1, step).start()
         net.z_copy(2, step).start()
+
+    @pl.when(jnp.logical_not(inner_z))
+    def _():
+        net.z_copy(1, 3).start()
+        net.z_copy(2, 3).start()
+
     xcopy.wait_recv()
 
     masks = [half_rows(0), half_rows(1)]
@@ -750,6 +766,7 @@
     acc_own[...] = jnp.zeros_like(acc_own)
     lax.fori_loop(0, 4, own_side, 0)
     back.run(SCATTER_AFTER[0])
+    back.run(SCATTER_AFTER[1])
     get_hidden.wait()
     swap.wait_recv()
     one_back = acc_own[...] + oth_in[...].astype(F32)
@@ -789,19 +806,22 @@
             value = value + small_near[k, lo : lo + n, :]
         return value
 
+    def squares_of(weight):
+        back.last(weight)
+        value = result_ref[weight]
+        value = value * value
+        parts = [
+            jnp.sum(value[:, n * LANES : (n + 1) * LANES].reshape(-1, 8, LANES), axis=0) for n in range(value.shape[1] // LANES)
+        ]
+        return functools.reduce(jnp.add, parts)
+
+    squares = squares_of(1) + squares_of(2)
+    back.run(SCATTER_AFTER[2])
     early = to_group(0, 32, 0)
     for copy in early:
         copy.start()
-    back.run(SCATTER_AFTER[1])
-    back.run(SCATTER_AFTER[2])
-    squares = jnp.zeros((8, LANES), F32)
-    for weight in (1, 2, 0):
-        back.last(weight)
-        value = result_ref[weight]
-        value = value * value
-        for n in range(value.shape[1] // LANES):
-            piece_sum = value[:, n * LANES : (n + 1) * LANES]
-            squares = squares + jnp.sum(piece_sum.reshape(-1, 8, LANES), axis=0)
+    back.run(SCATTER_AFTER[3])
+    squares = squares + squares_of(0)
     small[32:40, :] = squares
     late = to_group(32, 8, 11)
     for copy in late:

time: 177 us -> 175 us (0.989)
  Pallas kernels: 176 us -> 174 us
    pallas_call x1, Pallas kernels: 169 us -> 167 us  [run_layer(): pl.pallas_call(layer_kernel, in_specs=[pl.BlockSpec(memory_space=pltpu.SM...]
where the time goes in v6:
time: 175 us
  Pallas kernels  174 us (99%)
    pallas_call x1, Pallas kernels, run_layer(): pl.pallas_call(layer_kernel, in_specs=[pl.BlockSpec(memory_space=pltpu.SM...  167 us
    pallas_call x1, Pallas kernels, run_update(): pl.pallas_call(update_kernel, in_specs=[vmem] + [hbm] * 21, out_specs=[hb...  6.55 us

profile of v6, /device:TPU:0, one launch (start us, length us, event | category | flops | bytes accessed | tf_op | source)
XLA Modules:
  0.0 174.9 jit_solution(718222915433675791)
XLA Ops:
  0.7 167.5 %layer.1 = (f32[512,768]{1,0:T(8,128)}, f32[512,768]{1,0:T(8,128)}, f32[40,128]{1,0:T(8,128)}, f32[3,96,768]{2,1,0:T(8,128)}, bf16[4,4,2,96,768]{4,3,2,1,0:T(8,128)(2,1)}, /*index=5*/bf16[4,4,2,96,768]{4,3,2,1,0:T(8,128)(2,1)}) custom-call(s32[2]{0:T(128)} %lengths_ref.1, f32[3,96,192]{2,1,0:T(8,128)} %refs_0_.1, f32[192,96]{1,0:T(8,128)} %refs_1_.1, ...), custom_call_target="tpu_custom_call" | custom-call | tf_op jit(solution)/shard_map/layer/pallas_call | solution.py:937
  168.1 6.5 %update.1 = (f32[512,768]{1,0:T(8,128)}, f32[512,768]{1,0:T(8,128)}, f32[1,1]{1,0:T(1,128)}, f32[3,96,192]{2,1,0:T(8,128)}, f32[3,96,192]{2,1,0:T(8,128)}, /*ind...) custom-call(f32[40,128]{1,0:T(8,128)} %get-tuple-element.46.small_re, ...), custom_call_target="tpu_custom_call" | custom-call | tf_op jit(solution)/shard_map/update/pallas_call | solution.py:971
